TPU v7x, 32 devices: a whole 2x2x4 slice. The times are simulated.
32 devices in a mesh: section: 2 (over core), shard: 4 (over z), group: 4 (over y, x).
Axes of the slice: x: 2, y: 2, z: 4, core: 2. Of those that a mesh axis runs over, the one named last changes fastest.
Arguments:
- ends_in: bfloat16 [2, 8192, 1024], P('section', ('shard', 'group')), may hold values from -8 to 8
- lengths: int32 [32, 3], P(('shard', 'group')), may hold values from 1 to 128, 256 in all within a row
- norm_gain_a: float32 [2, 1024], P('section'), may hold values from 0.5 to 1.5
- norm_bias_a: float32 [2, 1024], P('section'), may hold values from -3 to 3
- w_qkv: bfloat16 [2, 1024, 3072], P('section'), may hold values from -0.1875 to 0.1875
- w_out: bfloat16 [2, 1024, 1024], P('section'), may hold values from -0.75 to 0.75
- norm_gain_f: float32 [2, 1024], P('section'), may hold values from 0.5 to 1.5
- norm_bias_f: float32 [2, 1024], P('section'), may hold values from -3 to 3
- w_gate_up: bfloat16 [2, 1024, 8192], P('section'), may hold values from -0.1875 to 0.1875
- w_down: bfloat16 [2, 4096, 1024], P('section'), may hold values from -0.09375 to 0.09375
Outputs:
- ends_out: float32 [2, 8192, 1024], P('section', ('shard', 'group'))
- grad_gain_a: float32 [2, 1024], P('section', 'shard')
- grad_bias_a: float32 [2, 1024], P('section', 'shard')
- grad_qkv: float32 [2, 1024, 3072], P('section', 'shard')
- grad_out: float32 [2, 1024, 1024], P('section', 'shard')
- grad_gain_f: float32 [2, 1024], P('section', 'shard')
- grad_bias_f: float32 [2, 1024], P('section', 'shard')
- grad_gate_up: float32 [2, 1024, 8192], P('section', 'shard')
- grad_down: float32 [2, 4096, 1024], P('section', 'shard')
Inputs may be any that keep to these rules, and one draw needn't show every extreme that they name: Each row holds the lengths of the 3 windows packed one after another into one micro-batch row of 256 tokens; they sum to 256.
All inputs are finite; a program needn't handle non-finite values.
Results may differ from a plain program's by a relative error of at most 0.014.
Values may be sent and summed in bfloat16 or wider, within the bound.
A program may use at most 320 MiB of HBM per device.

v0:
```python
import jax
import jax.numpy as jnp
from jax import lax
from jax.sharding import PartitionSpec as P

HEADS = 16


epsilon = 1e-05


def from_behind(array, axis, by):
    peers = lax.axis_size(axis)
    pairs = [(i, i + by) for i in range(peers) if 0 <= i + by < peers]
    return lax.ppermute(array, axis, pairs)


def layout(lengths_row, row_tokens):
    window_ends = jnp.cumsum(lengths_row, axis=-1)
    token_index = jnp.arange(row_tokens, dtype=jnp.int32)
    passed = token_index[:, None] >= window_ends[..., None, :]
    segment = jnp.sum(passed.astype(jnp.int32), axis=-1)
    before = jnp.sum(jnp.where(passed, lengths_row[..., None, :], 0), axis=-1)
    return (segment, token_index - before)


def tables(position, head_size):
    half_size = head_size // 2
    frequency = 10000.0 ** (-2.0 * jnp.arange(half_size, dtype=jnp.float32) / head_size)
    angles = position.astype(jnp.float32)[..., None] * frequency
    angles = jnp.concatenate([angles, angles], axis=-1)
    return (jnp.cos(angles)[..., None, :], jnp.sin(angles)[..., None, :])


def rotate(values, cosine, sine_table):
    half_size = values.shape[-1] // 2
    turned = jnp.concatenate([-values[..., half_size:], values[..., :half_size]], axis=-1)
    return values * cosine + turned * sine_table


def unrotate(values, cosine, sine_table):
    half_size = values.shape[-1] // 2
    scaled = values * sine_table
    return values * cosine + jnp.concatenate(
        [scaled[..., half_size:], -scaled[..., :half_size]], axis=-1
    )


def layer_norm(values, norm_gain, norm_bias):
    average = jnp.mean(values, axis=-1, keepdims=True)
    centered = values - average
    variance = jnp.mean(centered * centered, axis=-1, keepdims=True)
    return centered * lax.rsqrt(variance + epsilon) * norm_gain + norm_bias


def cross_rows(former, latter):
    return lax.dot_general(
        former, latter, (((0,), (0,)), ((), ())), preferred_element_type=jnp.float32
    )


def cross_cols(former, latter):
    return lax.dot_general(
        former, latter, (((1,), (1,)), ((), ())), preferred_element_type=jnp.float32
    )


def swiglu(gate_part, up_part):
    return jax.nn.silu(gate_part) * up_part


def layer_pass(hidden_in, params, lengths_row):
    gain_a, bias_a, weight_qkv, weight_out, gain_f, bias_f, weight_gu, weight_down = params
    row_tokens, features = hidden_in.shape
    head_size = features // HEADS
    ff_width = weight_down.shape[0]
    scaling = head_size ** (-0.5)
    segment, position = layout(lengths_row, row_tokens)
    cosine, sine_table = tables(position, head_size)
    normed_a, pull_norm_a = jax.vjp(layer_norm, hidden_in, gain_a, bias_a)
    low_a = normed_a.astype(jnp.bfloat16)
    projected = jnp.dot(low_a, weight_qkv, preferred_element_type=jnp.float32).reshape(
        row_tokens, 3, HEADS, head_size
    )
    queries = rotate(projected[:, 0], cosine, sine_table).astype(jnp.bfloat16)
    key_rot = rotate(projected[:, 1], cosine, sine_table).astype(jnp.bfloat16)
    values = projected[:, 2].astype(jnp.bfloat16)
    scores = (
        jnp.einsum("qhd,khd->hqk", queries, key_rot, preferred_element_type=jnp.float32) * scaling
    )
    same_window = segment[:, None] == segment[None, :]
    scores = jnp.where(same_window[None], scores, -1e30)
    attn_probs = jax.nn.softmax(scores, axis=-1)
    probs_low = attn_probs.astype(jnp.bfloat16)
    mixture = jnp.einsum("hqk,khd->qhd", probs_low, values, preferred_element_type=jnp.float32)
    mixture = mixture.reshape(row_tokens, features).astype(jnp.bfloat16)
    hidden_mid = hidden_in + jnp.dot(mixture, weight_out, preferred_element_type=jnp.float32)
    normed_f, pull_norm_f = jax.vjp(layer_norm, hidden_mid, gain_f, bias_f)
    low_f = normed_f.astype(jnp.bfloat16)
    gate_up = jnp.dot(low_f, weight_gu, preferred_element_type=jnp.float32)
    hidden, pull_act = jax.vjp(swiglu, gate_up[:, :ff_width], gate_up[:, ff_width:])
    hidden_low = hidden.astype(jnp.bfloat16)
    result = hidden_mid + jnp.dot(hidden_low, weight_down, preferred_element_type=jnp.float32)

    def backward(grad_result):
        grad_low = grad_result.astype(jnp.bfloat16)
        grad_down = cross_rows(hidden_low, grad_low)
        grad_hidden = cross_cols(grad_low, weight_down)
        grad_gate, grad_upper = pull_act(grad_hidden)
        grad_gu = jnp.concatenate([grad_gate, grad_upper], axis=1).astype(jnp.bfloat16)
        grad_gate_up = cross_rows(low_f, grad_gu)
        grad_normed_f = cross_cols(grad_gu, weight_gu)
        grad_from_f, grad_gain_f, grad_bias_f = pull_norm_f(grad_normed_f)
        grad_mid = grad_result + grad_from_f
        grad_branch = grad_mid.astype(jnp.bfloat16)
        grad_out = cross_rows(mixture, grad_branch)
        grad_mixture = (
            cross_cols(grad_branch, weight_out)
            .reshape(row_tokens, HEADS, head_size)
            .astype(jnp.bfloat16)
        )
        grad_probs = jnp.einsum(
            "qhd,khd->hqk", grad_mixture, values, preferred_element_type=jnp.float32
        )
        grad_values = jnp.einsum(
            "hqk,qhd->khd", probs_low, grad_mixture, preferred_element_type=jnp.float32
        )
        grad_scores = attn_probs * (
            grad_probs - jnp.sum(attn_probs * grad_probs, axis=-1, keepdims=True)
        )
        grad_scores = grad_scores.astype(jnp.bfloat16)
        grad_queries = (
            jnp.einsum("hqk,khd->qhd", grad_scores, key_rot, preferred_element_type=jnp.float32)
            * scaling
        )
        grad_keys = (
            jnp.einsum("hqk,qhd->khd", grad_scores, queries, preferred_element_type=jnp.float32)
            * scaling
        )
        grad_projected = jnp.stack(
            [
                unrotate(grad_queries, cosine, sine_table),
                unrotate(grad_keys, cosine, sine_table),
                grad_values,
            ],
            axis=1,
        )
        grad_projected = grad_projected.reshape(row_tokens, 3 * features).astype(jnp.bfloat16)
        grad_qkv = cross_rows(low_a, grad_projected)
        grad_normed_a = cross_cols(grad_projected, weight_qkv)
        grad_from_a, grad_gain_a, grad_bias_a = pull_norm_a(grad_normed_a)
        grads = (
            grad_gain_a,
            grad_bias_a,
            grad_qkv,
            grad_out,
            grad_gain_f,
            grad_bias_f,
            grad_gate_up,
            grad_down,
        )
        return (grad_mid + grad_from_a, grads)

    return (result, backward)


def body(
    ends_in,
    lengths,
    norm_gain_a,
    norm_bias_a,
    w_qkv,
    w_out,
    norm_gain_f,
    norm_bias_f,
    w_gate_up,
    w_down,
):
    section_index = lax.axis_index("section")
    is_first = section_index == 0
    batches = lengths.shape[0]
    features = ends_in.shape[2]
    row_tokens = ends_in.shape[1] // batches
    rows_in = ends_in[0].reshape(batches, row_tokens, features)
    params = (
        norm_gain_a[0],
        norm_bias_a[0],
        w_qkv[0],
        w_out[0],
        norm_gain_f[0],
        norm_bias_f[0],
        w_gate_up[0],
        w_down[0],
    )
    zero_rows = jnp.zeros((row_tokens, features), jnp.bfloat16)

    def lengths_of(turn_index, first_lag, second_lag):
        first_row = lengths[min(max(turn_index - first_lag, 0), batches - 1)]
        second_row = lengths[min(max(turn_index - second_lag, 0), batches - 1)]
        return jnp.where(is_first, first_row, second_row)

    arrived = zero_rows
    inputs = []
    produced = []
    for turn_index in range(batches + 1):
        own_rows = rows_in[turn_index] if turn_index < batches else zero_rows
        current = jnp.where(is_first, own_rows, arrived)
        inputs.append(current)
        result = layer_pass(current.astype(jnp.float32), params, lengths_of(turn_index, 0, 1))[0]
        produced.append(result)
        if turn_index < batches:
            arrived = from_behind(result.astype(jnp.bfloat16), "section", 1)
    returned = zero_rows
    totals = None
    grad_inputs = []
    for turn_index in range(batches + 1):
        own_rows = rows_in[turn_index] if turn_index < batches else zero_rows
        incoming = jnp.where(is_first, returned, own_rows)
        later_input = inputs[turn_index + 1] if turn_index < batches else zero_rows
        earlier = inputs[turn_index - 1] if turn_index > 0 else zero_rows
        source = jnp.where(is_first, earlier, later_input)
        backward = layer_pass(source.astype(jnp.float32), params, lengths_of(turn_index, 1, 0))[1]
        grad_source, grads = backward(incoming.astype(jnp.float32))
        totals = grads if totals is None else tuple(jax.tree.map(jnp.add, totals, grads))
        grad_inputs.append(grad_source)
        if turn_index < batches:
            returned = from_behind(grad_source.astype(jnp.bfloat16), "section", -1)
    first_side = jnp.concatenate(grad_inputs[1:], axis=0)
    second_side = jnp.concatenate(produced[1:], axis=0)
    ends_out = jnp.where(is_first, first_side, second_side)[None]
    pieces = (
        lax.psum_scatter(totals[0], ("shard", "group"), scatter_dimension=0, tiled=True),
        lax.psum_scatter(totals[1], ("shard", "group"), scatter_dimension=0, tiled=True),
        lax.psum_scatter(totals[2], ("shard", "group"), scatter_dimension=0, tiled=True),
        lax.psum_scatter(totals[3], ("shard", "group"), scatter_dimension=0, tiled=True),
        lax.psum_scatter(totals[4], ("shard", "group"), scatter_dimension=0, tiled=True),
        lax.psum_scatter(totals[5], ("shard", "group"), scatter_dimension=0, tiled=True),
        lax.psum_scatter(totals[6], ("shard", "group"), scatter_dimension=0, tiled=True),
        lax.psum_scatter(totals[7], ("shard", "group"), scatter_dimension=0, tiled=True),
    )
    summed = (
        lax.all_gather(pieces[0].astype(jnp.bfloat16), "group", axis=0, tiled=True).astype(
            jnp.float32
        ),
        lax.all_gather(pieces[1].astype(jnp.bfloat16), "group", axis=0, tiled=True).astype(
            jnp.float32
        ),
        lax.all_gather(pieces[2].astype(jnp.bfloat16), "group", axis=0, tiled=True).astype(
            jnp.float32
        ),
        lax.all_gather(pieces[3].astype(jnp.bfloat16), "group", axis=0, tiled=True).astype(
            jnp.float32
        ),
        lax.all_gather(pieces[4].astype(jnp.bfloat16), "group", axis=0, tiled=True).astype(
            jnp.float32
        ),
        lax.all_gather(pieces[5].astype(jnp.bfloat16), "group", axis=0, tiled=True).astype(
            jnp.float32
        ),
        lax.all_gather(pieces[6].astype(jnp.bfloat16), "group", axis=0, tiled=True).astype(
            jnp.float32
        ),
        lax.all_gather(pieces[7].astype(jnp.bfloat16), "group", axis=0, tiled=True).astype(
            jnp.float32
        ),
    )
    return (
        ends_out,
        summed[0][None],
        summed[1][None],
        summed[2][None],
        summed[3][None],
        summed[4][None],
        summed[5][None],
        summed[6][None],
        summed[7][None],
    )


def solution(mesh):
    placed = (
        P("section", ("shard", "group"), None),
        P(("shard", "group"), None),
        P("section", None),
        P("section", None),
        P("section", None, None),
        P("section", None, None),
        P("section", None),
        P("section", None),
        P("section", None, None),
        P("section", None, None),
    )
    return jax.shard_map(
        body,
        mesh=mesh,
        in_specs=placed,
        out_specs=(
            P("section", ("shard", "group"), None),
            P("section", "shard"),
            P("section", "shard"),
            P("section", "shard", None),
            P("section", "shard", None),
            P("section", "shard"),
            P("section", "shard"),
            P("section", "shard", None),
            P("section", "shard", None),
        ),
        check_vma=False,
    )
```

profile of v0, /device:TPU:0, one launch (start us, length us, event | category | flops | bytes accessed | tf_op | source)
XLA Modules:
  0.0 1838.7 jit_solution(11130972096193208404)
XLA Ops:
  12.8 8.6 copy.72
  33.9 6.9 fusion.22
  40.7 8.3 fusion.150
  74.7 8.7 fusion.20
  83.4 14.3 fusion.44
  97.8 19.7 %multiply_reduce_fusion.5 = (f32[1024]{0:T(1024)}, f32[256]{0:T(256)S(1)}, f32[1024]{0:T(1024)}, f32[256,1024]{1,0:T(8,128)}) fusion(f32[256,1024]{1,0:T(8,128)} %copy-done.2, f32[256]{0:T(256)S(1)} %fusion.333, f32[256]{0:T(256)S(1)} %broadcast_multiply_fusion.24, f32[1024]{0:T(1024)S(1)} %bitcast.426, bf16[1,1024,8192]{2,1,0:T(8,128)(2,1)} %param.18, ...), kind=kOutput, calls=%fused_computation.318 | convolution fusion | flops 4305451008 | bytes 23084032 | tf_op jit(solution)/shard_map/dot_general | solution.py:63
  157.7 12.8 fusion.16
  170.5 9.4 fusion.398
  181.5 7.3 fusion.10
  217.3 8.6 fusion.14
  227.5 13.0 fusion.47
  240.6 19.8 %multiply_reduce_fusion.4 = (f32[1024]{0:T(1024)}, f32[256]{0:T(256)S(1)}, f32[1024]{0:T(1024)}, f32[256,1024]{1,0:T(8,128)}) fusion(f32[256,1024]{1,0:T(8,128)} %copy-done.3, f32[256]{0:T(256)S(1)} %fusion.335, f32[256]{0:T(256)S(1)} %broadcast_multiply_fusion.20, f32[1024]{0:T(1024)S(1)} %bitcast.431, bf16[1,1024,8192]{2,1,0:T(8,128)(2,1)} %param.18, ...), kind=kOutput, calls=%fused_computation.317 | convolution fusion | flops 4305451008 | bytes 23084032 | tf_op jit(solution)/shard_map/dot_general | solution.py:63
  286.4 11.6 fusion.50
  298.0 20.1 %multiply_reduce_fusion.3 = (f32[1024]{0:T(1024)}, f32[256]{0:T(256)S(1)}, f32[1024]{0:T(1024)}, f32[256,1024]{1,0:T(8,128)}) fusion(f32[256,1024]{1,0:T(8,128)} %copy-done.1, f32[256]{0:T(256)S(1)} %fusion.337, f32[256]{0:T(256)S(1)} %broadcast_multiply_fusion.18, f32[1024]{0:T(1024)S(1)} %bitcast.433, bf16[1,1024,8192]{2,1,0:T(8,128)(2,1)} %param.18, ...), kind=kOutput, calls=%fused_computation.316 | convolution fusion | flops 4305451008 | bytes 23084032 | tf_op jit(solution)/shard_map/dot_general | solution.py:63
  330.4 14.7 add_add_fusion.2
  345.3 12.2 fusion.65
  357.5 11.8 fusion.66
  369.3 22.4 %add_add_fusion.1 = f32[4096,1024]{1,0:T(8,128)} fusion(f32[4096,1024]{1,0:T(8,128)} %fusion.65, f32[4096,1024]{1,0:T(8,128)} %fusion.66, f32[256,8192]{1,0:T(8,128)} %fusion.10, bf16[256,1024]{1,0:T(8,128)(2,1)S(1)} %copy-done.29, pred[]{:T(512)S(6)} %eq.42), kind=kOutput, calls=%fused_computation.25 | convolution fusion | flops 2162425856 | bytes 59244544 | tf_op jit(solution)/shard_map/dot_general | solution.py:57
  392.4 19.6 %fusion.64 = f32[1024,8192]{1,0:T(8,128)} fusion(bf16[256,4096]{1,0:T(8,128)(2,1)} %get-tuple-element.68, bf16[256,4096]{1,0:T(8,128)(2,1)} %get-tuple-element.67, f32[256,1024]{1,0:T(8,128)} %copy-done.2, f32[256]{0:T(256)S(1)} %copy-done.78, f32[256]{0:T(256)S(1)} %copy-done.76, f32[1024]{0:T(1024)S(1)} %bitcast.444, f32[1024]{0:T(1024)S(1)} %bitcast.435), kind=kOutput, calls=%fused_computation.111 | convolution fusion | flops 4304666624 | bytes 38807552 | tf_op jit(solution)/shard_map/dot_general | solution.py:57
  412.0 13.9 fusion.63
  425.9 36.7 %add_add_fusion = f32[1024,8192]{1,0:T(8,128)} fusion(f32[1024,8192]{1,0:T(8,128)} %fusion.64, f32[1024,8192]{1,0:T(8,128)} %fusion.63, bf16[256,4096]{1,0:T(8,128)(2,1)} %get-tuple-element.64, bf16[256,4096]{1,0:T(8,128)(2,1)} %get-tuple-element.63, f32[256,1024]{1,0:T(8,128)} %copy-done.1, f32[256]{0:T(256)S(1)} %fusion.337, ...), kind=kOutput, calls=%fused_computation.6 | convolution fusion | flops 4321443840 | bytes 105916416 | tf_op jit(solution)/shard_map/dot_general | solution.py:57
  468.7 84.0 %reduce-scatter.5.cloned.1.call-done = f32[64,3072]{1,0:T(8,128)} async-done(((f32[1024,3072]{1,0:T(8,128)}), f32[64,3072]{1,0:T(8,128)}) %reduce-scatter.5.cloned.1.call-update) | async-done | bytes 786448 | tf_op jit(solution)/shard_map/reduce_scatter | solution.py:234
  563.9 337.2 %reduce-scatter.11.cloned.1.call-done = f32[256,1024]{1,0:T(8,128)} async-done(((f32[4096,1024]{1,0:T(8,128)}), f32[256,1024]{1,0:T(8,128)}) %reduce-scatter.11.cloned.1.call-update) | async-done | bytes 1048592 | tf_op jit(solution)/shard_map/reduce_scatter | solution.py:239
  911.0 681.7 %reduce-scatter.9.cloned.1.call-done = f32[64,8192]{1,0:T(8,128)} async-done(((f32[1024,8192]{1,0:T(8,128)}), f32[64,8192]{1,0:T(8,128)}) %reduce-scatter.9.cloned.1.call-update) | async-done | bytes 2097168 | tf_op jit(solution)/shard_map/reduce_scatter | solution.py:238
  1595.4 10.6 fusion.6
  1606.1 7.2 fusion.145
  1617.1 80.3 %all-reduce.8 = (bf16[1024]{0:T(1024)(128)(2,1)S(1)}, bf16[1024]{0:T(1024)(128)(2,1)S(1)}, bf16[1024]{0:T(1024)(128)(2,1)S(1)}, bf16[1024]{0:T(1024)(128)(2,1)S(1)}) all-reduce(f32[1024]{0:T(1024)S(1)} %add_add_fusion.17, f32[1024]{0:T(1024)S(1)} %add_add_fusion.16, ...), channel_id=2, replica_groups=mesh['section'=2,'shard'=4,'group'=4] {'shard','group'}, use_global_device_ids=true, to_apply=%region_66.67.clone | all-reduce | flops 4096 | bytes 24576
  1698.6 7.4 all-reduce.9
  1713.2 10.6 all_gather.27
  1724.9 7.5 all-gather.4.cloned.1.call-done
  1735.9 33.6 %all-gather.8.cloned.1.call-done = bf16[1024,1024]{1,0:T(8,128)(2,1)} async-done(((bf16[256,1024]{1,0:T(8,128)(2,1)}), bf16[1024,1024]{1,0:T(8,128)(2,1)}) %all-gather.8.cloned.1.call-update) | async-done | bytes 2097168 | tf_op jit(solution)/shard_map/all_gather | solution.py:263
  1773.5 51.2 %all-gather.6.cloned.1.call-done = bf16[256,8192]{1,0:T(8,128)(2,1)} async-done(((bf16[64,8192]{1,0:T(8,128)(2,1)}), bf16[256,8192]{1,0:T(8,128)(2,1)}) %all-gather.6.cloned.1.call-update) | async-done | bytes 4194320 | tf_op jit(solution)/shard_map/all_gather | solution.py:260
  (503 shorter events, 208.5 us)
Async XLA Ops:
  7.2 22.1 %copy-start = (bf16[1,1024,1024]{2,1,0:T(8,128)(2,1)S(1)}, bf16[1,1024,1024]{2,1,0:T(8,128)(2,1)}, u32[]{:S(2)}) copy-start(bf16[1,1024,1024]{2,1,0:T(8,128)(2,1)} %param.15) | copy-start | bytes 6291460
  7.2 545.5 %reduce-scatter.5.cloned.1.call-start = ((), (), s32[]{:S(2)}) async-start(), calls=%async_computation.4 | async-start | bytes 13369344 | tf_op jit(solution)/shard_map/reduce_scatter | solution.py:234
  11.9 15.5 copy-start.83
  49.1 6.6 collective-permute-start
  53.2 92.8 %copy-start.59 = (f32[256,64]{0,1:T(8,128)}, f32[256,64]{0,1:T(8,128)S(1)}, u32[]{:S(2)}) copy-start(f32[256,64]{0,1:T(8,128)S(1)} %get-tuple-element.139) | copy-start | bytes 196612
  53.2 92.8 %copy-start.61 = (f32[256,64]{0,1:T(8,128)}, f32[256,64]{0,1:T(8,128)S(1)}, u32[]{:S(2)}) copy-start(f32[256,64]{0,1:T(8,128)S(1)} %get-tuple-element.140) | copy-start | bytes 196612
  73.8 43.7 %copy-start.75 = (f32[256]{0:T(256)}, f32[256]{0:T(256)S(1)}, u32[]{:S(2)}) copy-start(f32[256]{0:T(256)S(1)} %broadcast_multiply_fusion.24) | copy-start | bytes 3076
  74.7 42.8 %copy-start.77 = (f32[256]{0:T(256)}, f32[256]{0:T(256)S(1)}, u32[]{:S(2)}) copy-start(f32[256]{0:T(256)S(1)} %fusion.333) | copy-start | bytes 3076
  126.4 17.0 copy-start.91
  157.1 24.3 %copy-start.1 = (f32[256,1024]{1,0:T(8,128)}, f32[256,1024]{1,0:T(8,128)S(1)}, u32[]{:S(2)}) copy-start(f32[256,1024]{1,0:T(8,128)S(1)} %get-tuple-element.192) | copy-start | bytes 3145732
  157.7 23.7 %slice-start.4 = ((s8[16777216]{0:T(1024)(128)(4,1)}), s8[4194304]{0:T(1024)(128)(4,1)S(1)}, s32[]{:S(2)}) async-start(s8[16777216]{0:T(1024)(128)(4,1)} %bitcast.420), calls=%async_computation.15 | async-start | bytes 8388608
  157.7 23.8 %slice-start.5 = ((s8[16777216]{0:T(1024)(128)(4,1)}), s8[4194304]{0:T(1024)(128)(4,1)S(1)}, s32[]{:S(2)}) async-start(s8[16777216]{0:T(1024)(128)(4,1)} %bitcast.420), calls=%async_computation.16 | async-start | bytes 8388608
  180.0 15.4 collective-permute-start.2
  199.1 26.8 %collective-permute-start.1 = (bf16[256,1024]{1,0:T(8,128)(2,1)}, bf16[256,1024]{1,0:T(8,128)(2,1)}, u32[]{:S(2)}, u32[]{:S(2)}) collective-permute-start(bf16[256,1024]{1,0:T(8,128)(2,1)} %get-tuple-element.107), channel_id=1, source_target_pairs={{16,0},{17,1},{18,2},{19,3},{20,4},{21,5},{22,6},{23,7},{24,8},{25... | collective-permute-start | bytes 1572872 | tf_op jit(solution)/shard_map/ppermute | solution.py:15
  226.0 14.6 copy-start.19
  278.2 8.2 collective-permute-start.3
  298.0 23.2 %copy-start.29 = (bf16[256,1024]{1,0:T(8,128)(2,1)S(1)}, bf16[256,1024]{1,0:T(8,128)(2,1)}, u32[]{:S(2)}) copy-start(bf16[256,1024]{1,0:T(8,128)(2,1)} %copy-done.28) | copy-start | bytes 1572868
  345.1 556.0 %reduce-scatter.11.cloned.1.call-start = ((), (), s32[]{:S(2)}) async-start(), calls=%async_computation.9 | async-start | bytes 17825792 | tf_op jit(solution)/shard_map/reduce_scatter | solution.py:239
  391.7 1201.0 %reduce-scatter.9.cloned.1.call-start = ((), (), s32[]{:S(2)}) async-start(), calls=%async_computation.7 | async-start | bytes 35651584 | tf_op jit(solution)/shard_map/reduce_scatter | solution.py:238
  392.4 19.6 %copy-start.4 = (f32[256,1024]{1,0:T(8,128)S(1)}, f32[256,1024]{1,0:T(8,128)}, u32[]{:S(2)}) copy-start(f32[256,1024]{1,0:T(8,128)} %copy-done.3) | copy-start | bytes 3145732
  392.4 19.6 %copy-start.57 = (bf16[256,4096]{1,0:T(8,128)(2,1)S(1)}, bf16[256,4096]{1,0:T(8,128)(2,1)}, u32[]{:S(2)}) copy-start(bf16[256,4096]{1,0:T(8,128)(2,1)} %get-tuple-element.65) | copy-start | bytes 6291460
  392.4 19.6 %copy-start.58 = (bf16[256,4096]{1,0:T(8,128)(2,1)S(1)}, bf16[256,4096]{1,0:T(8,128)(2,1)}, u32[]{:S(2)}) copy-start(bf16[256,4096]{1,0:T(8,128)(2,1)} %get-tuple-element.66) | copy-start | bytes 6291460
  462.6 1249.6 %reduce-scatter.7.cloned.1.call-start = ((), (), s32[]{:S(2)}) async-start(), calls=%async_computation.6 | async-start | bytes 4456448 | tf_op jit(solution)/shard_map/reduce_scatter | solution.py:235
  468.6 86.4 %copy-start.118 = (u32[32]{0:T(128)S(1)}, u32[32]{0:T(128)}, u32[]{:S(2)}) copy-start(u32[32]{0:T(128)} %constant.122) | copy-start | bytes 388
  468.6 87.6 %copy-start.117 = (u32[32]{0:T(128)S(1)}, u32[32]{0:T(128)}, u32[]{:S(2)}) copy-start(u32[32]{0:T(128)} %constant.98) | copy-start | bytes 388
  468.6 88.9 %copy-start.104 = (f32[256]{0:T(256)S(1)}, f32[256]{0:T(256)}, u32[]{:S(2)}) copy-start(f32[256]{0:T(256)} %get-tuple-element.124) | copy-start | bytes 3076
  468.6 88.9 %copy-start.103 = (f32[256]{0:T(256)S(1)}, f32[256]{0:T(256)}, u32[]{:S(2)}) copy-start(f32[256]{0:T(256)} %copy-done.102) | copy-start | bytes 3076
  468.6 1263.8 %all-gather.4.cloned.1.call-start = ((), (), s32[]{:S(2)}) async-start(), calls=%async_computation.5 | async-start | bytes 1966080 | tf_op jit(solution)/shard_map/all_gather | solution.py:248
  554.7 1214.8 %all-gather.8.cloned.1.call-start = ((), (), s32[]{:S(2)}) async-start(), calls=%async_computation.10 | async-start | bytes 2621440 | tf_op jit(solution)/shard_map/all_gather | solution.py:263
  903.3 921.5 %all-gather.6.cloned.1.call-start = ((), (), s32[]{:S(2)}) async-start(), calls=%async_computation.8 | async-start | bytes 5242880 | tf_op jit(solution)/shard_map/all_gather | solution.py:260
  1595.4 17.9 slice-start.14
  1613.4 94.9 %copy-start.97 = (f32[256]{0:T(256)S(1)}, f32[256]{0:T(256)}, u32[]{:S(2)}) copy-start(f32[256]{0:T(256)} %copy-done.96) | copy-start | bytes 3076
  (116 other events, 478.9 us)
Sparse Core Ops, SparseCore 0:
  345.2 207.4 reduce-scatter.4
  555.1 345.9 reduce-scatter.10
  903.6 689.0 reduce-scatter.8
  1595.5 103.5 reduce-scatter.6
  1701.0 31.4 all-gather.3
  1734.3 35.1 all-gather.7
  1772.0 52.6 all-gather.5
where the time goes:
time: 1850 us; the launch traced here: 1840 us
  waiting for transfers between devices  1200 us (65%)
  matrix products  409 us (22%)
  blocking collectives  98.4 us (5%)
  other arithmetic  73 us (4%)
  local copies, waits for them, and re-layouts  37.3 us (2%)
    reduce_scatter x1, waiting for transfers between devices, body(): lax.psum_scatter(totals[6], ('shard', 'group'), scatter_dimension=0, tile...  682 us
    reduce_scatter x1, waiting for transfers between devices, body(): lax.psum_scatter(totals[7], ('shard', 'group'), scatter_dimension=0, tile...  337 us
    dot_general x12, matrix products, cross_rows(): lax.dot_general(former, latter, (((0,), (0,)), ((), ())), preferred_eleme...  150 us
    dot_general x12, matrix products, cross_cols(): lax.dot_general(former, latter, (((1,), (1,)), ((), ())), preferred_eleme...  109 us
    unnamed x2, blocking collectives  87.8 us
    reduce_scatter x1, waiting for transfers between devices, body(): lax.psum_scatter(totals[2], ('shard', 'group'), scatter_dimension=0, tile...  84 us
    dot_general x6, matrix products, layer_pass(): gate_up = jnp.dot(low_f, weight_gu, preferred_element_type=jnp.float32)  54.9 us
    all_gather x1, waiting for transfers between devices, body(): lax.all_gather(pieces[6].astype(jnp.bfloat16), 'group', axis=0, tiled=True)  51.2 us
  transfers between devices with their start and end apart: 11, of which 6 were waited for; matrix products, arithmetic and copies ran while one was open for 12% of the time, Pallas kernels for 0%

commit v1 on v0

v1 whole, which is shorter than its diff:
```python
import functools

import jax
import jax.numpy as jnp
from jax import lax
from jax.experimental import pallas as pl
from jax.experimental.pallas import tpu as pltpu
from jax.sharding import PartitionSpec as P

MESH = pl.DeviceIdType.MESH
F32, BF16 = jnp.float32, jnp.bfloat16
HEADS = 16
EPSILON = 1e-05


def dot(a, b):
    return jnp.dot(a, b, preferred_element_type=F32)


def dot_cols(a, b):
    return lax.dot_general(a, b, (((1,), (1,)), ((), ())), preferred_element_type=F32)


def dot_rows(a, b):
    return lax.dot_general(a, b, (((0,), (0,)), ((), ())), preferred_element_type=F32)


def in_rows(total, step, run):
    @pl.loop(0, total // step)
    def _(index):
        run(pl.ds(pl.multiple_of(index * step, step), step))


def normalized(values):
    average = jnp.mean(values, axis=-1, keepdims=True)
    centered = values - average
    variance = jnp.mean(centered * centered, axis=-1, keepdims=True)
    spread = lax.rsqrt(variance + EPSILON)
    return centered * spread, spread


def norm_back(grad, values, gain):
    unit, spread = normalized(values)
    scaled = grad * gain
    return spread * (
        scaled
        - jnp.mean(scaled, axis=-1, keepdims=True)
        - unit * jnp.mean(scaled * unit, axis=-1, keepdims=True)
    ), grad * unit


def lanes_of(shape):
    return lax.broadcasted_iota(jnp.int32, shape, len(shape) - 1)


def turn(values, half, size):
    wide = values.shape[-1]
    early = lax.rem(lanes_of(values.shape), size) < half
    return jnp.where(early, pltpu.roll(values, wide - half, 1), pltpu.roll(values, half, 1)), early


def rotated(values, cosine, sine, size):
    other, early = turn(values, size // 2, size)
    return values * cosine + jnp.where(early, -other, other) * sine


def unrotated(values, cosine, sine, size):
    other, early = turn(values * sine, size // 2, size)
    return values * cosine + jnp.where(early, other, -other)


def window_of(index, lengths_ref, row):
    windows = lengths_ref.shape[1]
    end = lengths_ref[row, 0]
    segment = (index >= end).astype(jnp.int32)
    for window in range(1, windows):
        end = end + lengths_ref[row, window]
        segment = segment + (index >= end).astype(jnp.int32)
    return segment


def same_window(lengths_ref, row, tokens):
    queries = window_of(lax.broadcasted_iota(jnp.int32, (tokens, 1), 0), lengths_ref, row)
    keys = window_of(lax.broadcasted_iota(jnp.int32, (1, tokens), 1), lengths_ref, row)
    return queries == keys


def softmax(scores, allowed):
    scores = jnp.where(allowed, scores, -1e30)
    weights = jnp.exp(scores - jnp.max(scores, axis=-1, keepdims=True))
    return weights * (1.0 / jnp.sum(weights, axis=-1, keepdims=True))


def attention_kernel(size, row_tokens, act_ref, lengths_ref, x_ref, gain_ref, bias_ref, wq_ref, wk_ref, wv_ref,
                     wo_ref, cos_ref, sin_ref, mid_ref, low_ref, qkv_ref, mix_ref):
    tokens = x_ref.shape[0]
    part = pl.program_id(0)
    block = wq_ref.shape[1]
    pair = 2 * size

    @pl.when(act_ref[0] == 1)
    def _():
        @pl.when(part == 0)
        def _():
            def begin(rows):
                values = x_ref[rows].astype(F32)
                unit, _ = normalized(values)
                low_ref[rows] = (unit * gain_ref[...] + bias_ref[...]).astype(BF16)
                mid_ref[rows] = values
            in_rows(tokens, 64, begin)

        def project(rows):
            low = low_ref[rows]
            cosine, sine = cos_ref[rows], sin_ref[rows]
            qkv_ref[0, rows] = rotated(dot(low, wq_ref[...]), cosine, sine, size).astype(BF16)
            qkv_ref[1, rows] = rotated(dot(low, wk_ref[...]), cosine, sine, size).astype(BF16)
            qkv_ref[2, rows] = dot(low, wv_ref[...]).astype(BF16)
        in_rows(tokens, row_tokens, project)

        @pl.loop(0, tokens // row_tokens)
        def _(row):
            rows = pl.ds(pl.multiple_of(row * row_tokens, row_tokens), row_tokens)
            allowed = same_window(lengths_ref, row, row_tokens)
            first = lanes_of((row_tokens, pair)) < size
            for at in range(block // pair):
                lanes = pl.ds(at * pair, pair)
                query, key, value = (qkv_ref[which, rows, lanes] for which in range(3))
                query = query * (size ** -0.5)
                results = []
                for head in range(2):
                    own = jnp.where(first if head == 0 else jnp.logical_not(first), query, jnp.zeros_like(query))
                    probs = softmax(dot_cols(own, key), allowed)
                    results.append(dot(probs.astype(BF16), value))
                mix_ref[rows, lanes] = jnp.where(first, results[0], results[1]).astype(BF16)

        def close(rows):
            mid_ref[rows] += dot(mix_ref[rows], wo_ref[...])
        in_rows(tokens, row_tokens, close)


def attention_back_kernel(size, row_tokens, act_ref, lengths_ref, grad_ref, x_ref, gain_ref, qkv_ref, wq_ref, wk_ref,
                          wv_ref, wo_ref, cos_ref, sin_ref, branch_ref, proj_ref, input_ref, input_low_ref,
                          dgain_ref, dbias_ref, gm_ref, total_ref):
    tokens = x_ref.shape[0]
    part = pl.program_id(0)
    block = wq_ref.shape[1]
    pair = 2 * size

    @pl.when(act_ref[0] == 1)
    def _():
        @pl.when(part == 0)
        def _():
            def begin(rows):
                branch_ref[rows] = grad_ref[rows].astype(BF16)
            in_rows(tokens, 64, begin)

        def mixture_grad(rows):
            gm_ref[rows] = dot_cols(branch_ref[rows], wo_ref[...]).astype(BF16)
        in_rows(tokens, row_tokens, mixture_grad)

        @pl.loop(0, tokens // row_tokens)
        def _(row):
            rows = pl.ds(pl.multiple_of(row * row_tokens, row_tokens), row_tokens)
            allowed = same_window(lengths_ref, row, row_tokens)
            first = lanes_of((row_tokens, pair)) < size
            for at in range(block // pair):
                lanes = pl.ds(at * pair, pair)
                query, key, value = (qkv_ref[which, rows, lanes] for which in range(3))
                grad_mix = gm_ref[rows, lanes]
                scaled = query * (size ** -0.5)
                results = []
                for head in range(2):
                    mine = first if head == 0 else jnp.logical_not(first)
                    probs = softmax(dot_cols(jnp.where(mine, scaled, jnp.zeros_like(scaled)), key), allowed)
                    grad_probs = dot_cols(jnp.where(mine, grad_mix, jnp.zeros_like(grad_mix)), value)
                    grad_value = dot_rows(probs.astype(BF16), grad_mix)
                    weighted = probs * grad_probs
                    grad_scores = (weighted - probs * jnp.sum(weighted, axis=-1, keepdims=True)).astype(BF16)
                    results.append((dot(grad_scores, key), dot_rows(grad_scores, query), grad_value))
                grad_query, grad_key, grad_value = (jnp.where(first, a, b) for a, b in zip(*results))
                cosine, sine = cos_ref[rows, lanes], sin_ref[rows, lanes]
                proj_ref[0, rows, lanes] = unrotated(grad_query * (size ** -0.5), cosine, sine, size).astype(BF16)
                proj_ref[1, rows, lanes] = unrotated(grad_key * (size ** -0.5), cosine, sine, size).astype(BF16)
                proj_ref[2, rows, lanes] = grad_value.astype(BF16)

        def normed_grad(rows):
            added = (
                dot_cols(proj_ref[0, rows], wq_ref[...])
                + dot_cols(proj_ref[1, rows], wk_ref[...])
                + dot_cols(proj_ref[2, rows], wv_ref[...])
            )
            total_ref[rows] = jnp.where(part == 0, added, total_ref[rows] + added)
        in_rows(tokens, row_tokens, normed_grad)

        @pl.when(part == pl.num_programs(0) - 1)
        def _():
            dgain_ref[...] = jnp.zeros_like(dgain_ref)
            dbias_ref[...] = jnp.zeros_like(dbias_ref)

            def finish(rows):
                grad = total_ref[rows]
                through, by_gain = norm_back(grad, x_ref[rows].astype(F32), gain_ref[...])
                result = grad_ref[rows] + through
                input_ref[rows] = result
                input_low_ref[rows] = result.astype(BF16)
                dgain_ref[...] += jnp.sum(by_gain, axis=0, keepdims=True)
                dbias_ref[...] += jnp.sum(grad, axis=0, keepdims=True)
            in_rows(tokens, 64, finish)


def feed_kernel(row_tokens, act_ref, mid_ref, gain_ref, bias_ref, wg_ref, wu_ref, wd_ref, out_ref, low_ref, total_ref):
    tokens = mid_ref.shape[0]
    part = pl.program_id(0)

    @pl.when(act_ref[0] == 1)
    def _():
        @pl.when(part == 0)
        def _():
            def begin(rows):
                values = mid_ref[rows]
                unit, _ = normalized(values)
                low_ref[rows] = (unit * gain_ref[...] + bias_ref[...]).astype(BF16)
                total_ref[rows] = values
            in_rows(tokens, 64, begin)

        def step(rows):
            low = low_ref[rows]
            gate = dot(low, wg_ref[...])
            up = dot(low, wu_ref[...])
            hidden = (gate / (1.0 + jnp.exp(-gate)) * up).astype(BF16)
            total_ref[rows] += dot(hidden, wd_ref[...])
        in_rows(tokens, row_tokens, step)

        @pl.when(part == pl.num_programs(0) - 1)
        def _():
            def finish(rows):
                out_ref[rows] = total_ref[rows].astype(BF16)
            in_rows(tokens, 64, finish)


def feed_both_kernel(row_tokens, act_ref, mid_ref, grad_ref, gain_ref, bias_ref, wg_ref, wu_ref, wd_ref, out_ref,
                     low_ref, hidden_ref, ggu_ref, grad_mid_ref, dgain_ref, dbias_ref, total_ref):
    tokens = mid_ref.shape[0]
    part = pl.program_id(0)

    @pl.when(act_ref[0] == 1)
    def _():
        @pl.when(part == 0)
        def _():
            def begin(rows):
                values = mid_ref[rows]
                unit, _ = normalized(values)
                low_ref[rows] = (unit * gain_ref[...] + bias_ref[...]).astype(BF16)
                out_ref[rows] = values
            in_rows(tokens, 64, begin)

        def step(rows):
            low = low_ref[rows]
            gate = dot(low, wg_ref[...])
            up = dot(low, wu_ref[...])
            sig = 1.0 / (1.0 + jnp.exp(-gate))
            silu = gate * sig
            hidden = (silu * up).astype(BF16)
            hidden_ref[rows] = hidden
            out_ref[rows] += dot(hidden, wd_ref[...])
            grad_hidden = dot_cols(grad_ref[rows], wd_ref[...])
            grad_gate = (grad_hidden * up * (sig * (1.0 + gate * (1.0 - sig)))).astype(BF16)
            grad_up = (grad_hidden * silu).astype(BF16)
            ggu_ref[0, rows] = grad_gate
            ggu_ref[1, rows] = grad_up
            added = dot_cols(grad_gate, wg_ref[...]) + dot_cols(grad_up, wu_ref[...])
            total_ref[rows] = jnp.where(part == 0, added, total_ref[rows] + added)
        in_rows(tokens, row_tokens, step)

        @pl.when(part == pl.num_programs(0) - 1)
        def _():
            dgain_ref[...] = jnp.zeros_like(dgain_ref)
            dbias_ref[...] = jnp.zeros_like(dbias_ref)

            def finish(rows):
                grad = total_ref[rows]
                through, by_gain = norm_back(grad, mid_ref[rows], gain_ref[...])
                grad_mid_ref[rows] = grad_ref[rows].astype(F32) + through
                dgain_ref[...] += jnp.sum(by_gain, axis=0, keepdims=True)
                dbias_ref[...] += jnp.sum(grad, axis=0, keepdims=True)
            in_rows(tokens, 64, finish)


def whole(shape):
    return pl.BlockSpec(shape, lambda part, *_: (0,) * len(shape))


def column(rows, wide, offset=0):
    return pl.BlockSpec((rows, wide), lambda part, act, *_: (0, (part + offset) * act[0]))


def stacked(count, rows, wide):
    return pl.BlockSpec((count, rows, wide), lambda part, act, *_: (0, 0, part * act[0]))


def lower(rows, wide):
    return pl.BlockSpec((rows, wide), lambda part, act, *_: (part * act[0], 0))


def local_call(kernel, name, grid, scalars, args, in_specs, outs, out_specs, scratch, flops, limit=56):
    return pl.pallas_call(
        kernel,
        grid_spec=pltpu.PrefetchScalarGridSpec(
            num_scalar_prefetch=len(scalars), grid=(grid,), in_specs=in_specs, out_specs=out_specs,
            scratch_shapes=scratch),
        out_shape=outs,
        name=name,
        cost_estimate=pl.CostEstimate(flops=flops, bytes_accessed=40 * 2 ** 20, transcendentals=0),
        compiler_params=pltpu.CompilerParams(
            dimension_semantics=("arbitrary",), vmem_limit_bytes=limit * 1024 * 1024),
    )(*scalars, *args)


def attention(active, lengths, x, gain, bias, w_qkv, w_out, cosine, sine, parts=4):
    tokens, features = x.shape
    row_tokens = tokens // lengths.shape[0]
    size = features // HEADS
    wide = features // parts
    return local_call(
        functools.partial(attention_kernel, size, row_tokens), "attention", parts, (active, lengths),
        (x, gain, bias, w_qkv, w_qkv, w_qkv, w_out, cosine, sine),
        [whole((tokens, features)), whole((1, features)), whole((1, features)), column(features, wide),
         column(features, wide, parts), column(features, wide, 2 * parts), lower(wide, features),
         whole((tokens, wide)), whole((tokens, wide))],
        (jax.ShapeDtypeStruct((tokens, features), F32), jax.ShapeDtypeStruct((tokens, features), BF16),
         jax.ShapeDtypeStruct((3, tokens, features), BF16), jax.ShapeDtypeStruct((tokens, features), BF16)),
        (whole((tokens, features)), whole((tokens, features)), stacked(3, tokens, wide), column(tokens, wide)),
        [], 8 * tokens * features ** 2)


def attention_back(active, lengths, grad_mid, x, gain, qkv, w_qkv, w_out, cosine, sine, parts=4):
    tokens, features = x.shape
    row_tokens = tokens // lengths.shape[0]
    size = features // HEADS
    wide = features // parts
    vector = jax.ShapeDtypeStruct((1, features), F32)
    return local_call(
        functools.partial(attention_back_kernel, size, row_tokens), "attention_back", parts, (active, lengths),
        (grad_mid, x, gain, qkv, w_qkv, w_qkv, w_qkv, w_out, cosine, sine),
        [whole((tokens, features)), whole((tokens, features)), whole((1, features)), stacked(3, tokens, wide),
         column(features, wide), column(features, wide, parts), column(features, wide, 2 * parts),
         lower(wide, features), whole((tokens, wide)), whole((tokens, wide))],
        (jax.ShapeDtypeStruct((tokens, features), BF16), jax.ShapeDtypeStruct((3, tokens, features), BF16),
         jax.ShapeDtypeStruct((tokens, features), F32), jax.ShapeDtypeStruct((tokens, features), BF16),
         vector, vector),
        (whole((tokens, features)), stacked(3, tokens, wide), whole((tokens, features)), whole((tokens, features)),
         whole((1, features)), whole((1, features))),
        [pltpu.VMEM((tokens, wide), BF16), pltpu.VMEM((tokens, features), F32)], 20 * tokens * features ** 2)


def feed(active, mid, gain, bias, w_gate_up, w_down, parts=8):
    tokens, features = mid.shape
    wide = w_down.shape[0] // parts
    return local_call(
        functools.partial(feed_kernel, tokens // 2), "feed", parts, (active,),
        (mid, gain, bias, w_gate_up, w_gate_up, w_down),
        [whole((tokens, features)), whole((1, features)), whole((1, features)), column(features, wide),
         column(features, wide, parts), lower(wide, features)],
        jax.ShapeDtypeStruct((tokens, features), BF16), whole((tokens, features)),
        [pltpu.VMEM((tokens, features), BF16), pltpu.VMEM((tokens, features), F32)],
        6 * tokens * features * w_down.shape[0])


def feed_both(active, mid, grad, gain, bias, w_gate_up, w_down, parts=8):
    tokens, features = mid.shape
    hidden = w_down.shape[0]
    wide = hidden // parts
    vector = jax.ShapeDtypeStruct((1, features), F32)
    return local_call(
        functools.partial(feed_both_kernel, tokens // 2), "feed_both", parts, (active,),
        (mid, grad, gain, bias, w_gate_up, w_gate_up, w_down),
        [whole((tokens, features)), whole((tokens, features)), whole((1, features)), whole((1, features)),
         column(features, wide), column(features, wide, parts), lower(wide, features)],
        (jax.ShapeDtypeStruct((tokens, features), F32), jax.ShapeDtypeStruct((tokens, features), BF16),
         jax.ShapeDtypeStruct((tokens, hidden), BF16), jax.ShapeDtypeStruct((2, tokens, hidden), BF16),
         jax.ShapeDtypeStruct((tokens, features), F32), vector, vector),
        (whole((tokens, features)), whole((tokens, features)), column(tokens, wide), stacked(2, tokens, wide),
         whole((tokens, features)), whole((1, features)), whole((1, features))),
        [pltpu.VMEM((tokens, features), F32)], 12 * tokens * features * hidden)


def tables(lengths, row_tokens, size, repeat):
    ends = jnp.cumsum(lengths, axis=-1)
    index = jnp.arange(row_tokens, dtype=jnp.int32)
    passed = index[:, None] >= ends[..., None, :]
    before = jnp.sum(jnp.where(passed, lengths[..., None, :], 0), axis=-1)
    position = (index - before).reshape(-1)
    frequency = 10000.0 ** (-2.0 * jnp.arange(size // 2, dtype=F32) / size)
    angles = position.astype(F32)[:, None] * frequency
    return jnp.tile(jnp.cos(angles), (1, 2 * repeat)), jnp.tile(jnp.sin(angles), (1, 2 * repeat))


def exchange_kernel(cfg, *refs):
    shards, bits, seats, unit_rows, width, section, aliased = cfg
    arrays = len(seats)
    lefts, rights = refs[:arrays], refs[arrays:2 * arrays]
    refs = refs[2 * arrays + (1 if aliased else 0):]
    out = refs[0]
    (left, right, left_sem, right_sem, own, give, landed, mine, chain, rest_send, rest_land, rest_keep, piece,
     land_send, land_recv, chain_send, chain_recv,
     rest_ssem, rest_rsem, store_sem, gather_send, gather_recv) = refs[1:]
    units = sum(seat[0] for seat in seats)
    half = unit_rows // 2
    others = bits - 1
    final_rows = unit_rows >> bits
    sec = lax.axis_index("section")
    here = lax.axis_index("shard")
    seat = lax.axis_index("group")

    def bit_of(index):
        return lax.rem(lax.div(seat, 1 << index), 2)

    def across(index):
        return (sec, here, seat + (1 - 2 * bit_of(index)) * (1 << index))

    above = (sec, jnp.minimum(here + 1, shards - 1), seat)
    below = (sec, jnp.maximum(here - 1, 0), seat)
    first = [path for path in range(2)]
    rest = [[index for index in range(bits) if index != path] for path in range(2)]
    sides = [rest[path][::-1] + [first[path]] for path in range(2)]

    def remote(source, target, send, recv, device):
        return pltpu.make_async_remote_copy(
            src_ref=source, dst_ref=target, send_sem=send, recv_sem=recv,
            device_id=device, device_id_type=MESH,
        )

    def seat_row(path, depth):
        row = bit_of(first[path]) * half
        for step in range(depth):
            row = row + bit_of(rest[path][step]) * (half >> (step + 1))
        return row

    def valid(chunk):
        return (chunk >= 0) & (chunk < units)

    def on(condition, run):
        pl.when(condition)(run)

    def by_rows(rows, run, tall=32):
        step = min(rows, tall)

        @pl.loop(0, rows // step)
        def _(index):
            run(pl.ds(pl.multiple_of(index * step, step), step))

    def shifted(part, offset):
        return pl.ds(pl.multiple_of(part.start + offset, part.size), part.size)

    def work():
        barrier = pltpu.get_barrier_semaphore()
        for index in range(bits):
            pl.semaphore_signal(barrier, inc=1, device_id=across(index), device_id_type=MESH)
        on(here < shards - 1, lambda: pl.semaphore_signal(barrier, inc=1, device_id=above, device_id_type=MESH))
        on(here > 0, lambda: pl.semaphore_signal(barrier, inc=1, device_id=below, device_id_type=MESH))
        ends = (here > 0).astype(jnp.int32) + (here < shards - 1).astype(jnp.int32)
        pl.semaphore_wait(barrier, bits + ends)

        for path in range(2):
            for way in range(2):
                @pl.loop(0, shards)
                def _(block):
                    def clear(rows):
                        chain[path, way, chain.shape[2] - 1, block, rows] = jnp.zeros((rows.size, width), BF16)
                    by_rows(half, clear)

        def loads(chunk, run):
            slot, start = lax.rem(chunk, 2), 0
            for which, (count, blocks, inner, rows) in enumerate(seats):
                def each(which=which, start=start, blocks=blocks, inner=inner, rows=rows):
                    local = chunk - start
                    row = lax.div(local, blocks)
                    block = local - row * blocks
                    outer = lax.div(block, inner)
                    column = pl.multiple_of((block - outer * inner) * (2 * width), 2 * width)
                    run(pltpu.make_async_copy(
                        rights[which].at[outer, :, pl.ds(column, 2 * width)], right.at[slot], right_sem.at[slot]))
                    for shard in range(shards):
                        offset = pl.multiple_of(shard * rows + row * unit_rows, unit_rows)
                        run(pltpu.make_async_copy(
                            lefts[which].at[:, pl.ds(offset, unit_rows)], left.at[slot, shard],
                            left_sem.at[slot, shard]))
                on((chunk >= start) & (chunk < start + count), each)
                start += count

        def first_copy(path, chunk):
            two, four = lax.rem(chunk, 2), lax.rem(chunk, 4)
            return remote(give.at[path, two], landed.at[path, four], land_send.at[path, four],
                          land_recv.at[path, four], across(first[path]))

        def opening(path, chunk):
            two = lax.rem(chunk, 2)
            away = (1 - bit_of(first[path])) * half

            @pl.loop(0, shards)
            def _(block):
                own[path, two, block] = lax.dot_general(
                    left[two, block], right[two, :, path * width:(path + 1) * width],
                    (((0,), (0,)), ((), ())), preferred_element_type=F32)

                def round_off(rows):
                    give[path, two, block, rows] = own[path, two, block, shifted(rows, away)].astype(BF16)
                by_rows(half, round_off)
            first_copy(path, chunk).start()

        def first_sum(path, chunk):
            slot, two, four = lax.rem(chunk, shards + 2), lax.rem(chunk, 2), lax.rem(chunk, 4)
            copy = first_copy(path, chunk)
            copy.wait_recv()
            copy.wait_send()
            kept = bit_of(first[path]) * half

            @pl.loop(0, shards)
            def _(block):
                def add(rows):
                    mine[path, slot, block, rows] = (
                        own[path, two, block, shifted(rows, kept)] + landed[path, four, block, rows].astype(F32)
                    ).astype(BF16)
                by_rows(half, add)

        depth = chain.shape[2] - 1

        def hop(path, way, chunk, block):
            slot = lax.rem(chunk, depth)
            ref = chain.at[path, way, slot, block]
            return remote(ref, ref, chain_send.at[path, way, slot, block],
                          chain_recv.at[path, way, slot, block], above if way == 0 else below)

        def onward(path, way, chunk):
            slot, base = lax.rem(chunk, depth), lax.rem(chunk, shards + 2)
            arrives = here > 0 if way == 0 else here < shards - 1

            @pl.loop(0, shards - 1 - here if way == 0 else here)
            def _(index):
                block = shards - 1 - index if way == 0 else index
                copy = hop(path, way, chunk, block)
                on(arrives, lambda: copy.wait_recv())
                source = jnp.where(arrives, slot, depth)

                def add(rows):
                    chain[path, way, slot, block, rows] = (
                        chain[path, way, source, block, rows].astype(F32) + mine[path, base, block, rows].astype(F32)
                    ).astype(BF16)
                by_rows(half, add)
                copy.start()

        def sent(path, way, chunk):
            @pl.loop(0, shards - 1 - here if way == 0 else here)
            def _(index):
                hop(path, way, chunk, shards - 1 - index if way == 0 else index).wait_send()

        def rest_rows(step):
            return half >> (step + 1)

        def rest_copy(path, step, chunk):
            slot = lax.rem(chunk, 4)
            rows = pl.ds(0, rest_rows(step))
            return remote(rest_send.at[path, step, slot, rows], rest_land.at[path, step, slot, rows],
                          rest_ssem.at[path, step, slot], rest_rsem.at[path, step, slot],
                          across(rest[path][step]))

        def share(path, step, chunk, total):
            slot, rows = lax.rem(chunk, 4), rest_rows(step)
            bit = bit_of(rest[path][step])

            def give(part):
                rest_send[path, step, slot, part] = total(part, (1 - bit) * rows).astype(BF16)
            by_rows(rows, give)
            rest_copy(path, step, chunk).start()

            def keep(part):
                rest_keep[path, step, slot, part] = total(part, bit * rows)
            by_rows(rows, keep)

        def last_hop(path, chunk):
            base, slot = lax.rem(chunk, shards + 2), lax.rem(chunk, depth)
            on(here > 0, lambda: hop(path, 0, chunk, here).wait_recv())
            on(here < shards - 1, lambda: hop(path, 1, chunk, here).wait_recv())
            from_below = jnp.where(here > 0, slot, depth)
            from_above = jnp.where(here < shards - 1, slot, depth)

            def total(part, offset):
                rows = shifted(part, offset)
                return (
                    mine[path, base, here, rows].astype(F32)
                    + chain[path, 0, from_below, here, rows].astype(F32)
                    + chain[path, 1, from_above, here, rows].astype(F32)
                )
            share(path, 0, chunk, total)

        def rest_sum(path, step, chunk):
            slot, rows = lax.rem(chunk, 4), rest_rows(step)
            copy = rest_copy(path, step, chunk)
            copy.wait_recv()
            copy.wait_send()

            def total(part, offset):
                part = shifted(part, offset)
                return rest_keep[path, step, slot, part] + rest_land[path, step, slot, part].astype(F32)
            if step + 1 < others:
                share(path, step + 1, chunk, total)
            else:
                def finish(part):
                    piece[path, slot, part] = total(part, 0).astype(BF16)
                by_rows(rows, finish)
                store(path, chunk).start()
                gather(path, 0, chunk).start()

        def place(path, chunk, rows, row):
            return out.at[chunk, pl.ds(pl.multiple_of(row, rows), rows), pl.ds(path * width, width)]

        def store(path, chunk):
            slot = lax.rem(chunk, 4)
            return pltpu.make_async_copy(
                piece.at[path, slot], place(path, chunk, final_rows, seat_row(path, others)),
                store_sem.at[path, slot])

        def gather(path, step, chunk):
            slot = lax.rem(chunk, 4)
            rows = final_rows << step
            target = place(path, chunk, rows, seat_row(path, others - step))
            source = piece.at[path, slot] if step == 0 else target
            return remote(source, target, gather_send.at[path, step, slot],
                          gather_recv.at[path, step, slot], across(sides[path][step]))

        def gathered(path, step, chunk):
            copy = gather(path, step, chunk)
            copy.wait_recv()
            copy.wait_send()
            if step == 0:
                store(path, chunk).wait()
            if step + 1 < bits:
                gather(path, step + 1, chunk).start()

        lag_last = shards + others + bits
        rounds = units + lag_last + 2

        loads(0, lambda copy: copy.start())

        @pl.loop(0, rounds)
        def _(turn):
            on(turn + 1 < units, lambda: loads(turn + 1, lambda copy: copy.start()))
            on(turn < units, lambda: loads(turn, lambda copy: copy.wait()))
            for path in range(2):
                on(turn < units, lambda path=path: opening(path, turn))
            for path in range(2):
                on(valid(turn - 1), lambda path=path: first_sum(path, turn - 1))
            for path in range(2):
                for way in range(2):
                    chunk = turn - 1 - (here if way == 0 else shards - 1 - here)
                    on(valid(chunk - 2), lambda path=path, way=way, chunk=chunk: sent(path, way, chunk - 2))
                    on(valid(chunk), lambda path=path, way=way, chunk=chunk: onward(path, way, chunk))
            for path in range(2):
                on(valid(turn - shards), lambda path=path: last_hop(path, turn - shards))
            for step in range(others):
                for path in range(2):
                    chunk = turn - shards - 1 - step
                    on(valid(chunk), lambda path=path, step=step, chunk=chunk: rest_sum(path, step, chunk))
            for step in range(bits):
                for path in range(2):
                    chunk = turn - shards - others - 1 - step
                    on(valid(chunk), lambda path=path, step=step, chunk=chunk: gathered(path, step, chunk))

    if section is None:
        work()
    else:
        pl.when(sec == section)(work)


def exchange(pairs, shards, group, section, collective_id, unit_width, previous=None, unit_rows_max=256,
             name="exchange"):
    bits = group.bit_length() - 1
    lefts, rights = [p[0] for p in pairs], [p[1] for p in pairs]
    tokens = lefts[0].shape[0]
    rows_of = [a.shape[1] // shards for a in lefts]
    unit_rows = min([unit_rows_max] + rows_of)
    width = unit_width // 2
    inner = [g.shape[2] // unit_width for g in rights]
    seats = tuple(
        (r // unit_rows * g.shape[0] * k, g.shape[0] * k, k, r) for r, g, k in zip(rows_of, rights, inner))
    units = sum(seat[0] for seat in seats)
    half = unit_rows // 2
    others = bits - 1
    final_rows = unit_rows >> bits
    depth = shards + 3
    dma = pltpu.SemaphoreType.DMA
    scratch = [
        pltpu.VMEM((2, shards, tokens, unit_rows), BF16),
        pltpu.VMEM((2, tokens, unit_width), BF16),
        dma((2, shards)), dma((2,)),
        pltpu.VMEM((2, 2, shards, unit_rows, width), F32),
        pltpu.VMEM((2, 2, shards, half, width), BF16),
        pltpu.VMEM((2, 4, shards, half, width), BF16),
        pltpu.VMEM((2, shards + 2, shards, half, width), BF16),
        pltpu.VMEM((2, 2, depth + 1, shards, half, width), BF16),
        pltpu.VMEM((2, others, 4, half // 2, width), BF16),
        pltpu.VMEM((2, others, 4, half // 2, width), BF16),
        pltpu.VMEM((2, others, 4, half // 2, width), F32),
        pltpu.VMEM((2, 4, final_rows, width), BF16),
        dma((2, 4)), dma((2, 4)),
        dma((2, 2, depth, shards)), dma((2, 2, depth, shards)),
        dma((2, others, 4)), dma((2, others, 4)),
        dma((2, 4)),
        dma((2, bits, 4)), dma((2, bits, 4)),
    ]
    cfg = (shards, bits, seats, unit_rows, width, section, previous is not None)
    operands = lefts + rights + ([] if previous is None else [previous])
    return pl.pallas_call(
        functools.partial(exchange_kernel, cfg),
        out_shape=jax.ShapeDtypeStruct((units, unit_rows, unit_width), BF16),
        in_specs=[pl.BlockSpec(memory_space=pl.ANY)] * len(operands),
        out_specs=pl.BlockSpec(memory_space=pl.ANY),
        scratch_shapes=scratch,
        input_output_aliases={} if previous is None else {len(operands) - 1: 0},
        name=name,
        cost_estimate=pl.CostEstimate(
            flops=2 * tokens * units * shards * unit_rows * unit_width, bytes_accessed=100 * 2 ** 20,
            transcendentals=0),
        compiler_params=pltpu.CompilerParams(
            collective_id=collective_id, has_side_effects=True, vmem_limit_bytes=56 * 1024 * 1024),
    )(*operands)


def body(
    ends_in,
    lengths,
    norm_gain_a,
    norm_bias_a,
    w_qkv,
    w_out,
    norm_gain_f,
    norm_bias_f,
    w_gate_up,
    w_down,
):
    section = lax.axis_index("section")
    shards, group = lax.axis_size("shard"), lax.axis_size("group")
    is_first = section == 0
    first, second = ((section == which).astype(jnp.int32).reshape(1) for which in range(2))
    tokens, features = ends_in.shape[1:]
    size = features // HEADS
    rows = ends_in[0]
    weight_qkv, weight_out, weight_gu, weight_down = w_qkv[0], w_out[0], w_gate_up[0], w_down[0]
    parts = 4
    cosine, sine = tables(lengths, tokens // lengths.shape[0], size, HEADS // parts)

    def attend(active, values):
        return attention(active, lengths, values, norm_gain_a, norm_bias_a, weight_qkv, weight_out, cosine, sine, parts)

    def back(active, middle, low_a, qkv, mixture, values, grad):
        result, low_f, hidden, grad_gu, grad_middle, gain_f, bias_f = feed_both(
            active, middle, grad, norm_gain_f, norm_bias_f, weight_gu, weight_down)
        branch, grad_qkv, grad_in, grad_in_low, gain_a, bias_a = attention_back(
            active, lengths, grad_middle, values, norm_gain_a, qkv, weight_qkv, weight_out, cosine, sine, parts)
        pairs = [(hidden, grad[None]), (low_f, grad_gu), (mixture, branch[None]), (low_a, grad_qkv)]
        return result, grad_in, grad_in_low, pairs, jnp.concatenate([gain_a, bias_a, gain_f, bias_f], axis=0)

    middle_0, low_0, qkv_0, mixture_0 = attend(first, rows)
    passed = feed(first, middle_0, norm_gain_f, norm_bias_f, weight_gu, weight_down)
    arrived = lax.ppermute(passed, "section", [(0, 1)])
    middle_1, low_1, qkv_1, mixture_1 = attend(second, arrived)
    result, _, returned, pairs_1, vectors_1 = back(second, middle_1, low_1, qkv_1, mixture_1, arrived, rows)
    returned = lax.ppermute(returned, "section", [(1, 0)])
    summed = exchange(pairs_1, shards, group, 1, 1, features, name="exchange_second")
    _, grad_in, _, pairs_0, vectors_0 = back(first, middle_0, low_0, qkv_0, mixture_0, rows, returned)
    summed = exchange(pairs_0, shards, group, 0, 2, features, previous=summed, name="exchange_first")
    vectors = lax.psum(jnp.where(is_first, vectors_0, vectors_1), ("shard", "group"))
    part = features // shards
    vectors = lax.dynamic_slice(vectors, (0, lax.axis_index("shard") * part), (vectors.shape[0], part))
    ends_out = jnp.where(is_first, grad_in, result)[None]
    unit_rows = summed.shape[1]

    def shaped(start, count, blocks):
        picked = summed[start:start + count].astype(F32).reshape(count // blocks, blocks, unit_rows, features)
        return jnp.transpose(picked, (0, 2, 1, 3)).reshape(1, count // blocks * unit_rows, blocks * features)

    starts, counts, blocks = [0], [], []
    for left, right in pairs_0:
        blocks.append(right.shape[0] * right.shape[2] // features)
        counts.append(left.shape[1] // shards // unit_rows * blocks[-1])
        starts.append(starts[-1] + counts[-1])
    grad_down, grad_gate_up, grad_out, grad_qkv = (shaped(*seat) for seat in zip(starts, counts, blocks))
    return (
        ends_out,
        vectors[0:1],
        vectors[1:2],
        grad_qkv,
        grad_out,
        vectors[2:3],
        vectors[3:4],
        grad_gate_up,
        grad_down,
    )


def solution(mesh):
    placed = (
        P("section", ("shard", "group"), None),
        P(("shard", "group"), None),
        P("section", None),
        P("section", None),
        P("section", None, None),
        P("section", None, None),
        P("section", None),
        P("section", None),
        P("section", None, None),
        P("section", None, None),
    )
    return jax.shard_map(
        body,
        mesh=mesh,
        in_specs=placed,
        out_specs=(
            P("section", ("shard", "group"), None),
            P("section", "shard"),
            P("section", "shard"),
            P("section", "shard", None),
            P("section", "shard", None),
            P("section", "shard"),
            P("section", "shard"),
            P("section", "shard", None),
            P("section", "shard", None),
        ),
        check_vma=False,
    )
```

time: 1850 us -> 590 us (0.32)
  waiting for transfers between devices: 1200 us -> 88.9 us
  matrix products: 409 us -> 0 us
  Pallas kernels: 0 us -> 378 us
  other arithmetic: 73 us -> 15.5 us
  blocking collectives: 98.4 us -> 73 us
    reduce_scatter x4 -> x0, waiting for transfers between devices: 1100 us -> none  [the longest x1 682 us: body(): lax.psum_scatter(totals[6], ('shard', 'group'), scatter_dimension=0, tile...]
    dot_general x66 -> x0, matrix products: 395 us -> none  [the longest x12 150 us: cross_rows(): lax.dot_general(former, latter, (((0,), (0,)), ((), ())), preferred_eleme...]
    pallas_call x0 -> x9, Pallas kernels: none -> 378 us  [the longest x2 233 us: exchange(): pl.pallas_call(functools.partial(exchange_kernel, cfg), out_shape=jax.Sha...]
    all_gather x3 -> x0, waiting for transfers between devices: 92.4 us -> none  [the longest x1 51.2 us: body(): lax.all_gather(pieces[6].astype(jnp.bfloat16), 'group', axis=0, tiled=True)]
    ppermute x4 -> x2, waiting for transfers between devices: 0.01 us -> 88.9 us  [the longest x1 86.5 us: body(): returned = lax.ppermute(returned, 'section', [(1, 0)])]
    unnamed x2 -> x0, blocking collectives: 87.8 us -> none
    psum x0 -> x1, blocking collectives: none -> 73 us  [body(): lax.psum(jnp.where(is_first, vectors_0, vectors_1), ('shard', 'group'))]
    unnamed x289 -> x28, local copies, waits for them, and re-layouts: 34.5 us -> 15.4 us
  transfers between devices with their start and end apart: 11 -> 2, of which waited for: 6 -> 2; matrix products, arithmetic and copies ran while one was open for 12% -> 0% of each run, Pallas kernels for 0% -> 1%
where the time goes in v1:
time: 590 us
  Pallas kernels  378 us (64%)
  waiting for transfers between devices  88.9 us (15%)
  blocking collectives  73 us (12%)
  local copies, waits for them, and re-layouts  31.3 us (5%)
  other arithmetic  15.5 us (3%)
    pallas_call x2, Pallas kernels, exchange(): pl.pallas_call(functools.partial(exchange_kernel, cfg), out_shape=jax.Sha...  233 us
    pallas_call x7, Pallas kernels, local_call(): pl.pallas_call(kernel, grid_spec=pltpu.PrefetchScalarGridSpec(num_scalar_...  145 us
    ppermute x1, waiting for transfers between devices, body(): returned = lax.ppermute(returned, 'section', [(1, 0)])  86.5 us
    psum x1, blocking collectives, body(): lax.psum(jnp.where(is_first, vectors_0, vectors_1), ('shard', 'group'))  73 us
    unnamed x28, local copies, waits for them, and re-layouts  15.4 us
  transfers between devices with their start and end apart: 2, of which 2 were waited for; matrix products, arithmetic and copies ran while one was open for 0% of the time, Pallas kernels for 1%

profile of v1, /device:TPU:0, one launch (start us, length us, event | category | flops | bytes accessed | tf_op | source)
XLA Modules:
  0.0 589.7 jit_solution(18243977748873528800)
XLA Ops:
  0.7 0.8 copy.33
  1.4 0.8 reduce_window_sum.11
  2.5 0.3 multiply_sine_fusion
  2.8 1.0 copy.34.cos_ref
  3.9 1.0 copy.35.sin_ref
  4.9 24.7 %attention.2 = (f32[512,1024]{1,0:T(8,128)}, bf16[512,1024]{1,0:T(8,128)(2,1)}, bf16[3,512,1024]{2,1,0:T(8,128)(2,1)}, bf16[512,1024]{1,0:T(8,128)(2,1)}) custom-call(s32[1]{0:T(128)} %bitcast.act_ref, s32[2,3]{1,0:T(2,128)} %lengths_ref.7, bf16[512,1024]{1,0:T(8,128)(2,1)} %bitcast.54, f32[1,1024]{1,0:T(1,128)} %gain_ref.13, f32[1,1024]{1,0:T(1,128)} %bias_ref.7, ...), custom_call_target="tpu_custom_call" | custom-call | flops 4294967296 | bytes 41943040 | tf_op jit(solution)/shard_map/attention/pallas_call | solution.py:306
  29.6 23.3 %feed.1 = bf16[512,1024]{1,0:T(8,128)(2,1)} custom-call(s32[1]{0:T(128)} %bitcast.act_ref, f32[512,1024]{1,0:T(8,128)} %get-tuple-element.40.mid_ref, f32[1,1024]{1,0:T(1,128)} %gain_ref.12, f32[1,1024]{1,0:T(1,128)} %bias_ref.9, bf16[1024,8192]{1,0:T(8,128)(2,1)} %bitcast.58, bf16[1024,8192]{1,0:T(8,128)(2,1)} %bitcast.59, bf16[4096,1024]{1,0:T(8,128)(2,1)} %bitcast.64), custom_call_target="tpu_custom_call" | custom-call | flops 12884901888 | bytes 41943040 | tf_op jit(solution)/shard_map/feed/pallas_call | solution.py:306
  52.8 1.3 collective-permute-start
  54.2 2.4 collective-permute-done.x_ref
  56.6 1.0 copy-done.2
  57.6 5.2 attention.3
  62.8 5.8 feed_both.2
  68.6 6.4 %attention_back.2 = (bf16[512,1024]{1,0:T(8,128)(2,1)}, bf16[3,512,1024]{2,1,0:T(8,128)(2,1)}, f32[512,1024]{1,0:T(8,128)}, bf16[512,1024]{1,0:T(8,128)(2,1)}, f32[1,1024]{1,0:T(1,128)}, /*index=5*/f32[1,1024]{1,0:T(1,128)}) custom-call(s32[1]{0:T(128)} %bitcast.6.act_ref, s32[2,3]{1,0:T(2,128)} %lengths_ref.7, f32[512,1024]{1,0:T(8,128)} %get-tuple-element.42.grad_ref, ...), custom_call_target="tpu_custom_call" | custom-call | flops 10737418240 | bytes 41943040 | tf_op jit(solution)/shard_map/attention_back/pallas_call | solution.py:306
  75.0 1.3 collective-permute-start.1
  76.3 3.0 exchange_second.1.refs_8_
  79.3 86.5 %collective-permute-done.1.grad_ref = bf16[512,1024]{1,0:T(8,128)(2,1)S(1)} collective-permute-done((bf16[512,1024]{1,0:T(8,128)(2,1)}, bf16[512,1024]{1,0:T(8,128)(2,1)S(1)}, u32[]{:S(2)}, u32[]{:S(2)}) %collective-permute-start.1) | collective-permute-done | bytes 1048608 | tf_op jit(solution)/shard_map/ppermute | solution.py:768
  165.8 1.0 copy-done.11
  166.8 43.3 %feed_both.3 = (f32[512,1024]{1,0:T(8,128)}, bf16[512,1024]{1,0:T(8,128)(2,1)}, bf16[512,4096]{1,0:T(8,128)(2,1)}, bf16[2,512,4096]{2,1,0:T(8,128)(2,1)}, f32[51...) custom-call(s32[1]{0:T(128)} %bitcast.act_ref, f32[512,1024]{1,0:T(8,128)} %get-tuple-element.40.mid_ref, ...), custom_call_target="tpu_custom_call" | custom-call | flops 25769803776 | bytes 41943040 | tf_op jit(solution)/shard_map/feed_both/pallas_call | solution.py:306
  210.1 36.2 %attention_back.3 = (bf16[512,1024]{1,0:T(8,128)(2,1)}, bf16[3,512,1024]{2,1,0:T(8,128)(2,1)}, f32[512,1024]{1,0:T(8,128)}, bf16[512,1024]{1,0:T(8,128)(2,1)}, f32[1,1024]{1,0:T(1,128)}, /*index=5*/f32[1,1024]{1,0:T(1,128)}) custom-call(s32[1]{0:T(128)} %bitcast.act_ref, s32[2,3]{1,0:T(2,128)} %lengths_ref.7, f32[512,1024]{1,0:T(8,128)} %get-tuple-element.45.grad_ref, ...), custom_call_target="tpu_custom_call" | custom-call | flops 10737418240 | bytes 41943040 | tf_op jit(solution)/shard_map/attention_back/pallas_call | solution.py:306
  246.3 229.7 %exchange_first.1 = bf16[16,256,1024]{2,1,0:T(8,128)(2,1)} custom-call(bf16[512,4096]{1,0:T(8,128)(2,1)} %get-tuple-element.57.refs_0_, bf16[512,1024]{1,0:T(8,128)(2,1)} %get-tuple-element.58.refs_1_, bf16[512,1024]{1,0:T(8,128)(2,1)} %get-tuple-element.59.refs_2_, bf16[512,1024]{1,0:T(8,128)(2,1)} %get-tuple-element.60.refs_3_, ...), custom_call_target="tpu_custom_call", output_to_operand_aliasing={{}: (8, {})} | custom-call | flops 17179869184 | bytes 104857600 | tf_op jit(solution)/shard_map/exchange_first/pallas_call | solution.py:713
  476.0 6.8 %convert_bitcast_fusion = f32[1,256,8,1024]{3,1,2,0:T(8,128)} fusion(bf16[16,256,1024]{2,1,0:T(8,128)(2,1)} %exchange_first.1), kind=kLoop, calls=%fused_computation | loop fusion | flops 2097152 | bytes 12582912 | tf_op jit(solution)/shard_map/reshape | solution.py:780
  482.8 0.4 convert_bitcast_fusion.1
  483.2 1.5 slice.31
  484.7 1.1 slice_convert_fusion
  485.8 9.2 %copy.43 = f32[1,256,8,1024]{1,3,2,0:T(8,128)} copy(f32[1,256,8,1024]{3,1,2,0:T(8,128)} %convert_bitcast_fusion) | data formatting | bytes 16777216 | tf_op jit(solution)/shard_map/reshape | solution.py:780
  495.0 8.9 %copy.45 = f32[1,256,8192]{2,1,0:T(8,128)} copy(f32[1,256,8192]{1,2,0:T(8,128)} %bitcast.45) | data formatting | bytes 16777216
  503.9 2.4 copy.42
  506.2 3.7 copy.44
  510.0 2.5 bitcast_convert_fusion
  512.6 73.0 %psum.7 = f32[4,1024]{1,0:T(4,128)S(1)} all-reduce(f32[4,1024]{1,0:T(4,128)S(1)} %maximum_select_fusion), channel_id=1, replica_groups=mesh['section'=2,'shard'=4,'group'=4] {'shard','group'}, use_global_device_ids=true, to_apply=%region_2.3 | all-reduce | flops 4096 | bytes 32768 | tf_op jit(solution)/shard_map/psum | solution.py:772
  585.6 3.5 select_bitcast_fusion
  589.0 0.6 fusion.1
  (30 shorter events, 0.4 us)
Async XLA Ops:
  52.8 3.8 collective-permute-start
  56.6 1.0 copy-start.2
  75.0 90.8 %collective-permute-start.1 = (bf16[512,1024]{1,0:T(8,128)(2,1)}, bf16[512,1024]{1,0:T(8,128)(2,1)S(1)}, u32[]{:S(2)}, u32[]{:S(2)}) collective-permute-start(bf16[512,1024]{1,0:T(8,128)(2,1)} %get-tuple-element.44), channel_id=1, source_target_pairs={{16,0},{17,1},{18,2},{19,3},{20,4},{21,5},{22,6},{23,7},{24,8},{25... | collective-permute-start | bytes 3145736 | tf_op jit(solution)/shard_map/ppermute | solution.py:768
  165.8 1.0 copy-start.11
  476.0 6.8 %copy-start = (bf16[16,256,1024]{2,1,0:T(8,128)(2,1)S(1)}, bf16[16,256,1024]{2,1,0:T(8,128)(2,1)}, u32[]{:S(2)}) copy-start(bf16[16,256,1024]{2,1,0:T(8,128)(2,1)} %exchange_first.1) | copy-start | bytes 25165828
  506.2 3.7 copy-start.1
  509.9 2.5 copy-start.3
  509.9 2.5 copy-start.4
  509.9 2.5 copy-start.5
  509.9 2.5 copy-start.6
  510.0 2.5 copy-start.7
  510.0 2.5 copy-start.8
  510.0 2.5 copy-start.9
  510.0 2.5 copy-start.10

commit v2 on v1

--- a/solution.py
+++ b/solution.py
@@ -399,11 +399,12 @@
     shards, bits, seats, unit_rows, width, section, aliased = cfg
     arrays = len(seats)
     lefts, rights = refs[:arrays], refs[arrays:2 * arrays]
-    refs = refs[2 * arrays + (1 if aliased else 0):]
-    out = refs[0]
-    (left, right, left_sem, right_sem, own, give, landed, mine, chain, rest_send, rest_land, rest_keep, piece,
+    vector = refs[2 * arrays]
+    refs = refs[2 * arrays + 1 + (arrays + 1 if aliased else 0):]
+    outs, vector_out = refs[:arrays], refs[arrays]
+    (vector_land, vector_sum, vector_send, vector_recv, vector_store, left, right, left_sem, right_sem, own, give, landed, mine, chain, rest_send, rest_land, rest_keep, piece,
      land_send, land_recv, chain_send, chain_recv,
-     rest_ssem, rest_rsem, store_sem, gather_send, gather_recv) = refs[1:]
+     rest_ssem, rest_rsem, store_sem, gather_send, gather_recv) = refs[arrays + 1:]
     units = sum(seat[0] for seat in seats)
     half = unit_rows // 2
     others = bits - 1
@@ -436,6 +437,33 @@
             row = row + bit_of(rest[path][step]) * (half >> (step + 1))
         return row
 
+    group = 1 << bits
+    peers = shards * group
+    me = here * group + seat
+    part = vector_out.shape[1]
+
+    def peer(step):
+        index = lax.rem(me + step, peers)
+        return index, (sec, lax.div(index, group), lax.rem(index, group))
+
+    def vector_copy(index, device):
+        lanes = pl.ds(pl.multiple_of(device[1] * part, part), part)
+        return remote(vector.at[:, lanes], vector_land.at[me], vector_send.at[index], vector_recv.at[me], device)
+
+    def vector_finish():
+        vector_sum[...] = vector[:, pl.ds(pl.multiple_of(here * part, part), part)]
+
+        @pl.loop(1, peers)
+        def _(step):
+            index, device = peer(step)
+            vector_copy(index, device).wait_send()
+            remote(vector_land.at[index], vector_land.at[index], vector_send.at[index], vector_recv.at[index],
+                   device).wait_recv()
+            vector_sum[...] += vector_land[index]
+        copy = pltpu.make_async_copy(vector_sum, vector_out, vector_store)
+        copy.start()
+        copy.wait()
+
     def valid(chunk):
         return (chunk >= 0) & (chunk < units)
 
@@ -454,12 +482,15 @@
 
     def work():
         barrier = pltpu.get_barrier_semaphore()
-        for index in range(bits):
-            pl.semaphore_signal(barrier, inc=1, device_id=across(index), device_id_type=MESH)
-        on(here < shards - 1, lambda: pl.semaphore_signal(barrier, inc=1, device_id=above, device_id_type=MESH))
-        on(here > 0, lambda: pl.semaphore_signal(barrier, inc=1, device_id=below, device_id_type=MESH))
-        ends = (here > 0).astype(jnp.int32) + (here < shards - 1).astype(jnp.int32)
-        pl.semaphore_wait(barrier, bits + ends)
+
+        @pl.loop(1, peers)
+        def _(step):
+            pl.semaphore_signal(barrier, inc=1, device_id=peer(step)[1], device_id_type=MESH)
+        pl.semaphore_wait(barrier, peers - 1)
+
+        @pl.loop(1, peers)
+        def _(step):
+            vector_copy(*peer(step)).start()
 
         for path in range(2):
             for way in range(2):
@@ -608,34 +639,50 @@
                 def finish(part):
                     piece[path, slot, part] = total(part, 0).astype(BF16)
                 by_rows(rows, finish)
-                store(path, chunk).start()
-                gather(path, 0, chunk).start()
-
-        def place(path, chunk, rows, row):
-            return out.at[chunk, pl.ds(pl.multiple_of(row, rows), rows), pl.ds(path * width, width)]
-
-        def store(path, chunk):
+                spread(path, 0, chunk)
+
+        def placed(path, chunk, rows, row, run):
+            start = 0
+            for which, (count, blocks, _, _) in enumerate(seats):
+                def each(which=which, start=start, blocks=blocks):
+                    local = chunk - start
+                    outer = lax.div(local, blocks)
+                    column = (local - outer * blocks) * (2 * width) + path * width
+                    run(outs[which].at[
+                        pl.ds(pl.multiple_of(outer * unit_rows + row, rows), rows),
+                        pl.ds(pl.multiple_of(column, width), width)])
+                on((chunk >= start) & (chunk < start + count), each)
+                start += count
+
+        def any_place(rows):
+            return outs[0].at[pl.ds(0, rows), pl.ds(0, width)]
+
+        def store(path, chunk, target):
             slot = lax.rem(chunk, 4)
-            return pltpu.make_async_copy(
-                piece.at[path, slot], place(path, chunk, final_rows, seat_row(path, others)),
-                store_sem.at[path, slot])
-
-        def gather(path, step, chunk):
+            return pltpu.make_async_copy(piece.at[path, slot], target, store_sem.at[path, slot])
+
+        def gather(path, step, chunk, target):
             slot = lax.rem(chunk, 4)
-            rows = final_rows << step
-            target = place(path, chunk, rows, seat_row(path, others - step))
             source = piece.at[path, slot] if step == 0 else target
             return remote(source, target, gather_send.at[path, step, slot],
                           gather_recv.at[path, step, slot], across(sides[path][step]))
 
+        def spread(path, step, chunk):
+            def launch(target):
+                if step == 0:
+                    store(path, chunk, target).start()
+                gather(path, step, chunk, target).start()
+            placed(path, chunk, final_rows << step, seat_row(path, others - step), launch)
+
         def gathered(path, step, chunk):
-            copy = gather(path, step, chunk)
+            target = any_place(final_rows << step)
+            copy = gather(path, step, chunk, target)
             copy.wait_recv()
             copy.wait_send()
             if step == 0:
-                store(path, chunk).wait()
+                store(path, chunk, target).wait()
             if step + 1 < bits:
-                gather(path, step + 1, chunk).start()
+                spread(path, step + 1, chunk)
 
         lag_last = shards + others + bits
         rounds = units + lag_last + 2
@@ -666,13 +713,15 @@
                     chunk = turn - shards - others - 1 - step
                     on(valid(chunk), lambda path=path, step=step, chunk=chunk: gathered(path, step, chunk))
 
+        vector_finish()
+
     if section is None:
         work()
     else:
         pl.when(sec == section)(work)
 
 
-def exchange(pairs, shards, group, section, collective_id, unit_width, previous=None, unit_rows_max=256,
+def exchange(pairs, vector, shards, group, section, collective_id, unit_width, previous=None, unit_rows_max=256,
              name="exchange"):
     bits = group.bit_length() - 1
     lefts, rights = [p[0] for p in pairs], [p[1] for p in pairs]
@@ -689,7 +738,12 @@
     final_rows = unit_rows >> bits
     depth = shards + 3
     dma = pltpu.SemaphoreType.DMA
+    peers = shards * group
+    lanes = vector.shape[1] // shards
     scratch = [
+        pltpu.VMEM((peers, vector.shape[0], lanes), F32),
+        pltpu.VMEM((vector.shape[0], lanes), F32),
+        dma((peers,)), dma((peers,)), dma,
         pltpu.VMEM((2, shards, tokens, unit_rows), BF16),
         pltpu.VMEM((2, tokens, unit_width), BF16),
         dma((2, shards)), dma((2,)),
@@ -709,14 +763,19 @@
         dma((2, bits, 4)), dma((2, bits, 4)),
     ]
     cfg = (shards, bits, seats, unit_rows, width, section, previous is not None)
-    operands = lefts + rights + ([] if previous is None else [previous])
+    operands = lefts + rights + [vector] + list(previous or [])
+    first = 2 * len(pairs) + 1
+    results = [jax.ShapeDtypeStruct((r, g.shape[0] * g.shape[2]), BF16) for r, g in zip(rows_of, rights)]
+    results.append(jax.ShapeDtypeStruct((vector.shape[0], lanes), F32))
+    hbm, vmem = pl.BlockSpec(memory_space=pl.ANY), pl.BlockSpec(memory_space=pltpu.VMEM)
+    in_specs = [vmem if index == first - 1 else hbm for index in range(len(operands))]
     return pl.pallas_call(
         functools.partial(exchange_kernel, cfg),
-        out_shape=jax.ShapeDtypeStruct((units, unit_rows, unit_width), BF16),
-        in_specs=[pl.BlockSpec(memory_space=pl.ANY)] * len(operands),
-        out_specs=pl.BlockSpec(memory_space=pl.ANY),
+        out_shape=results,
+        in_specs=in_specs,
+        out_specs=[hbm] * len(results),
         scratch_shapes=scratch,
-        input_output_aliases={} if previous is None else {len(operands) - 1: 0},
+        input_output_aliases={first + index: index for index in range(len(previous or []))},
         name=name,
         cost_estimate=pl.CostEstimate(
             flops=2 * tokens * units * shards * unit_rows * unit_width, bytes_accessed=100 * 2 ** 20,
@@ -758,7 +817,8 @@
         branch, grad_qkv, grad_in, grad_in_low, gain_a, bias_a = attention_back(
             active, lengths, grad_middle, values, norm_gain_a, qkv, weight_qkv, weight_out, cosine, sine, parts)
         pairs = [(hidden, grad[None]), (low_f, grad_gu), (mixture, branch[None]), (low_a, grad_qkv)]
-        return result, grad_in, grad_in_low, pairs, jnp.concatenate([gain_a, bias_a, gain_f, bias_f], axis=0)
+        vectors = jnp.concatenate([gain_a, bias_a, gain_f, bias_f, jnp.zeros((4, features), F32)], axis=0)
+        return result, grad_in, grad_in_low, pairs, vectors
 
     middle_0, low_0, qkv_0, mixture_0 = attend(first, rows)
     passed = feed(first, middle_0, norm_gain_f, norm_bias_f, weight_gu, weight_down)
@@ -766,25 +826,12 @@
     middle_1, low_1, qkv_1, mixture_1 = attend(second, arrived)
     result, _, returned, pairs_1, vectors_1 = back(second, middle_1, low_1, qkv_1, mixture_1, arrived, rows)
     returned = lax.ppermute(returned, "section", [(1, 0)])
-    summed = exchange(pairs_1, shards, group, 1, 1, features, name="exchange_second")
+    summed = exchange(pairs_1, vectors_1, shards, group, 1, 1, features, name="exchange_second")
     _, grad_in, _, pairs_0, vectors_0 = back(first, middle_0, low_0, qkv_0, mixture_0, rows, returned)
-    summed = exchange(pairs_0, shards, group, 0, 2, features, previous=summed, name="exchange_first")
-    vectors = lax.psum(jnp.where(is_first, vectors_0, vectors_1), ("shard", "group"))
-    part = features // shards
-    vectors = lax.dynamic_slice(vectors, (0, lax.axis_index("shard") * part), (vectors.shape[0], part))
+    summed = exchange(pairs_0, vectors_0, shards, group, 0, 2, features, previous=summed, name="exchange_first")
     ends_out = jnp.where(is_first, grad_in, result)[None]
-    unit_rows = summed.shape[1]
-
-    def shaped(start, count, blocks):
-        picked = summed[start:start + count].astype(F32).reshape(count // blocks, blocks, unit_rows, features)
-        return jnp.transpose(picked, (0, 2, 1, 3)).reshape(1, count // blocks * unit_rows, blocks * features)
-
-    starts, counts, blocks = [0], [], []
-    for left, right in pairs_0:
-        blocks.append(right.shape[0] * right.shape[2] // features)
-        counts.append(left.shape[1] // shards // unit_rows * blocks[-1])
-        starts.append(starts[-1] + counts[-1])
-    grad_down, grad_gate_up, grad_out, grad_qkv = (shaped(*seat) for seat in zip(starts, counts, blocks))
+    grad_down, grad_gate_up, grad_out, grad_qkv = (item.astype(F32)[None] for item in summed[:4])
+    vectors = summed[4]
     return (
         ends_out,
         vectors[0:1],

time: 590 us -> 497 us (0.84)
  blocking collectives: 73 us -> 0 us
  local copies, waits for them, and re-layouts: 31.3 us -> 10.2 us
    psum x1 -> x0, blocking collectives: 73 us -> none  [body(): lax.psum(jnp.where(is_first, vectors_0, vectors_1), ('shard', 'group'))]
    broadcast_in_dim x0 -> x4, other arithmetic: none -> 12.7 us  [body(): item.astype(F32)[None]]
    unnamed x28 -> x22, local copies, waits for them, and re-layouts: 15.4 us -> 3.84 us
    reshape x2 -> x0, local copies, waits for them, and re-layouts: 11.5 us -> none  [shaped(): jnp.transpose(picked, (0, 2, 1, 3))]
    reshape x2 -> x0, other arithmetic: 7.19 us -> none  [shaped(): jnp.transpose(picked, (0, 2, 1, 3))]
where the time goes in v2:
time: 497 us; the launch traced here: 496 us
  Pallas kernels  380 us (76%)
  waiting for transfers between devices  86.6 us (17%)
  other arithmetic  15.7 us (3%)
  local copies, waits for them, and re-layouts  10.2 us (2%)
    pallas_call x2, Pallas kernels, exchange(): pl.pallas_call(functools.partial(exchange_kernel, cfg), out_shape=results...  236 us
    pallas_call x7, Pallas kernels, local_call(): pl.pallas_call(kernel, grid_spec=pltpu.PrefetchScalarGridSpec(num_scalar_...  145 us
    ppermute x1, waiting for transfers between devices, body(): returned = lax.ppermute(returned, 'section', [(1, 0)])  84.2 us
    broadcast_in_dim x4, other arithmetic, body(): item.astype(F32)[None]  12.7 us
  transfers between devices with their start and end apart: 2, of which 2 were waited for; matrix products, arithmetic and copies ran while one was open for 0% of the time, Pallas kernels for 1%

profile of v2, /device:TPU:0, one launch (start us, length us, event | category | flops | bytes accessed | tf_op | source)
XLA Modules:
  0.0 496.3 jit_solution(13289080488063882543)
XLA Ops:
  0.7 0.8 copy.33
  1.4 0.8 reduce_window_sum.11
  2.3 0.1 copy.32
  2.4 0.1 fusion
  2.5 0.3 multiply_sine_fusion
  2.8 0.1 tile.20
  2.8 1.0 copy.35.sin_ref
  3.9 1.0 copy.34.cos_ref
  4.9 24.6 %attention.2 = (f32[512,1024]{1,0:T(8,128)}, bf16[512,1024]{1,0:T(8,128)(2,1)}, bf16[3,512,1024]{2,1,0:T(8,128)(2,1)}, bf16[512,1024]{1,0:T(8,128)(2,1)}) custom-call(s32[1]{0:T(128)} %bitcast.act_ref, s32[2,3]{1,0:T(2,128)} %lengths_ref.7, bf16[512,1024]{1,0:T(8,128)(2,1)} %bitcast.47, f32[1,1024]{1,0:T(1,128)} %gain_ref.13, f32[1,1024]{1,0:T(1,128)} %bias_ref.7, ...), custom_call_target="tpu_custom_call" | custom-call | flops 4294967296 | bytes 41943040 | tf_op jit(solution)/shard_map/attention/pallas_call | solution.py:306
  29.6 23.3 %feed.1 = bf16[512,1024]{1,0:T(8,128)(2,1)} custom-call(s32[1]{0:T(128)} %bitcast.act_ref, f32[512,1024]{1,0:T(8,128)} %get-tuple-element.50.mid_ref, f32[1,1024]{1,0:T(1,128)} %gain_ref.12, f32[1,1024]{1,0:T(1,128)} %bias_ref.9, bf16[1024,8192]{1,0:T(8,128)(2,1)} %bitcast.51, bf16[1024,8192]{1,0:T(8,128)(2,1)} %bitcast.52, bf16[4096,1024]{1,0:T(8,128)(2,1)} %bitcast.57), custom_call_target="tpu_custom_call" | custom-call | flops 12884901888 | bytes 41943040 | tf_op jit(solution)/shard_map/feed/pallas_call | solution.py:306
  52.9 1.3 collective-permute-start
  54.2 2.4 collective-permute-done.x_ref
  56.6 1.0 copy-done.4
  57.6 5.2 %attention.3 = (f32[512,1024]{1,0:T(8,128)}, bf16[512,1024]{1,0:T(8,128)(2,1)}, bf16[3,512,1024]{2,1,0:T(8,128)(2,1)}, bf16[512,1024]{1,0:T(8,128)(2,1)}) custom-call(s32[1]{0:T(128)} %bitcast.6.act_ref, s32[2,3]{1,0:T(2,128)} %lengths_ref.7, bf16[512,1024]{1,0:T(8,128)(2,1)} %copy-done.4, f32[1,1024]{1,0:T(1,128)} %gain_ref.13, f32[1,1024]{1,0:T(1,128)} %bias_ref.7, ...), custom_call_target="tpu_custom_call" | custom-call | flops 4294967296 | bytes 41943040 | tf_op jit(solution)/shard_map/attention/pallas_call | solution.py:306
  62.8 5.8 %feed_both.2 = (f32[512,1024]{1,0:T(8,128)}, bf16[512,1024]{1,0:T(8,128)(2,1)}, bf16[512,4096]{1,0:T(8,128)(2,1)}, bf16[2,512,4096]{2,1,0:T(8,128)(2,1)}, f32[51...) custom-call(s32[1]{0:T(128)} %bitcast.6.act_ref, f32[512,1024]{1,0:T(8,128)} %get-tuple-element.51.mid_ref, ...), custom_call_target="tpu_custom_call" | custom-call | flops 25769803776 | bytes 41943040 | tf_op jit(solution)/shard_map/feed_both/pallas_call | solution.py:306
  68.6 6.5 %attention_back.2 = (bf16[512,1024]{1,0:T(8,128)(2,1)}, bf16[3,512,1024]{2,1,0:T(8,128)(2,1)}, f32[512,1024]{1,0:T(8,128)}, bf16[512,1024]{1,0:T(8,128)(2,1)}, f32[1,1024]{1,0:T(1,128)}, /*index=5*/f32[1,1024]{1,0:T(1,128)}) custom-call(s32[1]{0:T(128)} %bitcast.6.act_ref, s32[2,3]{1,0:T(2,128)} %lengths_ref.7, f32[512,1024]{1,0:T(8,128)} %get-tuple-element.52.grad_ref, ...), custom_call_target="tpu_custom_call" | custom-call | flops 10737418240 | bytes 41943040 | tf_op jit(solution)/shard_map/attention_back/pallas_call | solution.py:306
  75.0 1.3 collective-permute-start.1
  76.4 1.3 concatenate.7.refs_8_
  77.7 3.8 exchange_second.1
  81.5 84.2 %collective-permute-done.1.grad_ref = bf16[512,1024]{1,0:T(8,128)(2,1)S(1)} collective-permute-done((bf16[512,1024]{1,0:T(8,128)(2,1)}, bf16[512,1024]{1,0:T(8,128)(2,1)S(1)}, u32[]{:S(2)}, u32[]{:S(2)}) %collective-permute-start.1) | collective-permute-done | bytes 1048608 | tf_op jit(solution)/shard_map/ppermute | solution.py:828
  165.7 1.0 copy-done.9
  166.7 43.3 %feed_both.3 = (f32[512,1024]{1,0:T(8,128)}, bf16[512,1024]{1,0:T(8,128)(2,1)}, bf16[512,4096]{1,0:T(8,128)(2,1)}, bf16[2,512,4096]{2,1,0:T(8,128)(2,1)}, f32[51...) custom-call(s32[1]{0:T(128)} %bitcast.act_ref, f32[512,1024]{1,0:T(8,128)} %get-tuple-element.50.mid_ref, ...), custom_call_target="tpu_custom_call" | custom-call | flops 25769803776 | bytes 41943040 | tf_op jit(solution)/shard_map/feed_both/pallas_call | solution.py:306
  210.0 36.2 %attention_back.3 = (bf16[512,1024]{1,0:T(8,128)(2,1)}, bf16[3,512,1024]{2,1,0:T(8,128)(2,1)}, f32[512,1024]{1,0:T(8,128)}, bf16[512,1024]{1,0:T(8,128)(2,1)}, f32[1,1024]{1,0:T(1,128)}, /*index=5*/f32[1,1024]{1,0:T(1,128)}) custom-call(s32[1]{0:T(128)} %bitcast.act_ref, s32[2,3]{1,0:T(2,128)} %lengths_ref.7, f32[512,1024]{1,0:T(8,128)} %get-tuple-element.55.grad_ref, ...), custom_call_target="tpu_custom_call" | custom-call | flops 10737418240 | bytes 41943040 | tf_op jit(solution)/shard_map/attention_back/pallas_call | solution.py:306
  246.2 1.3 concatenate.6.refs_8_
  247.6 231.8 %exchange_first.1 = (bf16[1024,1024]{1,0:T(8,128)(2,1)}, bf16[256,8192]{1,0:T(8,128)(2,1)}, bf16[256,1024]{1,0:T(8,128)(2,1)}, bf16[256,3072]{1,0:T(8,128)(2,1)}, f32[8,256]{1,0:T(8,128)}) custom-call(bf16[512,4096]{1,0:T(8,128)(2,1)} %get-tuple-element.59.refs_0_, ...), custom_call_target="tpu_custom_call", output_to_operand_aliasing={{0}: (9, {}), {1}: (10, {}), {2}: (11, {}), {3}: (12, {}), ... | custom-call | flops 17179869184 | bytes 104857600 | tf_op jit(solution)/shard_map/exchange_first/pallas_call | solution.py:772
  479.3 1.4 fusion.1
  480.8 2.3 bitcast_convert_fusion.3
  483.0 3.4 bitcast_convert_fusion.2
  486.5 2.6 bitcast_convert_fusion.1
  489.1 1.1 copy-done
  490.2 4.4 bitcast_convert_fusion
  494.6 1.7 select_bitcast_fusion
  (22 shorter events, 0.1 us)
Async XLA Ops:
  52.9 3.8 collective-permute-start
  56.6 1.0 copy-start.4
  68.6 7.8 %copy-start.5 = (f32[1,1024]{1,0:T(1,128)S(1)}, f32[1,1024]{1,0:T(1,128)}, u32[]{:S(2)}) copy-start(f32[1,1024]{1,0:T(1,128)} %get-tuple-element.79) | copy-start | bytes 12292
  68.6 7.8 %copy-start.6 = (f32[1,1024]{1,0:T(1,128)S(1)}, f32[1,1024]{1,0:T(1,128)}, u32[]{:S(2)}) copy-start(f32[1,1024]{1,0:T(1,128)} %get-tuple-element.80) | copy-start | bytes 12292
  75.0 90.6 %collective-permute-start.1 = (bf16[512,1024]{1,0:T(8,128)(2,1)}, bf16[512,1024]{1,0:T(8,128)(2,1)S(1)}, u32[]{:S(2)}, u32[]{:S(2)}) collective-permute-start(bf16[512,1024]{1,0:T(8,128)(2,1)} %get-tuple-element.54), channel_id=1, source_target_pairs={{16,0},{17,1},{18,2},{19,3},{20,4},{21,5},{22,6},{23,7},{24,8},{25... | collective-permute-start | bytes 3145736 | tf_op jit(solution)/shard_map/ppermute | solution.py:828
  165.7 1.0 copy-start.9
  209.9 36.3 %copy-start.7 = (f32[1,1024]{1,0:T(1,128)S(1)}, f32[1,1024]{1,0:T(1,128)}, u32[]{:S(2)}) copy-start(f32[1,1024]{1,0:T(1,128)} %get-tuple-element.68) | copy-start | bytes 12292
  209.9 36.3 %copy-start.8 = (f32[1,1024]{1,0:T(1,128)S(1)}, f32[1,1024]{1,0:T(1,128)}, u32[]{:S(2)}) copy-start(f32[1,1024]{1,0:T(1,128)} %get-tuple-element.69) | copy-start | bytes 12292
  480.8 5.7 %copy-start.2 = (bf16[1024,1024]{1,0:T(8,128)(2,1)S(1)}, bf16[1024,1024]{1,0:T(8,128)(2,1)}, u32[]{:S(2)}) copy-start(bf16[1024,1024]{1,0:T(8,128)(2,1)} %get-tuple-element.90) | copy-start | bytes 6291460
  486.5 3.7 copy-start
  490.2 4.4 copy-start.1
  490.2 4.4 copy-start.3

commit v3 on v2

--- a/solution.py
+++ b/solution.py
@@ -109,33 +109,35 @@
                 mid_ref[rows] = values
             in_rows(tokens, 64, begin)
 
-        def project(rows):
-            low = low_ref[rows]
-            cosine, sine = cos_ref[rows], sin_ref[rows]
-            qkv_ref[0, rows] = rotated(dot(low, wq_ref[...]), cosine, sine, size).astype(BF16)
-            qkv_ref[1, rows] = rotated(dot(low, wk_ref[...]), cosine, sine, size).astype(BF16)
-            qkv_ref[2, rows] = dot(low, wv_ref[...]).astype(BF16)
-        in_rows(tokens, row_tokens, project)
-
-        @pl.loop(0, tokens // row_tokens)
-        def _(row):
-            rows = pl.ds(pl.multiple_of(row * row_tokens, row_tokens), row_tokens)
+        for which, weight in enumerate((wq_ref, wk_ref, wv_ref)):
+            projected = dot(low_ref[...], weight[...])
+            for at in range(block // pair):
+                lanes = slice(at * pair, (at + 1) * pair)
+                values = projected[:, lanes]
+                if which < 2:
+                    values = rotated(values, cos_ref[...], sin_ref[...], size)
+                qkv_ref[which, :, lanes] = values.astype(BF16)
+
+        first = lanes_of((row_tokens, pair)) < size
+        for row in range(tokens // row_tokens):
+            rows = pl.ds(row * row_tokens, row_tokens)
             allowed = same_window(lengths_ref, row, row_tokens)
-            first = lanes_of((row_tokens, pair)) < size
-            for at in range(block // pair):
-                lanes = pl.ds(at * pair, pair)
-                query, key, value = (qkv_ref[which, rows, lanes] for which in range(3))
-                query = query * (size ** -0.5)
-                results = []
-                for head in range(2):
-                    own = jnp.where(first if head == 0 else jnp.logical_not(first), query, jnp.zeros_like(query))
-                    probs = softmax(dot_cols(own, key), allowed)
-                    results.append(dot(probs.astype(BF16), value))
-                mix_ref[rows, lanes] = jnp.where(first, results[0], results[1]).astype(BF16)
-
-        def close(rows):
-            mid_ref[rows] += dot(mix_ref[rows], wo_ref[...])
-        in_rows(tokens, row_tokens, close)
+            for start in range(0, block // pair, 2):
+                work = []
+                for at in range(start, start + 2):
+                    lanes = pl.ds(at * pair, pair)
+                    query, key, value = (qkv_ref[which, rows, lanes] for which in range(3))
+                    query = query * (size ** -0.5)
+                    for head in range(2):
+                        own = jnp.where(first if head == 0 else jnp.logical_not(first), query, jnp.zeros_like(query))
+                        work.append((dot_cols(own, key), value))
+                work = [(softmax(scores, allowed).astype(BF16), value) for scores, value in work]
+                work = [dot(probs, value) for probs, value in work]
+                for at in range(2):
+                    lanes = pl.ds((start + at) * pair, pair)
+                    mix_ref[rows, lanes] = jnp.where(first, work[2 * at], work[2 * at + 1]).astype(BF16)
+
+        mid_ref[...] += dot(mix_ref[...], wo_ref[...])
 
 
 def attention_back_kernel(size, row_tokens, act_ref, lengths_ref, grad_ref, x_ref, gain_ref, qkv_ref, wq_ref, wk_ref,
@@ -145,6 +147,7 @@
     part = pl.program_id(0)
     block = wq_ref.shape[1]
     pair = 2 * size
+    scale = size ** -0.5
 
     @pl.when(act_ref[0] == 1)
     def _():
@@ -154,43 +157,48 @@
                 branch_ref[rows] = grad_ref[rows].astype(BF16)
             in_rows(tokens, 64, begin)
 
-        def mixture_grad(rows):
-            gm_ref[rows] = dot_cols(branch_ref[rows], wo_ref[...]).astype(BF16)
-        in_rows(tokens, row_tokens, mixture_grad)
-
-        @pl.loop(0, tokens // row_tokens)
-        def _(row):
-            rows = pl.ds(pl.multiple_of(row * row_tokens, row_tokens), row_tokens)
+        gm_ref[...] = dot_cols(branch_ref[...], wo_ref[...]).astype(BF16)
+        first = lanes_of((row_tokens, pair)) < size
+        for row in range(tokens // row_tokens):
+            rows = pl.ds(row * row_tokens, row_tokens)
             allowed = same_window(lengths_ref, row, row_tokens)
-            first = lanes_of((row_tokens, pair)) < size
-            for at in range(block // pair):
-                lanes = pl.ds(at * pair, pair)
-                query, key, value = (qkv_ref[which, rows, lanes] for which in range(3))
-                grad_mix = gm_ref[rows, lanes]
-                scaled = query * (size ** -0.5)
+            cosine, sine = cos_ref[rows], sin_ref[rows]
+            for start in range(0, block // pair, 2):
+                work = []
+                for at in range(start, start + 2):
+                    lanes = pl.ds(at * pair, pair)
+                    query, key, value = (qkv_ref[which, rows, lanes] for which in range(3))
+                    grad_mix = gm_ref[rows, lanes]
+                    scaled = query * scale
+                    for head in range(2):
+                        mine = first if head == 0 else jnp.logical_not(first)
+                        work.append((
+                            query, key, grad_mix,
+                            dot_cols(jnp.where(mine, scaled, jnp.zeros_like(scaled)), key),
+                            dot_cols(jnp.where(mine, grad_mix, jnp.zeros_like(grad_mix)), value)))
                 results = []
-                for head in range(2):
-                    mine = first if head == 0 else jnp.logical_not(first)
-                    probs = softmax(dot_cols(jnp.where(mine, scaled, jnp.zeros_like(scaled)), key), allowed)
-                    grad_probs = dot_cols(jnp.where(mine, grad_mix, jnp.zeros_like(grad_mix)), value)
-                    grad_value = dot_rows(probs.astype(BF16), grad_mix)
+                for query, key, grad_mix, scores, grad_probs in work:
+                    probs = softmax(scores, allowed)
                     weighted = probs * grad_probs
                     grad_scores = (weighted - probs * jnp.sum(weighted, axis=-1, keepdims=True)).astype(BF16)
-                    results.append((dot(grad_scores, key), dot_rows(grad_scores, query), grad_value))
-                grad_query, grad_key, grad_value = (jnp.where(first, a, b) for a, b in zip(*results))
-                cosine, sine = cos_ref[rows, lanes], sin_ref[rows, lanes]
-                proj_ref[0, rows, lanes] = unrotated(grad_query * (size ** -0.5), cosine, sine, size).astype(BF16)
-                proj_ref[1, rows, lanes] = unrotated(grad_key * (size ** -0.5), cosine, sine, size).astype(BF16)
-                proj_ref[2, rows, lanes] = grad_value.astype(BF16)
-
-        def normed_grad(rows):
-            added = (
-                dot_cols(proj_ref[0, rows], wq_ref[...])
-                + dot_cols(proj_ref[1, rows], wk_ref[...])
-                + dot_cols(proj_ref[2, rows], wv_ref[...])
-            )
-            total_ref[rows] = jnp.where(part == 0, added, total_ref[rows] + added)
-        in_rows(tokens, row_tokens, normed_grad)
+                    results.append((query, key, grad_mix, grad_scores, probs.astype(BF16)))
+                results = [
+                    (dot(grad_scores, key), dot_rows(grad_scores, query), dot_rows(probs, grad_mix))
+                    for query, key, grad_mix, grad_scores, probs in results]
+                for at in range(2):
+                    lanes = pl.ds((start + at) * pair, pair)
+                    grad_query, grad_key, grad_value = (
+                        jnp.where(first, a, b) for a, b in zip(results[2 * at], results[2 * at + 1]))
+                    proj_ref[0, rows, lanes] = unrotated(grad_query * scale, cosine, sine, size).astype(BF16)
+                    proj_ref[1, rows, lanes] = unrotated(grad_key * scale, cosine, sine, size).astype(BF16)
+                    proj_ref[2, rows, lanes] = grad_value.astype(BF16)
+
+        added = (
+            dot_cols(proj_ref[0], wq_ref[...])
+            + dot_cols(proj_ref[1], wk_ref[...])
+            + dot_cols(proj_ref[2], wv_ref[...])
+        )
+        total_ref[...] = jnp.where(part == 0, added, total_ref[...] + added)
 
         @pl.when(part == pl.num_programs(0) - 1)
         def _():
@@ -208,7 +216,7 @@
             in_rows(tokens, 64, finish)
 
 
-def feed_kernel(row_tokens, act_ref, mid_ref, gain_ref, bias_ref, wg_ref, wu_ref, wd_ref, out_ref, low_ref, total_ref):
+def feed_kernel(act_ref, mid_ref, gain_ref, bias_ref, wg_ref, wu_ref, wd_ref, out_ref, low_ref, total_ref):
     tokens = mid_ref.shape[0]
     part = pl.program_id(0)
 
@@ -223,13 +231,11 @@
                 total_ref[rows] = values
             in_rows(tokens, 64, begin)
 
-        def step(rows):
-            low = low_ref[rows]
-            gate = dot(low, wg_ref[...])
-            up = dot(low, wu_ref[...])
-            hidden = (gate / (1.0 + jnp.exp(-gate)) * up).astype(BF16)
-            total_ref[rows] += dot(hidden, wd_ref[...])
-        in_rows(tokens, row_tokens, step)
+        low = low_ref[...]
+        gate = dot(low, wg_ref[...])
+        up = dot(low, wu_ref[...])
+        hidden = (gate / (1.0 + jnp.exp(-gate)) * up).astype(BF16)
+        total_ref[...] += dot(hidden, wd_ref[...])
 
         @pl.when(part == pl.num_programs(0) - 1)
         def _():
@@ -238,7 +244,7 @@
             in_rows(tokens, 64, finish)
 
 
-def feed_both_kernel(row_tokens, act_ref, mid_ref, grad_ref, gain_ref, bias_ref, wg_ref, wu_ref, wd_ref, out_ref,
+def feed_both_kernel(act_ref, mid_ref, grad_ref, gain_ref, bias_ref, wg_ref, wu_ref, wd_ref, out_ref,
                      low_ref, hidden_ref, ggu_ref, grad_mid_ref, dgain_ref, dbias_ref, total_ref):
     tokens = mid_ref.shape[0]
     part = pl.program_id(0)
@@ -254,23 +260,18 @@
                 out_ref[rows] = values
             in_rows(tokens, 64, begin)
 
-        def step(rows):
-            low = low_ref[rows]
-            gate = dot(low, wg_ref[...])
-            up = dot(low, wu_ref[...])
-            sig = 1.0 / (1.0 + jnp.exp(-gate))
-            silu = gate * sig
-            hidden = (silu * up).astype(BF16)
-            hidden_ref[rows] = hidden
-            out_ref[rows] += dot(hidden, wd_ref[...])
-            grad_hidden = dot_cols(grad_ref[rows], wd_ref[...])
-            grad_gate = (grad_hidden * up * (sig * (1.0 + gate * (1.0 - sig)))).astype(BF16)
-            grad_up = (grad_hidden * silu).astype(BF16)
-            ggu_ref[0, rows] = grad_gate
-            ggu_ref[1, rows] = grad_up
-            added = dot_cols(grad_gate, wg_ref[...]) + dot_cols(grad_up, wu_ref[...])
-            total_ref[rows] = jnp.where(part == 0, added, total_ref[rows] + added)
-        in_rows(tokens, row_tokens, step)
+        low = low_ref[...]
+        gate = dot(low, wg_ref[...])
+        up = dot(low, wu_ref[...])
+        grad_hidden = dot_cols(grad_ref[...], wd_ref[...])
+        sig = 1.0 / (1.0 + jnp.exp(-gate))
+        silu = gate * sig
+        hidden_ref[...] = (silu * up).astype(BF16)
+        ggu_ref[0] = (grad_hidden * up * (sig * (1.0 + gate * (1.0 - sig)))).astype(BF16)
+        ggu_ref[1] = (grad_hidden * silu).astype(BF16)
+        out_ref[...] += dot(hidden_ref[...], wd_ref[...])
+        added = dot_cols(ggu_ref[0], wg_ref[...]) + dot_cols(ggu_ref[1], wu_ref[...])
+        total_ref[...] = jnp.where(part == 0, added, total_ref[...] + added)
 
         @pl.when(part == pl.num_programs(0) - 1)
         def _():
@@ -316,7 +317,7 @@
     )(*scalars, *args)
 
 
-def attention(active, lengths, x, gain, bias, w_qkv, w_out, cosine, sine, parts=4):
+def attention(active, lengths, x, gain, bias, w_qkv, w_out, cosine, sine, parts=2):
     tokens, features = x.shape
     row_tokens = tokens // lengths.shape[0]
     size = features // HEADS
@@ -326,14 +327,14 @@
         (x, gain, bias, w_qkv, w_qkv, w_qkv, w_out, cosine, sine),
         [whole((tokens, features)), whole((1, features)), whole((1, features)), column(features, wide),
          column(features, wide, parts), column(features, wide, 2 * parts), lower(wide, features),
-         whole((tokens, wide)), whole((tokens, wide))],
+         whole(cosine.shape), whole(sine.shape)],
         (jax.ShapeDtypeStruct((tokens, features), F32), jax.ShapeDtypeStruct((tokens, features), BF16),
          jax.ShapeDtypeStruct((3, tokens, features), BF16), jax.ShapeDtypeStruct((tokens, features), BF16)),
         (whole((tokens, features)), whole((tokens, features)), stacked(3, tokens, wide), column(tokens, wide)),
         [], 8 * tokens * features ** 2)
 
 
-def attention_back(active, lengths, grad_mid, x, gain, qkv, w_qkv, w_out, cosine, sine, parts=4):
+def attention_back(active, lengths, grad_mid, x, gain, qkv, w_qkv, w_out, cosine, sine, parts=2):
     tokens, features = x.shape
     row_tokens = tokens // lengths.shape[0]
     size = features // HEADS
@@ -344,7 +345,7 @@
         (grad_mid, x, gain, qkv, w_qkv, w_qkv, w_qkv, w_out, cosine, sine),
         [whole((tokens, features)), whole((tokens, features)), whole((1, features)), stacked(3, tokens, wide),
          column(features, wide), column(features, wide, parts), column(features, wide, 2 * parts),
-         lower(wide, features), whole((tokens, wide)), whole((tokens, wide))],
+         lower(wide, features), whole(cosine.shape), whole(sine.shape)],
         (jax.ShapeDtypeStruct((tokens, features), BF16), jax.ShapeDtypeStruct((3, tokens, features), BF16),
          jax.ShapeDtypeStruct((tokens, features), F32), jax.ShapeDtypeStruct((tokens, features), BF16),
          vector, vector),
@@ -357,7 +358,7 @@
     tokens, features = mid.shape
     wide = w_down.shape[0] // parts
     return local_call(
-        functools.partial(feed_kernel, tokens // 2), "feed", parts, (active,),
+        feed_kernel, "feed", parts, (active,),
         (mid, gain, bias, w_gate_up, w_gate_up, w_down),
         [whole((tokens, features)), whole((1, features)), whole((1, features)), column(features, wide),
          column(features, wide, parts), lower(wide, features)],
@@ -372,7 +373,7 @@
     wide = hidden // parts
     vector = jax.ShapeDtypeStruct((1, features), F32)
     return local_call(
-        functools.partial(feed_both_kernel, tokens // 2), "feed_both", parts, (active,),
+        feed_both_kernel, "feed_both", parts, (active,),
         (mid, grad, gain, bias, w_gate_up, w_gate_up, w_down),
         [whole((tokens, features)), whole((tokens, features)), whole((1, features)), whole((1, features)),
          column(features, wide), column(features, wide, parts), lower(wide, features)],
@@ -384,7 +385,7 @@
         [pltpu.VMEM((tokens, features), F32)], 12 * tokens * features * hidden)
 
 
-def tables(lengths, row_tokens, size, repeat):
+def tables(lengths, row_tokens, size):
     ends = jnp.cumsum(lengths, axis=-1)
     index = jnp.arange(row_tokens, dtype=jnp.int32)
     passed = index[:, None] >= ends[..., None, :]
@@ -392,7 +393,7 @@
     position = (index - before).reshape(-1)
     frequency = 10000.0 ** (-2.0 * jnp.arange(size // 2, dtype=F32) / size)
     angles = position.astype(F32)[:, None] * frequency
-    return jnp.tile(jnp.cos(angles), (1, 2 * repeat)), jnp.tile(jnp.sin(angles), (1, 2 * repeat))
+    return jnp.tile(jnp.cos(angles), (1, 4)), jnp.tile(jnp.sin(angles), (1, 4))
 
 
 def exchange_kernel(cfg, *refs):
@@ -400,7 +401,7 @@
     arrays = len(seats)
     lefts, rights = refs[:arrays], refs[arrays:2 * arrays]
     vector = refs[2 * arrays]
-    refs = refs[2 * arrays + 1 + (arrays + 1 if aliased else 0):]
+    refs = refs[2 * arrays + 1 + (arrays if aliased else 0):]
     outs, vector_out = refs[:arrays], refs[arrays]
     (vector_land, vector_sum, vector_send, vector_recv, vector_store, left, right, left_sem, right_sem, own, give, landed, mine, chain, rest_send, rest_land, rest_keep, piece,
      land_send, land_recv, chain_send, chain_recv,
@@ -514,7 +515,7 @@
                     for shard in range(shards):
                         offset = pl.multiple_of(shard * rows + row * unit_rows, unit_rows)
                         run(pltpu.make_async_copy(
-                            lefts[which].at[:, pl.ds(offset, unit_rows)], left.at[slot, shard],
+                            lefts[which].at[:, pl.ds(offset, unit_rows)], left.at[slot, :, shard * unit_rows:(shard + 1) * unit_rows],
                             left_sem.at[slot, shard]))
                 on((chunk >= start) & (chunk < start + count), each)
                 start += count
@@ -528,14 +529,14 @@
             two = lax.rem(chunk, 2)
             away = (1 - bit_of(first[path])) * half
 
+            own[path, two] = lax.dot_general(
+                left[two], right[two, :, path * width:(path + 1) * width],
+                (((0,), (0,)), ((), ())), preferred_element_type=F32)
+
             @pl.loop(0, shards)
             def _(block):
-                own[path, two, block] = lax.dot_general(
-                    left[two, block], right[two, :, path * width:(path + 1) * width],
-                    (((0,), (0,)), ((), ())), preferred_element_type=F32)
-
                 def round_off(rows):
-                    give[path, two, block, rows] = own[path, two, block, shifted(rows, away)].astype(BF16)
+                    give[path, two, block, rows] = own[path, two, shifted(rows, block * unit_rows + away)].astype(BF16)
                 by_rows(half, round_off)
             first_copy(path, chunk).start()
 
@@ -550,7 +551,7 @@
             def _(block):
                 def add(rows):
                     mine[path, slot, block, rows] = (
-                        own[path, two, block, shifted(rows, kept)] + landed[path, four, block, rows].astype(F32)
+                        own[path, two, shifted(rows, block * unit_rows + kept)] + landed[path, four, block, rows].astype(F32)
                     ).astype(BF16)
                 by_rows(half, add)
 
@@ -721,7 +722,7 @@
         pl.when(sec == section)(work)
 
 
-def exchange(pairs, vector, shards, group, section, collective_id, unit_width, previous=None, unit_rows_max=256,
+def exchange(pairs, vector, shards, group, section, collective_id, unit_width, previous=None, after=None, unit_rows_max=256,
              name="exchange"):
     bits = group.bit_length() - 1
     lefts, rights = [p[0] for p in pairs], [p[1] for p in pairs]
@@ -744,10 +745,10 @@
         pltpu.VMEM((peers, vector.shape[0], lanes), F32),
         pltpu.VMEM((vector.shape[0], lanes), F32),
         dma((peers,)), dma((peers,)), dma,
-        pltpu.VMEM((2, shards, tokens, unit_rows), BF16),
+        pltpu.VMEM((2, tokens, shards * unit_rows), BF16),
         pltpu.VMEM((2, tokens, unit_width), BF16),
         dma((2, shards)), dma((2,)),
-        pltpu.VMEM((2, 2, shards, unit_rows, width), F32),
+        pltpu.VMEM((2, 2, shards * unit_rows, width), F32),
         pltpu.VMEM((2, 2, shards, half, width), BF16),
         pltpu.VMEM((2, 4, shards, half, width), BF16),
         pltpu.VMEM((2, shards + 2, shards, half, width), BF16),
@@ -763,6 +764,8 @@
         dma((2, bits, 4)), dma((2, bits, 4)),
     ]
     cfg = (shards, bits, seats, unit_rows, width, section, previous is not None)
+    if after is not None:
+        vector, _ = lax.optimization_barrier((vector, after))
     operands = lefts + rights + [vector] + list(previous or [])
     first = 2 * len(pairs) + 1
     results = [jax.ShapeDtypeStruct((r, g.shape[0] * g.shape[2]), BF16) for r, g in zip(rows_of, rights)]
@@ -805,33 +808,54 @@
     size = features // HEADS
     rows = ends_in[0]
     weight_qkv, weight_out, weight_gu, weight_down = w_qkv[0], w_out[0], w_gate_up[0], w_down[0]
-    parts = 4
-    cosine, sine = tables(lengths, tokens // lengths.shape[0], size, HEADS // parts)
+    cosine, sine = tables(lengths, tokens // lengths.shape[0], size)
+    nothing = jnp.zeros((2, features), F32)
 
     def attend(active, values):
-        return attention(active, lengths, values, norm_gain_a, norm_bias_a, weight_qkv, weight_out, cosine, sine, parts)
-
-    def back(active, middle, low_a, qkv, mixture, values, grad):
-        result, low_f, hidden, grad_gu, grad_middle, gain_f, bias_f = feed_both(
-            active, middle, grad, norm_gain_f, norm_bias_f, weight_gu, weight_down)
-        branch, grad_qkv, grad_in, grad_in_low, gain_a, bias_a = attention_back(
-            active, lengths, grad_middle, values, norm_gain_a, qkv, weight_qkv, weight_out, cosine, sine, parts)
-        pairs = [(hidden, grad[None]), (low_f, grad_gu), (mixture, branch[None]), (low_a, grad_qkv)]
-        vectors = jnp.concatenate([gain_a, bias_a, gain_f, bias_f, jnp.zeros((4, features), F32)], axis=0)
-        return result, grad_in, grad_in_low, pairs, vectors
+        return attention(active, lengths, values, norm_gain_a, norm_bias_a, weight_qkv, weight_out, cosine, sine)
+
+    def feed_back(active, middle, grad):
+        return feed_both(active, middle, grad, norm_gain_f, norm_bias_f, weight_gu, weight_down)
+
+    def attend_back(grad_middle, values, gain, qkv, weight_qkv, weight_out):
+        return attention_back(first, lengths, grad_middle, values, gain, qkv, weight_qkv, weight_out, cosine, sine)
+
+    def upward(*arrays):
+        return [lax.ppermute(array, "section", [(0, 1)]) for array in arrays]
+
+    def downward(*arrays):
+        return [lax.ppermute(array, "section", [(1, 0)]) for array in arrays]
 
     middle_0, low_0, qkv_0, mixture_0 = attend(first, rows)
     passed = feed(first, middle_0, norm_gain_f, norm_bias_f, weight_gu, weight_down)
-    arrived = lax.ppermute(passed, "section", [(0, 1)])
+    (arrived,) = upward(passed)
+    _, later_qkv, later_out, later_gain = lax.optimization_barrier((passed, weight_qkv, weight_out, norm_gain_a))
+    later_qkv, later_out, later_gain = downward(later_qkv, later_out, later_gain)
     middle_1, low_1, qkv_1, mixture_1 = attend(second, arrived)
-    result, _, returned, pairs_1, vectors_1 = back(second, middle_1, low_1, qkv_1, mixture_1, arrived, rows)
-    returned = lax.ppermute(returned, "section", [(1, 0)])
-    summed = exchange(pairs_1, vectors_1, shards, group, 1, 1, features, name="exchange_second")
-    _, grad_in, _, pairs_0, vectors_0 = back(first, middle_0, low_0, qkv_0, mixture_0, rows, returned)
-    summed = exchange(pairs_0, vectors_0, shards, group, 0, 2, features, previous=summed, name="exchange_first")
+    (qkv_there,) = downward(qkv_1)
+    result, low_f, hidden, grad_gu, grad_middle, gain_f, bias_f = feed_back(second, middle_1, rows)
+    (grad_middle,) = downward(grad_middle)
+    feed_sums = exchange(
+        [(hidden, rows[None]), (low_f, grad_gu)], jnp.concatenate([nothing, gain_f, bias_f, nothing, nothing], axis=0),
+        shards, group, 1, 1, features, name="exchange_second_feed")
+    branch, grad_qkv, _, returned, gain_a, bias_a = attend_back(
+        grad_middle, passed, later_gain, qkv_there, later_qkv, later_out)
+    branch, grad_qkv, attention_vectors = upward(branch, grad_qkv, jnp.concatenate([gain_a, bias_a], axis=0))
+    _, low_f, hidden, grad_gu, grad_middle, gain_f, bias_f = feed_back(first, middle_0, returned)
+    branch_0, grad_qkv_0, grad_in, _, gain_a, bias_a = attend_back(
+        grad_middle, rows, norm_gain_a, qkv_0, weight_qkv, weight_out)
+    attention_sums = exchange(
+        [(mixture_1, branch[None]), (low_1, grad_qkv)],
+        jnp.concatenate([attention_vectors, nothing, nothing, nothing], axis=0),
+        shards, group, 1, 2, features, after=feed_sums[-1], name="exchange_second_attention")
+    vectors = feed_sums[-1] + attention_sums[-1]
+    sums = exchange(
+        [(hidden, returned[None]), (low_f, grad_gu), (mixture_0, branch_0[None]), (low_0, grad_qkv_0)],
+        jnp.concatenate([gain_a, bias_a, gain_f, bias_f, nothing, nothing], axis=0),
+        shards, group, 0, 3, features, previous=feed_sums[:-1] + attention_sums[:-1], name="exchange_first")
     ends_out = jnp.where(is_first, grad_in, result)[None]
-    grad_down, grad_gate_up, grad_out, grad_qkv = (item.astype(F32)[None] for item in summed[:4])
-    vectors = summed[4]
+    grad_down, grad_gate_up, grad_out, grad_qkv = (item.astype(F32)[None] for item in sums[:4])
+    vectors = jnp.where(is_first, sums[4], vectors)
     return (
         ends_out,
         vectors[0:1],

time: 497 us -> 547 us (1.10); the launches traced: 496 us -> 537 us
  starting transfers between devices: 2.62 us -> 138 us
  Pallas kernels: 380 us -> 323 us
  waiting for transfers between devices: 86.6 us -> 46.6 us
    ppermute x2 -> x9, starting transfers between devices: 2.62 us -> 138 us  [the longest x4 131 us: upward(): return [lax.ppermute(array, 'section', [(0, 1)]) for array in arrays]]
    pallas_call x2 -> x3, Pallas kernels: 236 us -> 181 us  [exchange(): pl.pallas_call(functools.partial(exchange_kernel, cfg), out_shape=results...]
    ppermute x2 -> x9, waiting for transfers between devices: 86.6 us -> 46.6 us  [the longest x5 45.5 us: downward(): return [lax.ppermute(array, 'section', [(1, 0)]) for array in arrays]]
  transfers between devices with their start and end apart: 2 -> 9, of which waited for: 2 -> 3; matrix products, arithmetic and copies ran while one was open for 0% -> 1% of each run, Pallas kernels for 1% -> 15%
where the time goes in v3:
time: 547 us; the launch traced here: 537 us
  Pallas kernels  323 us (59%)
  starting transfers between devices  138 us (25%)
  waiting for transfers between devices  46.6 us (9%)
  other arithmetic  20.2 us (4%)
  local copies, waits for them, and re-layouts  8.82 us (2%)
    pallas_call x3, Pallas kernels, exchange(): pl.pallas_call(functools.partial(exchange_kernel, cfg), out_shape=results...  181 us
    pallas_call x7, Pallas kernels, local_call(): pl.pallas_call(kernel, grid_spec=pltpu.PrefetchScalarGridSpec(num_scalar_...  142 us
    ppermute x4, starting transfers between devices, upward(): return [lax.ppermute(array, 'section', [(0, 1)]) for array in arrays]  131 us
    ppermute x5, waiting for transfers between devices, downward(): return [lax.ppermute(array, 'section', [(1, 0)]) for array in arrays]  45.5 us
    broadcast_in_dim x4, other arithmetic, body(): item.astype(F32)[None]  12.7 us
  transfers between devices with their start and end apart: 9, of which 3 were waited for; matrix products, arithmetic and copies ran while one was open for 1% of the time, Pallas kernels for 15%

profile of v3, /device:TPU:0, one launch (start us, length us, event | category | flops | bytes accessed | tf_op | source)
XLA Modules:
  0.0 537.4 jit_solution(16202512766955541658)
XLA Ops:
  3.7 0.9 copy.33.cos_ref
  4.5 17.5 %attention.2 = (f32[512,1024]{1,0:T(8,128)}, bf16[512,1024]{1,0:T(8,128)(2,1)}, bf16[3,512,1024]{2,1,0:T(8,128)(2,1)}, bf16[512,1024]{1,0:T(8,128)(2,1)}) custom-call(s32[1]{0:T(128)} %bitcast.act_ref, s32[2,3]{1,0:T(2,128)} %lengths_ref.7, bf16[512,1024]{1,0:T(8,128)(2,1)} %bitcast.33, f32[1,1024]{1,0:T(1,128)} %gain_ref.11, f32[1,1024]{1,0:T(1,128)} %bias_ref.7, ...), custom_call_target="tpu_custom_call" | custom-call | flops 4294967296 | bytes 41943040 | tf_op jit(solution)/shard_map/attention/pallas_call | solution.py:307
  22.0 21.1 %feed.1.x_ref = bf16[512,1024]{1,0:T(8,128)(2,1)} custom-call(s32[1]{0:T(128)} %bitcast.act_ref, f32[512,1024]{1,0:T(8,128)} %get-tuple-element.55.mid_ref, f32[1,1024]{1,0:T(1,128)} %gain_ref.10, f32[1,1024]{1,0:T(1,128)} %bias_ref.9, bf16[1024,8192]{1,0:T(8,128)(2,1)} %bitcast.39, bf16[1024,8192]{1,0:T(8,128)(2,1)} %bitcast.40, bf16[4096,1024]{1,0:T(8,128)(2,1)} %bitcast.45), custom_call_target="tpu_custom_call" | custom-call | flops 12884901888 | bytes 41943040 | tf_op jit(solution)/shard_map/feed/pallas_call | solution.py:307
  43.2 1.3 collective-permute-start.4
  44.5 5.7 %collective-permute-start = (bf16[512,1024]{1,0:T(8,128)(2,1)}, bf16[512,1024]{1,0:T(8,128)(2,1)S(1)}, u32[]{:S(2)}, u32[]{:S(2)}) collective-permute-start(bf16[512,1024]{1,0:T(8,128)(2,1)} %feed.1.x_ref), channel_id=1, source_target_pairs={{0,16},{1,17},{2,18},{3,19},{4,20},{5,21},{6,22},{7,23},{8,24},{9,... | collective-permute-start | bytes 3145736 | tf_op jit(solution)/shard_map/ppermute | solution.py:824
  50.2 1.3 collective-permute-start.5
  51.5 1.1 collective-permute-done.x_ref
  52.6 1.0 copy-done.4
  53.6 5.9 %attention.3 = (f32[512,1024]{1,0:T(8,128)}, bf16[512,1024]{1,0:T(8,128)(2,1)}, bf16[3,512,1024]{2,1,0:T(8,128)(2,1)}, bf16[512,1024]{1,0:T(8,128)(2,1)}) custom-call(s32[1]{0:T(128)} %bitcast.6.act_ref, s32[2,3]{1,0:T(2,128)} %lengths_ref.7, bf16[512,1024]{1,0:T(8,128)(2,1)} %copy-done.4, f32[1,1024]{1,0:T(1,128)} %gain_ref.11, f32[1,1024]{1,0:T(1,128)} %bias_ref.7, ...), custom_call_target="tpu_custom_call" | custom-call | flops 4294967296 | bytes 41943040 | tf_op jit(solution)/shard_map/attention/pallas_call | solution.py:307
  59.5 1.6 collective-permute-start.3
  61.1 5.8 %feed_both.2 = (f32[512,1024]{1,0:T(8,128)}, bf16[512,1024]{1,0:T(8,128)(2,1)}, bf16[512,4096]{1,0:T(8,128)(2,1)}, bf16[2,512,4096]{2,1,0:T(8,128)(2,1)}, f32[51...) custom-call(s32[1]{0:T(128)} %bitcast.6.act_ref, f32[512,1024]{1,0:T(8,128)} %get-tuple-element.56.mid_ref, ...), custom_call_target="tpu_custom_call" | custom-call | flops 25769803776 | bytes 41943040 | tf_op jit(solution)/shard_map/feed_both/pallas_call | solution.py:307
  67.0 1.3 collective-permute-start.1
  68.3 1.3 collective-permute-start.2
  69.6 1.4 pad_maximum_fusion.refs_4_
  71.0 3.8 exchange_second_feed.1
  74.8 45.3 %collective-permute-done.2.gain_ref = f32[1,1024]{1,0:T(1,128)S(1)} collective-permute-done((f32[1,1024]{1,0:T(1,128)S(1)}, f32[1,1024]{1,0:T(1,128)S(1)}, u32[]{:S(2)}, u32[]{:S(2)}) %collective-permute-start.2) | collective-permute-done | bytes 4128 | tf_op jit(solution)/shard_map/ppermute | solution.py:827
  120.6 0.9 copy-done.12
  121.5 25.8 %attention_back.2 = (bf16[512,1024]{1,0:T(8,128)(2,1)}, bf16[3,512,1024]{2,1,0:T(8,128)(2,1)}, f32[512,1024]{1,0:T(8,128)}, bf16[512,1024]{1,0:T(8,128)(2,1)}, f32[1,1024]{1,0:T(1,128)}, /*index=5*/f32[1,1024]{1,0:T(1,128)}) custom-call(s32[1]{0:T(128)} %bitcast.act_ref, s32[2,3]{1,0:T(2,128)} %lengths_ref.7, f32[512,1024]{1,0:T(8,128)} %copy-done.12, ...), custom_call_target="tpu_custom_call" | custom-call | flops 10737418240 | bytes 41943040 | tf_op jit(solution)/shard_map/attention_back/pallas_call | solution.py:307
  148.0 121.0 %collective-permute-start.8 = (f32[2,1024]{1,0:T(2,128)S(1)}, f32[2,1024]{1,0:T(2,128)S(1)}, u32[]{:S(2)}, u32[]{:S(2)}) collective-permute-start(f32[2,1024]{1,0:T(2,128)S(1)} %pad_maximum_fusion.1), channel_id=1, source_target_pairs={{0,16},{1,17},{2,18},{3,19},{4,20},{5,21},{6,22},{7,23},{8,24},{9,... | collective-permute-start | bytes 24584 | tf_op jit(solution)/shard_map/ppermute | solution.py:824
  269.0 1.4 collective-permute-start.6
  270.4 3.1 collective-permute-start.7
  273.5 39.5 %feed_both.3 = (f32[512,1024]{1,0:T(8,128)}, bf16[512,1024]{1,0:T(8,128)(2,1)}, bf16[512,4096]{1,0:T(8,128)(2,1)}, bf16[2,512,4096]{2,1,0:T(8,128)(2,1)}, f32[51...) custom-call(s32[1]{0:T(128)} %bitcast.act_ref, f32[512,1024]{1,0:T(8,128)} %get-tuple-element.55.mid_ref, ...), custom_call_target="tpu_custom_call" | custom-call | flops 25769803776 | bytes 41943040 | tf_op jit(solution)/shard_map/feed_both/pallas_call | solution.py:307
  313.0 26.1 %attention_back.3 = (bf16[512,1024]{1,0:T(8,128)(2,1)}, bf16[3,512,1024]{2,1,0:T(8,128)(2,1)}, f32[512,1024]{1,0:T(8,128)}, bf16[512,1024]{1,0:T(8,128)(2,1)}, f32[1,1024]{1,0:T(1,128)}, /*index=5*/f32[1,1024]{1,0:T(1,128)}) custom-call(s32[1]{0:T(128)} %bitcast.act_ref, s32[2,3]{1,0:T(2,128)} %lengths_ref.7, f32[512,1024]{1,0:T(8,128)} %get-tuple-element.63.grad_ref, ...), custom_call_target="tpu_custom_call" | custom-call | flops 10737418240 | bytes 41943040 | tf_op jit(solution)/shard_map/attention_back/pallas_call | solution.py:307
  339.1 3.5 select_bitcast_fusion
  343.9 1.0 copy-done.13
  344.8 4.0 exchange_second_attention.1
  348.8 173.2 %exchange_first.1 = (bf16[1024,1024]{1,0:T(8,128)(2,1)}, bf16[256,8192]{1,0:T(8,128)(2,1)}, bf16[256,1024]{1,0:T(8,128)(2,1)}, bf16[256,3072]{1,0:T(8,128)(2,1)}, f32[8,256]{1,0:T(8,128)}) custom-call(bf16[512,4096]{1,0:T(8,128)(2,1)} %get-tuple-element.67.refs_0_, ...), custom_call_target="tpu_custom_call", output_to_operand_aliasing={{0}: (9, {}), {1}: (10, {}), {2}: (11, {}), {3}: (12, {})} | custom-call | flops 17179869184 | bytes 104857600 | tf_op jit(solution)/shard_map/exchange_first/pallas_call | solution.py:775
  523.4 2.3 bitcast_convert_fusion.3
  525.7 3.4 bitcast_convert_fusion.2
  529.1 2.6 bitcast_convert_fusion.1
  531.7 1.1 copy-done.1
  532.8 4.4 bitcast_convert_fusion
  (52 shorter events, 6.9 us)
Async XLA Ops:
  22.0 28.2 %copy-start = (bf16[1,1024,1024]{2,1,0:T(8,128)(2,1)S(1)}, bf16[1,1024,1024]{2,1,0:T(8,128)(2,1)}, u32[]{:S(2)}) copy-start(bf16[1,1024,1024]{2,1,0:T(8,128)(2,1)} %param.15) | copy-start | bytes 6291460
  43.2 77.1 %collective-permute-start.4 = (bf16[1024,3072]{1,0:T(8,128)(2,1)}, bf16[1024,3072]{1,0:T(8,128)(2,1)}, u32[]{:S(2)}, u32[]{:S(2)}) collective-permute-start(bf16[1024,3072]{1,0:T(8,128)(2,1)} %bitcast.2.wq_ref.wk_ref.wv_ref), channel_id=1, source_target_pairs={{16,0},{17,1},{18,2},{19,3},{20,4},{21,5},{22,6},{23,7},{24,8},{25... | collective-permute-start | bytes 18874376 | tf_op jit(solution)/shard_map/ppermute | solution.py:827
  44.5 8.1 %collective-permute-start = (bf16[512,1024]{1,0:T(8,128)(2,1)}, bf16[512,1024]{1,0:T(8,128)(2,1)S(1)}, u32[]{:S(2)}, u32[]{:S(2)}) collective-permute-start(bf16[512,1024]{1,0:T(8,128)(2,1)} %feed.1.x_ref), channel_id=1, source_target_pairs={{0,16},{1,17},{2,18},{3,19},{4,20},{5,21},{6,22},{7,23},{8,24},{9,... | collective-permute-start | bytes 3145736 | tf_op jit(solution)/shard_map/ppermute | solution.py:824
  50.2 69.8 %collective-permute-start.5 = (bf16[1024,1024]{1,0:T(8,128)(2,1)S(1)}, bf16[1024,1024]{1,0:T(8,128)(2,1)}, u32[]{:S(2)}, u32[]{:S(2)}) collective-permute-start(bf16[1024,1024]{1,0:T(8,128)(2,1)S(1)} %bitcast.32), channel_id=1, source_target_pairs={{16,0},{17,1},{18,2},{19,3},{20,4},{21,5},{22,6},{23,7},{24,8},{25... | collective-permute-start | bytes 6291464 | tf_op jit(solution)/shard_map/ppermute | solution.py:827
  52.6 1.0 copy-start.4
  59.5 60.7 %collective-permute-start.3 = (bf16[3,512,1024]{2,1,0:T(8,128)(2,1)}, bf16[3,512,1024]{2,1,0:T(8,128)(2,1)}, u32[]{:S(2)}, u32[]{:S(2)}) collective-permute-start(bf16[3,512,1024]{2,1,0:T(8,128)(2,1)} %get-tuple-element.59), channel_id=1, source_target_pairs={{16,0},{17,1},{18,2},{19,3},{20,4},{21,5},{22,6},{23,7},{24,8},{25... | collective-permute-start | bytes 9437192 | tf_op jit(solution)/shard_map/ppermute | solution.py:827
  61.1 7.1 %copy-start.5 = (f32[1,1024]{1,0:T(1,128)S(1)}, f32[1,1024]{1,0:T(1,128)}, u32[]{:S(2)}) copy-start(f32[1,1024]{1,0:T(1,128)} %gain_ref.11) | copy-start | bytes 12292
  67.0 53.3 %collective-permute-start.1 = (f32[512,1024]{1,0:T(8,128)}, f32[512,1024]{1,0:T(8,128)S(1)}, u32[]{:S(2)}, u32[]{:S(2)}) collective-permute-start(f32[512,1024]{1,0:T(8,128)} %get-tuple-element.57), channel_id=1, source_target_pairs={{16,0},{17,1},{18,2},{19,3},{20,4},{21,5},{22,6},{23,7},{24,8},{25... | collective-permute-start | bytes 6291464 | tf_op jit(solution)/shard_map/ppermute | solution.py:827
  68.3 51.8 %collective-permute-start.2 = (f32[1,1024]{1,0:T(1,128)S(1)}, f32[1,1024]{1,0:T(1,128)S(1)}, u32[]{:S(2)}, u32[]{:S(2)}) collective-permute-start(f32[1,1024]{1,0:T(1,128)S(1)} %copy-done.5), channel_id=1, source_target_pairs={{16,0},{17,1},{18,2},{19,3},{20,4},{21,5},{22,6},{23,7},{24,8},{25... | collective-permute-start | bytes 12296 | tf_op jit(solution)/shard_map/ppermute | solution.py:827
  120.0 0.6 copy-start.14
  120.2 1.3 copy-start.12
  148.0 195.2 %collective-permute-start.8 = (f32[2,1024]{1,0:T(2,128)S(1)}, f32[2,1024]{1,0:T(2,128)S(1)}, u32[]{:S(2)}, u32[]{:S(2)}) collective-permute-start(f32[2,1024]{1,0:T(2,128)S(1)} %pad_maximum_fusion.1), channel_id=1, source_target_pairs={{0,16},{1,17},{2,18},{3,19},{4,20},{5,21},{6,22},{7,23},{8,24},{9,... | collective-permute-start | bytes 24584 | tf_op jit(solution)/shard_map/ppermute | solution.py:824
  269.0 74.8 %collective-permute-start.6 = (bf16[512,1024]{1,0:T(8,128)(2,1)}, bf16[512,1024]{1,0:T(8,128)(2,1)S(1)}, u32[]{:S(2)}, u32[]{:S(2)}) collective-permute-start(bf16[512,1024]{1,0:T(8,128)(2,1)} %get-tuple-element.87), channel_id=1, source_target_pairs={{0,16},{1,17},{2,18},{3,19},{4,20},{5,21},{6,22},{7,23},{8,24},{9,... | collective-permute-start | bytes 3145736 | tf_op jit(solution)/shard_map/ppermute | solution.py:824
  270.4 73.5 %collective-permute-start.7 = (bf16[3,512,1024]{2,1,0:T(8,128)(2,1)}, bf16[3,512,1024]{2,1,0:T(8,128)(2,1)}, u32[]{:S(2)}, u32[]{:S(2)}) collective-permute-start(bf16[3,512,1024]{2,1,0:T(8,128)(2,1)} %get-tuple-element.88), channel_id=1, source_target_pairs={{0,16},{1,17},{2,18},{3,19},{4,20},{5,21},{6,22},{7,23},{8,24},{9,... | collective-permute-start | bytes 9437192 | tf_op jit(solution)/shard_map/ppermute | solution.py:824
  313.0 26.1 %copy-start.3 = (f32[512,1024]{1,0:T(8,128)S(1)}, f32[512,1024]{1,0:T(8,128)}, u32[]{:S(2)}) copy-start(f32[512,1024]{1,0:T(8,128)} %get-tuple-element.66) | copy-start | bytes 6291460
  339.1 3.5 copy-start.8
  339.1 3.5 copy-start.9
  339.1 3.5 copy-start.10
  339.1 3.5 copy-start.11
  343.9 1.0 copy-start.13
  348.8 173.3 %copy-start.6 = (f32[8,256]{1,0:T(8,128)S(1)}, f32[8,256]{1,0:T(8,128)}, u32[]{:S(2)}) copy-start(f32[8,256]{1,0:T(8,128)} %get-tuple-element.91) | copy-start | bytes 24580
  348.8 173.3 %copy-start.7 = (f32[8,256]{1,0:T(8,128)S(1)}, f32[8,256]{1,0:T(8,128)}, u32[]{:S(2)}) copy-start(f32[8,256]{1,0:T(8,128)} %get-tuple-element.96) | copy-start | bytes 24580
  523.4 5.7 %copy-start.2 = (bf16[1024,1024]{1,0:T(8,128)(2,1)S(1)}, bf16[1024,1024]{1,0:T(8,128)(2,1)}, u32[]{:S(2)}) copy-start(bf16[1024,1024]{1,0:T(8,128)(2,1)} %get-tuple-element.100) | copy-start | bytes 6291460
  529.1 3.7 copy-start.1

commit v4 on v3

--- a/solution.py
+++ b/solution.py
@@ -386,14 +386,17 @@
 
 
 def tables(lengths, row_tokens, size):
-    ends = jnp.cumsum(lengths, axis=-1)
-    index = jnp.arange(row_tokens, dtype=jnp.int32)
-    passed = index[:, None] >= ends[..., None, :]
-    before = jnp.sum(jnp.where(passed, lengths[..., None, :], 0), axis=-1)
-    position = (index - before).reshape(-1)
-    frequency = 10000.0 ** (-2.0 * jnp.arange(size // 2, dtype=F32) / size)
-    angles = position.astype(F32)[:, None] * frequency
-    return jnp.tile(jnp.cos(angles), (1, 4)), jnp.tile(jnp.sin(angles), (1, 4))
+    index = jnp.arange(row_tokens, dtype=jnp.int32)[None]
+    end, before = 0, 0
+    for window in range(lengths.shape[1]):
+        length = lengths[:, window:window + 1]
+        end = end + length
+        before = before + jnp.where(index >= end, length, 0)
+    position = (index - before).astype(F32).reshape(-1, 1)
+    half = jnp.arange(2 * size, dtype=jnp.int32) % (size // 2)
+    frequency = 10000.0 ** (-2.0 * half.astype(F32) / size)
+    angles = position * frequency
+    return jnp.cos(angles), jnp.sin(angles)
 
 
 def exchange_kernel(cfg, *refs):
@@ -401,7 +404,7 @@
     arrays = len(seats)
     lefts, rights = refs[:arrays], refs[arrays:2 * arrays]
     vector = refs[2 * arrays]
-    refs = refs[2 * arrays + 1 + (arrays if aliased else 0):]
+    refs = refs[2 * arrays + 1 + (arrays + 1 if aliased else 0):]
     outs, vector_out = refs[:arrays], refs[arrays]
     (vector_land, vector_sum, vector_send, vector_recv, vector_store, left, right, left_sem, right_sem, own, give, landed, mine, chain, rest_send, rest_land, rest_keep, piece,
      land_send, land_recv, chain_send, chain_recv,
@@ -809,53 +812,31 @@
     rows = ends_in[0]
     weight_qkv, weight_out, weight_gu, weight_down = w_qkv[0], w_out[0], w_gate_up[0], w_down[0]
     cosine, sine = tables(lengths, tokens // lengths.shape[0], size)
-    nothing = jnp.zeros((2, features), F32)
+    nothing = jnp.zeros((4, features), F32)
 
     def attend(active, values):
         return attention(active, lengths, values, norm_gain_a, norm_bias_a, weight_qkv, weight_out, cosine, sine)
 
-    def feed_back(active, middle, grad):
-        return feed_both(active, middle, grad, norm_gain_f, norm_bias_f, weight_gu, weight_down)
-
-    def attend_back(grad_middle, values, gain, qkv, weight_qkv, weight_out):
-        return attention_back(first, lengths, grad_middle, values, gain, qkv, weight_qkv, weight_out, cosine, sine)
-
-    def upward(*arrays):
-        return [lax.ppermute(array, "section", [(0, 1)]) for array in arrays]
-
-    def downward(*arrays):
-        return [lax.ppermute(array, "section", [(1, 0)]) for array in arrays]
+    def back(active, middle, low_a, qkv, mixture, values, grad):
+        result, low_f, hidden, grad_gu, grad_middle, gain_f, bias_f = feed_both(
+            active, middle, grad, norm_gain_f, norm_bias_f, weight_gu, weight_down)
+        branch, grad_qkv, grad_in, grad_in_low, gain_a, bias_a = attention_back(
+            active, lengths, grad_middle, values, norm_gain_a, qkv, weight_qkv, weight_out, cosine, sine)
+        pairs = [(low_f, grad_gu), (hidden, grad[None]), (mixture, branch[None]), (low_a, grad_qkv)]
+        return result, grad_in, grad_in_low, pairs, jnp.concatenate([gain_a, bias_a, gain_f, bias_f, nothing], axis=0)
 
     middle_0, low_0, qkv_0, mixture_0 = attend(first, rows)
     passed = feed(first, middle_0, norm_gain_f, norm_bias_f, weight_gu, weight_down)
-    (arrived,) = upward(passed)
-    _, later_qkv, later_out, later_gain = lax.optimization_barrier((passed, weight_qkv, weight_out, norm_gain_a))
-    later_qkv, later_out, later_gain = downward(later_qkv, later_out, later_gain)
+    arrived = lax.ppermute(passed, "section", [(0, 1)])
     middle_1, low_1, qkv_1, mixture_1 = attend(second, arrived)
-    (qkv_there,) = downward(qkv_1)
-    result, low_f, hidden, grad_gu, grad_middle, gain_f, bias_f = feed_back(second, middle_1, rows)
-    (grad_middle,) = downward(grad_middle)
-    feed_sums = exchange(
-        [(hidden, rows[None]), (low_f, grad_gu)], jnp.concatenate([nothing, gain_f, bias_f, nothing, nothing], axis=0),
-        shards, group, 1, 1, features, name="exchange_second_feed")
-    branch, grad_qkv, _, returned, gain_a, bias_a = attend_back(
-        grad_middle, passed, later_gain, qkv_there, later_qkv, later_out)
-    branch, grad_qkv, attention_vectors = upward(branch, grad_qkv, jnp.concatenate([gain_a, bias_a], axis=0))
-    _, low_f, hidden, grad_gu, grad_middle, gain_f, bias_f = feed_back(first, middle_0, returned)
-    branch_0, grad_qkv_0, grad_in, _, gain_a, bias_a = attend_back(
-        grad_middle, rows, norm_gain_a, qkv_0, weight_qkv, weight_out)
-    attention_sums = exchange(
-        [(mixture_1, branch[None]), (low_1, grad_qkv)],
-        jnp.concatenate([attention_vectors, nothing, nothing, nothing], axis=0),
-        shards, group, 1, 2, features, after=feed_sums[-1], name="exchange_second_attention")
-    vectors = feed_sums[-1] + attention_sums[-1]
-    sums = exchange(
-        [(hidden, returned[None]), (low_f, grad_gu), (mixture_0, branch_0[None]), (low_0, grad_qkv_0)],
-        jnp.concatenate([gain_a, bias_a, gain_f, bias_f, nothing, nothing], axis=0),
-        shards, group, 0, 3, features, previous=feed_sums[:-1] + attention_sums[:-1], name="exchange_first")
+    result, _, returned, pairs_1, vectors_1 = back(second, middle_1, low_1, qkv_1, mixture_1, arrived, rows)
+    returned = lax.ppermute(returned, "section", [(1, 0)])
+    sums = exchange(pairs_1, vectors_1, shards, group, 1, 1, features // 2, name="exchange_second")
+    _, grad_in, _, pairs_0, vectors_0 = back(first, middle_0, low_0, qkv_0, mixture_0, rows, returned)
+    sums = exchange(pairs_0, vectors_0, shards, group, 0, 2, features // 2, previous=sums, name="exchange_first")
     ends_out = jnp.where(is_first, grad_in, result)[None]
-    grad_down, grad_gate_up, grad_out, grad_qkv = (item.astype(F32)[None] for item in sums[:4])
-    vectors = jnp.where(is_first, sums[4], vectors)
+    grad_gate_up, grad_down, grad_out, grad_qkv = (item.astype(F32)[None] for item in sums[:4])
+    vectors = sums[4]
     return (
         ends_out,
         vectors[0:1],

time: 547 us -> 471 us (0.86)
  starting transfers between devices: 138 us -> 2.8 us
  Pallas kernels: 323 us -> 373 us
  waiting for transfers between devices: 46.6 us -> 63.1 us
    ppermute x9 -> x2, starting transfers between devices: 138 us -> 2.8 us  [the longest x1 1.52 us: body(): arrived = lax.ppermute(passed, 'section', [(0, 1)])]
    pallas_call x3 -> x2, Pallas kernels: 181 us -> 249 us  [exchange(): pl.pallas_call(functools.partial(exchange_kernel, cfg), out_shape=results...]
    pallas_call x7, Pallas kernels: 142 us -> 124 us  [local_call(): pl.pallas_call(kernel, grid_spec=pltpu.PrefetchScalarGridSpec(num_scalar_...]
    ppermute x9 -> x2, waiting for transfers between devices: 46.6 us -> 63.1 us  [the longest x1 60.9 us: body(): returned = lax.ppermute(returned, 'section', [(1, 0)])]
  transfers between devices with their start and end apart: 9 -> 2, of which waited for: 3 -> 2; matrix products, arithmetic and copies ran while one was open for 1% -> 0% of each run, Pallas kernels for 15% -> 1%
where the time goes in v4:
time: 471 us; the launch traced here: 465 us
  Pallas kernels  373 us (79%)
  waiting for transfers between devices  63.1 us (13%)
  other arithmetic  17.3 us (4%)
  local copies, waits for them, and re-layouts  7.44 us (2%)
    pallas_call x2, Pallas kernels, exchange(): pl.pallas_call(functools.partial(exchange_kernel, cfg), out_shape=results...  249 us
    pallas_call x7, Pallas kernels, local_call(): pl.pallas_call(kernel, grid_spec=pltpu.PrefetchScalarGridSpec(num_scalar_...  124 us
    ppermute x1, waiting for transfers between devices, body(): returned = lax.ppermute(returned, 'section', [(1, 0)])  60.9 us
    broadcast_in_dim x4, other arithmetic, body(): item.astype(F32)[None]  12.7 us
  transfers between devices with their start and end apart: 2, of which 2 were waited for; matrix products, arithmetic and copies ran while one was open for 0% of the time, Pallas kernels for 1%

profile of v4, /device:TPU:0, one launch (start us, length us, event | category | flops | bytes accessed | tf_op | source)
XLA Modules:
  0.0 465.1 jit_solution(11903306969351466915)
XLA Ops:
  0.7 1.0 fusion.7
  1.7 0.1 broadcast_bitcast_fusion.4
  1.8 0.1 broadcast_bitcast_fusion.2
  1.9 0.1 broadcast_bitcast_fusion
  2.0 1.9 multiply_sine_fusion
  3.9 17.5 %attention.2 = (f32[512,1024]{1,0:T(8,128)}, bf16[512,1024]{1,0:T(8,128)(2,1)}, bf16[3,512,1024]{2,1,0:T(8,128)(2,1)}, bf16[512,1024]{1,0:T(8,128)(2,1)}) custom-call(s32[1]{0:T(128)} %bitcast.act_ref, s32[2,3]{1,0:T(2,128)} %lengths_ref.7, bf16[512,1024]{1,0:T(8,128)(2,1)} %bitcast.58, f32[1,1024]{1,0:T(1,128)} %gain_ref.13, f32[1,1024]{1,0:T(1,128)} %bias_ref.7, ...), custom_call_target="tpu_custom_call" | custom-call | flops 4294967296 | bytes 41943040 | tf_op jit(solution)/shard_map/attention/pallas_call | solution.py:307
  21.3 21.0 %feed.1 = bf16[512,1024]{1,0:T(8,128)(2,1)} custom-call(s32[1]{0:T(128)} %bitcast.act_ref, f32[512,1024]{1,0:T(8,128)} %get-tuple-element.50.mid_ref, f32[1,1024]{1,0:T(1,128)} %gain_ref.12, f32[1,1024]{1,0:T(1,128)} %bias_ref.9, bf16[1024,8192]{1,0:T(8,128)(2,1)} %bitcast.67, bf16[1024,8192]{1,0:T(8,128)(2,1)} %bitcast.68, bf16[4096,1024]{1,0:T(8,128)(2,1)} %bitcast.73), custom_call_target="tpu_custom_call" | custom-call | flops 12884901888 | bytes 41943040 | tf_op jit(solution)/shard_map/feed/pallas_call | solution.py:307
  42.3 1.5 collective-permute-start
  43.9 2.2 collective-permute-done.x_ref
  46.1 1.0 copy-done.4
  47.1 6.2 %attention.3 = (f32[512,1024]{1,0:T(8,128)}, bf16[512,1024]{1,0:T(8,128)(2,1)}, bf16[3,512,1024]{2,1,0:T(8,128)(2,1)}, bf16[512,1024]{1,0:T(8,128)(2,1)}) custom-call(s32[1]{0:T(128)} %bitcast.4.act_ref, s32[2,3]{1,0:T(2,128)} %lengths_ref.7, bf16[512,1024]{1,0:T(8,128)(2,1)} %copy-done.4, f32[1,1024]{1,0:T(1,128)} %gain_ref.13, f32[1,1024]{1,0:T(1,128)} %bias_ref.7, ...), custom_call_target="tpu_custom_call" | custom-call | flops 4294967296 | bytes 41943040 | tf_op jit(solution)/shard_map/attention/pallas_call | solution.py:307
  53.3 5.8 %feed_both.2 = (f32[512,1024]{1,0:T(8,128)}, bf16[512,1024]{1,0:T(8,128)(2,1)}, bf16[512,4096]{1,0:T(8,128)(2,1)}, bf16[2,512,4096]{2,1,0:T(8,128)(2,1)}, f32[51...) custom-call(s32[1]{0:T(128)} %bitcast.4.act_ref, f32[512,1024]{1,0:T(8,128)} %get-tuple-element.51.mid_ref, ...), custom_call_target="tpu_custom_call" | custom-call | flops 25769803776 | bytes 41943040 | tf_op jit(solution)/shard_map/feed_both/pallas_call | solution.py:307
  59.1 0.0 copy-start.6
  59.1 7.6 %attention_back.2 = (bf16[512,1024]{1,0:T(8,128)(2,1)}, bf16[3,512,1024]{2,1,0:T(8,128)(2,1)}, f32[512,1024]{1,0:T(8,128)}, bf16[512,1024]{1,0:T(8,128)(2,1)}, f32[1,1024]{1,0:T(1,128)}, /*index=5*/f32[1,1024]{1,0:T(1,128)}) custom-call(s32[1]{0:T(128)} %bitcast.4.act_ref, s32[2,3]{1,0:T(2,128)} %lengths_ref.7, f32[512,1024]{1,0:T(8,128)} %get-tuple-element.52.grad_ref, ...), custom_call_target="tpu_custom_call" | custom-call | flops 10737418240 | bytes 41943040 | tf_op jit(solution)/shard_map/attention_back/pallas_call | solution.py:307
  66.7 1.3 collective-permute-start.1
  68.0 1.3 concatenate.7.refs_8_
  69.3 3.8 exchange_second.1
  73.1 60.9 %collective-permute-done.1.grad_ref = bf16[512,1024]{1,0:T(8,128)(2,1)S(1)} collective-permute-done((bf16[512,1024]{1,0:T(8,128)(2,1)}, bf16[512,1024]{1,0:T(8,128)(2,1)S(1)}, u32[]{:S(2)}, u32[]{:S(2)}) %collective-permute-start.1) | collective-permute-done | bytes 1048608 | tf_op jit(solution)/shard_map/ppermute | solution.py:833
  134.0 1.0 copy-done.9
  135.0 39.7 %feed_both.3 = (f32[512,1024]{1,0:T(8,128)}, bf16[512,1024]{1,0:T(8,128)(2,1)}, bf16[512,4096]{1,0:T(8,128)(2,1)}, bf16[2,512,4096]{2,1,0:T(8,128)(2,1)}, f32[51...) custom-call(s32[1]{0:T(128)} %bitcast.act_ref, f32[512,1024]{1,0:T(8,128)} %get-tuple-element.50.mid_ref, ...), custom_call_target="tpu_custom_call" | custom-call | flops 25769803776 | bytes 41943040 | tf_op jit(solution)/shard_map/feed_both/pallas_call | solution.py:307
  174.7 25.9 %attention_back.3 = (bf16[512,1024]{1,0:T(8,128)(2,1)}, bf16[3,512,1024]{2,1,0:T(8,128)(2,1)}, f32[512,1024]{1,0:T(8,128)}, bf16[512,1024]{1,0:T(8,128)(2,1)}, f32[1,1024]{1,0:T(1,128)}, /*index=5*/f32[1,1024]{1,0:T(1,128)}) custom-call(s32[1]{0:T(128)} %bitcast.act_ref, s32[2,3]{1,0:T(2,128)} %lengths_ref.7, f32[512,1024]{1,0:T(8,128)} %get-tuple-element.55.grad_ref, ...), custom_call_target="tpu_custom_call" | custom-call | flops 10737418240 | bytes 41943040 | tf_op jit(solution)/shard_map/attention_back/pallas_call | solution.py:307
  200.6 0.0 copy-done.8
  200.6 1.3 concatenate.6.refs_8_
  201.9 245.7 %exchange_first.1 = (bf16[256,8192]{1,0:T(8,128)(2,1)}, bf16[1024,1024]{1,0:T(8,128)(2,1)}, bf16[256,1024]{1,0:T(8,128)(2,1)}, bf16[256,3072]{1,0:T(8,128)(2,1)}, f32[8,256]{1,0:T(8,128)}) custom-call(bf16[512,1024]{1,0:T(8,128)(2,1)} %get-tuple-element.59.refs_0_, ...), custom_call_target="tpu_custom_call", output_to_operand_aliasing={{0}: (9, {}), {1}: (10, {}), {2}: (11, {}), {3}: (12, {}), ... | custom-call | flops 17179869184 | bytes 104857600 | tf_op jit(solution)/shard_map/exchange_first/pallas_call | solution.py:778
  447.6 1.4 fusion.8
  449.1 2.3 bitcast_convert_fusion.3
  451.3 3.4 bitcast_convert_fusion.2
  454.8 2.6 bitcast_convert_fusion.1
  457.4 1.1 copy-done
  458.5 4.4 bitcast_convert_fusion
  462.9 0.0 copy-done.1
  462.9 1.7 select_bitcast_fusion
  (24 shorter events, 0.1 us)
Async XLA Ops:
  42.3 3.8 collective-permute-start
  46.1 1.0 copy-start.4
  59.1 8.9 %copy-start.5 = (f32[1,1024]{1,0:T(1,128)S(1)}, f32[1,1024]{1,0:T(1,128)}, u32[]{:S(2)}) copy-start(f32[1,1024]{1,0:T(1,128)} %get-tuple-element.79) | copy-start | bytes 12292
  59.1 8.9 %copy-start.6 = (f32[1,1024]{1,0:T(1,128)S(1)}, f32[1,1024]{1,0:T(1,128)}, u32[]{:S(2)}) copy-start(f32[1,1024]{1,0:T(1,128)} %get-tuple-element.80) | copy-start | bytes 12292
  66.7 67.3 %collective-permute-start.1 = (bf16[512,1024]{1,0:T(8,128)(2,1)}, bf16[512,1024]{1,0:T(8,128)(2,1)S(1)}, u32[]{:S(2)}, u32[]{:S(2)}) collective-permute-start(bf16[512,1024]{1,0:T(8,128)(2,1)} %get-tuple-element.54), channel_id=1, source_target_pairs={{16,0},{17,1},{18,2},{19,3},{20,4},{21,5},{22,6},{23,7},{24,8},{25... | collective-permute-start | bytes 3145736 | tf_op jit(solution)/shard_map/ppermute | solution.py:833
  134.0 1.0 copy-start.9
  174.7 25.9 %copy-start.7 = (f32[1,1024]{1,0:T(1,128)S(1)}, f32[1,1024]{1,0:T(1,128)}, u32[]{:S(2)}) copy-start(f32[1,1024]{1,0:T(1,128)} %get-tuple-element.68) | copy-start | bytes 12292
  174.7 25.9 %copy-start.8 = (f32[1,1024]{1,0:T(1,128)S(1)}, f32[1,1024]{1,0:T(1,128)}, u32[]{:S(2)}) copy-start(f32[1,1024]{1,0:T(1,128)} %get-tuple-element.69) | copy-start | bytes 12292
  449.1 5.7 %copy-start.2 = (bf16[1024,1024]{1,0:T(8,128)(2,1)S(1)}, bf16[1024,1024]{1,0:T(8,128)(2,1)}, u32[]{:S(2)}) copy-start(bf16[1024,1024]{1,0:T(8,128)(2,1)} %get-tuple-element.90) | copy-start | bytes 6291460
  454.8 3.7 copy-start
  458.5 4.4 copy-start.1
  458.5 4.4 copy-start.3

commit v5 on v4

v5 whole, which is shorter than its diff:
```python
import functools

import jax
import jax.numpy as jnp
from jax import lax
from jax.experimental import pallas as pl
from jax.experimental.pallas import tpu as pltpu
from jax.sharding import PartitionSpec as P

MESH = pl.DeviceIdType.MESH
F32, BF16 = jnp.float32, jnp.bfloat16
HEADS = 16
EPSILON = 1e-05


def dot(a, b):
    return jnp.dot(a, b, preferred_element_type=F32)


def dot_cols(a, b):
    return lax.dot_general(a, b, (((1,), (1,)), ((), ())), preferred_element_type=F32)


def dot_rows(a, b):
    return lax.dot_general(a, b, (((0,), (0,)), ((), ())), preferred_element_type=F32)


def in_rows(total, step, run):
    @pl.loop(0, total // step)
    def _(index):
        run(pl.ds(pl.multiple_of(index * step, step), step))


def normalized(values):
    average = jnp.mean(values, axis=-1, keepdims=True)
    centered = values - average
    variance = jnp.mean(centered * centered, axis=-1, keepdims=True)
    spread = lax.rsqrt(variance + EPSILON)
    return centered * spread, spread


def norm_back(grad, values, gain):
    unit, spread = normalized(values)
    scaled = grad * gain
    return spread * (
        scaled
        - jnp.mean(scaled, axis=-1, keepdims=True)
        - unit * jnp.mean(scaled * unit, axis=-1, keepdims=True)
    ), grad * unit


def lanes_of(shape):
    return lax.broadcasted_iota(jnp.int32, shape, len(shape) - 1)


def turn(values, half, size):
    wide = values.shape[-1]
    early = lax.rem(lanes_of(values.shape), size) < half
    return jnp.where(early, pltpu.roll(values, wide - half, 1), pltpu.roll(values, half, 1)), early


def rotated(values, cosine, sine, size):
    other, early = turn(values, size // 2, size)
    return values * cosine + jnp.where(early, -other, other) * sine


def unrotated(values, cosine, sine, size):
    other, early = turn(values * sine, size // 2, size)
    return values * cosine + jnp.where(early, other, -other)


def window_of(index, lengths_ref, row):
    windows = lengths_ref.shape[1]
    end = lengths_ref[row, 0]
    segment = (index >= end).astype(jnp.int32)
    for window in range(1, windows):
        end = end + lengths_ref[row, window]
        segment = segment + (index >= end).astype(jnp.int32)
    return segment


def same_window(lengths_ref, row, tokens):
    queries = window_of(lax.broadcasted_iota(jnp.int32, (tokens, 1), 0), lengths_ref, row)
    keys = window_of(lax.broadcasted_iota(jnp.int32, (1, tokens), 1), lengths_ref, row)
    return queries == keys


def softmax(scores, allowed):
    scores = jnp.where(allowed, scores, -1e30)
    weights = jnp.exp(scores - jnp.max(scores, axis=-1, keepdims=True))
    return weights * (1.0 / jnp.sum(weights, axis=-1, keepdims=True))


def attention_kernel(size, row_tokens, act_ref, lengths_ref, x_ref, gain_ref, bias_ref, gain_f_ref, bias_f_ref,
                     wq_ref, wk_ref, wv_ref, wo_ref, cos_ref, sin_ref, mid_ref, lefts_ref, qkv_ref, mix_ref):
    tokens = x_ref.shape[0]
    part = pl.program_id(0)
    block = wq_ref.shape[1]
    pair = 2 * size

    @pl.when(act_ref[0] == 1)
    def _():
        @pl.when(part == 0)
        def _():
            def begin(rows):
                values = x_ref[rows].astype(F32)
                unit, _ = normalized(values)
                lefts_ref[0, rows] = (unit * gain_ref[...] + bias_ref[...]).astype(BF16)
                mid_ref[rows] = values
            in_rows(tokens, 64, begin)

        for which, weight in enumerate((wq_ref, wk_ref, wv_ref)):
            projected = dot(lefts_ref[0], weight[...])
            for at in range(block // pair):
                lanes = slice(at * pair, (at + 1) * pair)
                values = projected[:, lanes]
                if which < 2:
                    values = rotated(values, cos_ref[...], sin_ref[...], size)
                qkv_ref[which, :, lanes] = values.astype(BF16)

        first = lanes_of((row_tokens, pair)) < size
        for row in range(tokens // row_tokens):
            rows = pl.ds(row * row_tokens, row_tokens)
            allowed = same_window(lengths_ref, row, row_tokens)
            for start in range(0, block // pair, 2):
                work = []
                for at in range(start, start + 2):
                    lanes = pl.ds(at * pair, pair)
                    query, key, value = (qkv_ref[which, rows, lanes] for which in range(3))
                    query = query * (size ** -0.5)
                    for head in range(2):
                        own = jnp.where(first if head == 0 else jnp.logical_not(first), query, jnp.zeros_like(query))
                        work.append((dot_cols(own, key), value))
                work = [(softmax(scores, allowed).astype(BF16), value) for scores, value in work]
                work = [dot(probs, value) for probs, value in work]
                for at in range(2):
                    lanes = pl.ds((start + at) * pair, pair)
                    mix_ref[rows, lanes] = jnp.where(first, work[2 * at], work[2 * at + 1]).astype(BF16)

        mixture = mix_ref[...]
        lefts_ref[1, :, pl.ds(pl.multiple_of(part * block, block), block)] = mixture
        mid_ref[...] += dot(mixture, wo_ref[...])

        @pl.when(part == pl.num_programs(0) - 1)
        def _():
            def close(rows):
                unit, _ = normalized(mid_ref[rows])
                lefts_ref[2, rows] = (unit * gain_f_ref[...] + bias_f_ref[...]).astype(BF16)
            in_rows(tokens, 64, close)


def attention_back_kernel(size, row_tokens, act_ref, lengths_ref, grad_ref, x_ref, gain_ref, qkv_ref, wq_ref, wk_ref,
                          wv_ref, wo_ref, cos_ref, sin_ref, branch_ref, proj_ref, input_ref, input_low_ref,
                          dgain_ref, dbias_ref, gm_ref, total_ref):
    tokens = x_ref.shape[0]
    part = pl.program_id(0)
    block = wq_ref.shape[1]
    pair = 2 * size
    scale = size ** -0.5

    @pl.when(act_ref[0] == 1)
    def _():
        @pl.when(part == 0)
        def _():
            def begin(rows):
                branch_ref[rows] = grad_ref[rows].astype(BF16)
            in_rows(tokens, 64, begin)

        gm_ref[...] = dot_cols(branch_ref[...], wo_ref[...]).astype(BF16)
        first = lanes_of((row_tokens, pair)) < size
        for row in range(tokens // row_tokens):
            rows = pl.ds(row * row_tokens, row_tokens)
            allowed = same_window(lengths_ref, row, row_tokens)
            cosine, sine = cos_ref[rows], sin_ref[rows]
            for start in range(0, block // pair, 2):
                work = []
                for at in range(start, start + 2):
                    lanes = pl.ds(at * pair, pair)
                    query, key, value = (qkv_ref[which, rows, lanes] for which in range(3))
                    grad_mix = gm_ref[rows, lanes]
                    scaled = query * scale
                    for head in range(2):
                        mine = first if head == 0 else jnp.logical_not(first)
                        work.append((
                            query, key, grad_mix,
                            dot_cols(jnp.where(mine, scaled, jnp.zeros_like(scaled)), key),
                            dot_cols(jnp.where(mine, grad_mix, jnp.zeros_like(grad_mix)), value)))
                results = []
                for query, key, grad_mix, scores, grad_probs in work:
                    probs = softmax(scores, allowed)
                    weighted = probs * grad_probs
                    grad_scores = (weighted - probs * jnp.sum(weighted, axis=-1, keepdims=True)).astype(BF16)
                    results.append((query, key, grad_mix, grad_scores, probs.astype(BF16)))
                results = [
                    (dot(grad_scores, key), dot_rows(grad_scores, query), dot_rows(probs, grad_mix))
                    for query, key, grad_mix, grad_scores, probs in results]
                for at in range(2):
                    lanes = pl.ds((start + at) * pair, pair)
                    grad_query, grad_key, grad_value = (
                        jnp.where(first, a, b) for a, b in zip(results[2 * at], results[2 * at + 1]))
                    proj_ref[0, rows, lanes] = unrotated(grad_query * scale, cosine, sine, size).astype(BF16)
                    proj_ref[1, rows, lanes] = unrotated(grad_key * scale, cosine, sine, size).astype(BF16)
                    proj_ref[2, rows, lanes] = grad_value.astype(BF16)

        added = (
            dot_cols(proj_ref[0], wq_ref[...])
            + dot_cols(proj_ref[1], wk_ref[...])
            + dot_cols(proj_ref[2], wv_ref[...])
        )
        total_ref[...] = jnp.where(part == 0, added, total_ref[...] + added)

        @pl.when(part == pl.num_programs(0) - 1)
        def _():
            dgain_ref[...] = jnp.zeros_like(dgain_ref)
            dbias_ref[...] = jnp.zeros_like(dbias_ref)

            def finish(rows):
                grad = total_ref[rows]
                through, by_gain = norm_back(grad, x_ref[rows].astype(F32), gain_ref[...])
                result = grad_ref[rows] + through
                input_ref[rows] = result
                input_low_ref[rows] = result.astype(BF16)
                dgain_ref[...] += jnp.sum(by_gain, axis=0, keepdims=True)
                dbias_ref[...] += jnp.sum(grad, axis=0, keepdims=True)
            in_rows(tokens, 64, finish)


def feed_kernel(unit_rows, act_ref, mid_ref, low_ref, wg_ref, wu_ref, wd_ref, out_ref, half_ref, total_ref):
    part = pl.program_id(0)

    @pl.when(act_ref[0] == 1)
    def _():
        @pl.when(part == 0)
        def _():
            total_ref[...] = mid_ref[...]

        low = low_ref[0]
        gate = dot(low, wg_ref[...])
        up = dot(low, wu_ref[...])
        hidden = (gate / (1.0 + jnp.exp(-gate)) * up).astype(BF16)
        for at in range(half_ref.shape[1] // unit_rows):
            rows = [hidden[:, (2 * at + side) * unit_rows:(2 * at + side + 1) * unit_rows] for side in range(2)]
            half_ref[:, at * unit_rows:(at + 1) * unit_rows] = jnp.where(act_ref[1] == 0, rows[0], rows[1])
        total_ref[...] += dot(hidden, wd_ref[...])

        @pl.when(part == pl.num_programs(0) - 1)
        def _():
            out_ref[...] = total_ref[...].astype(BF16)


def feed_both_kernel(act_ref, mid_ref, low_ref, grad_ref, gain_ref, wg_ref, wu_ref, wd_ref, out_ref,
                     hidden_ref, ggu_ref, grad_mid_ref, dgain_ref, dbias_ref, total_ref):
    tokens = mid_ref.shape[0]
    part = pl.program_id(0)

    @pl.when(act_ref[0] == 1)
    def _():
        @pl.when(part == 0)
        def _():
            out_ref[...] = mid_ref[...]

        low = low_ref[0]
        gate = dot(low, wg_ref[...])
        up = dot(low, wu_ref[...])
        grad_hidden = dot_cols(grad_ref[...], wd_ref[...])
        sig = 1.0 / (1.0 + jnp.exp(-gate))
        silu = gate * sig
        hidden_ref[...] = (silu * up).astype(BF16)
        ggu_ref[0] = (grad_hidden * up * (sig * (1.0 + gate * (1.0 - sig)))).astype(BF16)
        ggu_ref[1] = (grad_hidden * silu).astype(BF16)
        out_ref[...] += dot(hidden_ref[...], wd_ref[...])
        added = dot_cols(ggu_ref[0], wg_ref[...]) + dot_cols(ggu_ref[1], wu_ref[...])
        total_ref[...] = jnp.where(part == 0, added, total_ref[...] + added)

        @pl.when(part == pl.num_programs(0) - 1)
        def _():
            dgain_ref[...] = jnp.zeros_like(dgain_ref)
            dbias_ref[...] = jnp.zeros_like(dbias_ref)

            def finish(rows):
                grad = total_ref[rows]
                through, by_gain = norm_back(grad, mid_ref[rows], gain_ref[...])
                grad_mid_ref[rows] = grad_ref[rows].astype(F32) + through
                dgain_ref[...] += jnp.sum(by_gain, axis=0, keepdims=True)
                dbias_ref[...] += jnp.sum(grad, axis=0, keepdims=True)
            in_rows(tokens, 64, finish)


def whole(shape):
    return pl.BlockSpec(shape, lambda part, *_: (0,) * len(shape))


def column(rows, wide, offset=0):
    return pl.BlockSpec((rows, wide), lambda part, act, *_: (0, (part + offset) * act[0]))


def stacked(count, rows, wide):
    return pl.BlockSpec((count, rows, wide), lambda part, act, *_: (0, 0, part * act[0]))


def lower(rows, wide):
    return pl.BlockSpec((rows, wide), lambda part, act, *_: (part * act[0], 0))


def local_call(kernel, name, grid, scalars, args, in_specs, outs, out_specs, scratch, flops, limit=56):
    return pl.pallas_call(
        kernel,
        grid_spec=pltpu.PrefetchScalarGridSpec(
            num_scalar_prefetch=len(scalars), grid=(grid,), in_specs=in_specs, out_specs=out_specs,
            scratch_shapes=scratch),
        out_shape=outs,
        name=name,
        cost_estimate=pl.CostEstimate(flops=flops, bytes_accessed=40 * 2 ** 20, transcendentals=0),
        compiler_params=pltpu.CompilerParams(
            dimension_semantics=("arbitrary",), vmem_limit_bytes=limit * 1024 * 1024),
    )(*scalars, *args)


def attention(active, lengths, x, gain, bias, gain_f, bias_f, w_qkv, w_out, cosine, sine, parts=2):
    tokens, features = x.shape
    row_tokens = tokens // lengths.shape[0]
    size = features // HEADS
    wide = features // parts
    stack = jax.ShapeDtypeStruct((3, tokens, features), BF16)
    return local_call(
        functools.partial(attention_kernel, size, row_tokens), "attention", parts, (active, lengths),
        (x, gain, bias, gain_f, bias_f, w_qkv, w_qkv, w_qkv, w_out, cosine, sine),
        [whole((tokens, features))] + [whole((1, features))] * 4 + [column(features, wide),
         column(features, wide, parts), column(features, wide, 2 * parts), lower(wide, features),
         whole(cosine.shape), whole(sine.shape)],
        (jax.ShapeDtypeStruct((tokens, features), F32), stack, stack),
        (whole((tokens, features)), whole(stack.shape), stacked(3, tokens, wide)),
        [pltpu.VMEM((tokens, wide), BF16)], 8 * tokens * features ** 2)


def attention_back(active, lengths, grad_mid, x, gain, qkv, w_qkv, w_out, cosine, sine, parts=2):
    tokens, features = x.shape
    row_tokens = tokens // lengths.shape[0]
    size = features // HEADS
    wide = features // parts
    vector = jax.ShapeDtypeStruct((1, features), F32)
    return local_call(
        functools.partial(attention_back_kernel, size, row_tokens), "attention_back", parts, (active, lengths),
        (grad_mid, x, gain, qkv, w_qkv, w_qkv, w_qkv, w_out, cosine, sine),
        [whole((tokens, features)), whole((tokens, features)), whole((1, features)), stacked(3, tokens, wide),
         column(features, wide), column(features, wide, parts), column(features, wide, 2 * parts),
         lower(wide, features), whole(cosine.shape), whole(sine.shape)],
        (jax.ShapeDtypeStruct((tokens, features), BF16), jax.ShapeDtypeStruct((3, tokens, features), BF16),
         jax.ShapeDtypeStruct((tokens, features), F32), jax.ShapeDtypeStruct((tokens, features), BF16),
         vector, vector),
        (whole((tokens, features)), stacked(3, tokens, wide), whole((tokens, features)), whole((tokens, features)),
         whole((1, features)), whole((1, features))),
        [pltpu.VMEM((tokens, wide), BF16), pltpu.VMEM((tokens, features), F32)], 20 * tokens * features ** 2)


def third(tokens, features):
    return pl.BlockSpec((1, tokens, features), lambda part, *_: (2, 0, 0))


def feed(active, mid, lefts, w_gate_up, w_down, unit_rows, parts=8):
    tokens, features = mid.shape
    wide = w_down.shape[0] // parts
    return local_call(
        functools.partial(feed_kernel, unit_rows), "feed", parts, (active,),
        (mid, lefts, w_gate_up, w_gate_up, w_down),
        [whole((tokens, features)), third(tokens, features), column(features, wide), column(features, wide, parts),
         lower(wide, features)],
        (jax.ShapeDtypeStruct((tokens, features), BF16), jax.ShapeDtypeStruct((tokens, w_down.shape[0] // 2), BF16)),
        (whole((tokens, features)), column(tokens, wide // 2)),
        [pltpu.VMEM((tokens, features), F32)], 6 * tokens * features * w_down.shape[0])


def feed_both(active, mid, lefts, grad, gain, w_gate_up, w_down, parts=8):
    tokens, features = mid.shape
    hidden = w_down.shape[0]
    wide = hidden // parts
    vector = jax.ShapeDtypeStruct((1, features), F32)
    return local_call(
        feed_both_kernel, "feed_both", parts, (active,),
        (mid, lefts, grad, gain, w_gate_up, w_gate_up, w_down),
        [whole((tokens, features)), third(tokens, features), whole((tokens, features)), whole((1, features)),
         column(features, wide), column(features, wide, parts), lower(wide, features)],
        (jax.ShapeDtypeStruct((tokens, features), F32), jax.ShapeDtypeStruct((tokens, hidden), BF16),
         jax.ShapeDtypeStruct((2, tokens, hidden), BF16), jax.ShapeDtypeStruct((tokens, features), F32),
         vector, vector),
        (whole((tokens, features)), column(tokens, wide), stacked(2, tokens, wide),
         whole((tokens, features)), whole((1, features)), whole((1, features))),
        [pltpu.VMEM((tokens, features), F32)], 12 * tokens * features * hidden)


def tables(lengths, row_tokens, size):
    index = jnp.arange(row_tokens, dtype=jnp.int32)[None]
    end, before = 0, 0
    for window in range(lengths.shape[1]):
        length = lengths[:, window:window + 1]
        end = end + length
        before = before + jnp.where(index >= end, length, 0)
    position = (index - before).astype(F32).reshape(-1, 1)
    half = jnp.arange(2 * size, dtype=jnp.int32) % (size // 2)
    frequency = 10000.0 ** (-2.0 * half.astype(F32) / size)
    angles = position * frequency
    return jnp.cos(angles), jnp.sin(angles)


def exchange_kernel(cfg, *refs):
    shards, bits, seats, unit_rows, width, section, aliased, late, layers = cfg
    arrays = len(seats)
    refs = list(refs)

    def take(count):
        taken = refs[:count]
        del refs[:count]
        return taken

    lefts, rights = take(arrays), take(arrays)
    left_others, right_others = take(arrays - (1 if late else 0)), take(1)
    lefts = [ref if at is None else ref.at[at] for ref, at in zip(lefts, layers)]
    left_others = [ref if at is None else ref.at[at] for ref, at in zip(left_others, layers)]
    (vector,) = take(1)
    take(arrays + 1 if aliased else 0)
    outs, (vector_out,) = take(arrays), take(1)
    if late:
        left_others = left_others + take(1)
    (vector_land, vector_sum, vector_send, vector_recv, vector_store, left, right, left_sem, right_sem, other_sem,
     right_send, right_recv, late_send, late_recv, mine, side_land, side, side_send, side_recv, chain_a, chain_b,
     chain_send, chain_recv, rest_send, rest_land, rest_keep, rest_ssem, rest_rsem, piece, store_sem, gather_send,
     gather_recv) = refs
    units = sum(seat[0] for seat in seats)
    by_column = units - seats[-1][0]
    others = bits - 1
    final_rows = unit_rows >> others
    tokens = left.shape[1] // 2
    chains = (chain_a, chain_b)
    chain_rows = (final_rows, unit_rows)
    depth = chain_a.shape[1] - 1
    ring = mine.shape[1]
    sec = lax.axis_index("section")
    here = lax.axis_index("shard")
    seat = lax.axis_index("group")
    group = 1 << bits
    peers = shards * group
    me = here * group + seat
    part = vector_out.shape[1]

    def bit_of(index):
        return lax.rem(lax.div(seat, 1 << index), 2)

    def across(index):
        return (sec, here, seat + (1 - 2 * bit_of(index)) * (1 << index))

    above = (sec, jnp.minimum(here + 1, shards - 1), seat)
    below = (sec, jnp.maximum(here - 1, 0), seat)
    half = bit_of(0)

    def remote(source, target, send, recv, device):
        return pltpu.make_async_remote_copy(
            src_ref=source, dst_ref=target, send_sem=send, recv_sem=recv,
            device_id=device, device_id_type=MESH,
        )

    def aligned(start, size):
        return pl.ds(pl.multiple_of(start, size), size)

    def peer(step):
        index = lax.rem(me + step, peers)
        return index, (sec, lax.div(index, group), lax.rem(index, group))

    def vector_copy(index, device):
        return remote(vector.at[:, aligned(device[1] * part, part)], vector_land.at[me], vector_send.at[index],
                      vector_recv.at[me], device)

    def vector_finish():
        vector_sum[...] = vector[:, aligned(here * part, part)]

        @pl.loop(1, peers)
        def _(step):
            index, device = peer(step)
            vector_copy(index, device).wait_send()
            remote(vector_land.at[index], vector_land.at[index], vector_send.at[index], vector_recv.at[index],
                   device).wait_recv()
            vector_sum[...] += vector_land[index]
        copy = pltpu.make_async_copy(vector_sum, vector_out, vector_store)
        copy.start()
        copy.wait()

    def valid(chunk):
        return (chunk >= 0) & (chunk < units)

    def on(condition, run):
        pl.when(condition)(run)

    def by_rows(rows, run, tall=64):
        step = min(rows, tall)

        @pl.loop(0, rows // step)
        def _(index):
            run(aligned(index * step, step))

    def shifted(rows, offset):
        return aligned(rows.start + offset, rows.size)

    pace = min(by_column // seats[-1][0], 2)
    lead = by_column - pace * seats[-1][0]

    def seat_of(chunk):
        behind = jnp.maximum(chunk - lead, 0)
        period = lax.div(behind, pace + 1)
        step = behind - period * (pace + 1)
        last = (chunk >= lead) & (step == 0)
        return last, jnp.where(last, period, jnp.where(chunk < lead, chunk, lead + period * pace + step - 1))

    def each_array(chunk, run):
        last, index = seat_of(chunk)
        start = 0
        for which, (count, blocks, _, _) in enumerate(seats):
            begin = 0 if split_rows(which) else start

            def launch(which=which, begin=begin, blocks=blocks):
                local = index - begin
                row = lax.div(local, blocks)
                run(which, row, local - row * blocks)
            here_it_is = last if split_rows(which) else jnp.logical_not(last) & (index >= start) & (index < start + count)
            on((chunk < units) & here_it_is, launch)
            start += count

    def split_rows(which):
        return which == arrays - 1

    def right_columns(which, block, bit):
        inner = seats[which][2]
        if split_rows(which):
            return 0, aligned(block * (2 * width), 2 * width)
        outer = lax.div(block, inner)
        return outer, aligned((block - outer * inner) * (4 * width) + bit * (2 * width), 2 * width)

    def loads(chunk, run):
        two, four = lax.rem(chunk, 2), lax.rem(chunk, 5)

        def each(which, row, block):
            rows = seats[which][3]
            outer, columns = right_columns(which, block, half)
            run(pltpu.make_async_copy(
                rights[which].at[outer, :, columns], right.at[four, :tokens], right_sem.at[four]))
            if split_rows(which):
                run(pltpu.make_async_copy(
                    right_others[0].at[:, columns], right.at[four, tokens:], other_sem.at[four]))
            for shard in range(shards):
                if split_rows(which):
                    offsets = (shard * rows + (2 * row + half) * unit_rows, shard * (rows // 2) + row * unit_rows)
                else:
                    offsets = (shard * rows + row * unit_rows,) * 2
                for which_side, source in enumerate((lefts[which], left_others[which])):
                    run(pltpu.make_async_copy(
                        source.at[:, aligned(offsets[which_side], unit_rows)],
                        left.at[two, which_side * tokens:(which_side + 1) * tokens,
                                shard * unit_rows:(shard + 1) * unit_rows],
                        left_sem.at[two, which_side, shard]))
        each_array(chunk, each)

    def right_copy(chunk, source):
        four = lax.rem(chunk, 5)
        return remote(source, right.at[four, tokens:], right_send.at[four], right_recv.at[four], across(0))

    def send_right(chunk):
        def each(which, row, block):
            if not split_rows(which):
                outer, columns = right_columns(which, block, 1 - half)
                right_copy(chunk, rights[which].at[outer, :, columns]).start()
        each_array(chunk, each)

    late_rows = seats[-1][3] // (2 * unit_rows)

    def late_copy(row, shard):
        source = aligned(shard * seats[-1][3] + (2 * row + 1 - half) * unit_rows, unit_rows)
        target = aligned(shard * (seats[-1][3] // 2) + row * unit_rows, unit_rows)
        return remote(lefts[-1].at[:, source], left_others[-1].at[:, target], late_send.at[row, shard],
                      late_recv.at[row, shard], across(0))

    def late_turn(turn):
        begin = 0
        for row in range(late_rows):
            need = max(lead + row * seats[-1][1] * (pace + 1) - 1, 0)
            at_once = -(-shards // max(need - begin, 1))
            for index in range(at_once):
                shard = (turn - begin) * at_once + index
                on((turn >= begin) & (shard < shards), lambda row=row, shard=shard: late_copy(row, shard).start())

            def finish(row=row):
                @pl.loop(0, shards)
                def _(shard):
                    late_copy(row, shard).wait_send()
                    late_copy(row, shard).wait_recv()
            on(turn == need, finish)
            begin = need

    def multiply(chunk):
        two, four, slot = lax.rem(chunk, 2), lax.rem(chunk, 5), lax.rem(chunk, ring)
        loads(chunk, lambda copy: copy.wait())

        def arrived():
            copy = right_copy(chunk, right.at[four, tokens:])
            copy.wait_recv()
            copy.wait_send()
        on(jnp.logical_not(seat_of(chunk)[0]), arrived)
        result = lax.dot_general(left[two], right[four], (((0,), (0,)), ((), ())), preferred_element_type=F32)
        for shard in range(shards):
            for path in range(2):
                mine[path, slot, shard] = result[
                    shard * unit_rows:(shard + 1) * unit_rows, path * width:(path + 1) * width].astype(BF16)

    def side_copy(step, chunk):
        slot, four = lax.rem(chunk, ring), lax.rem(chunk, 4)
        rows = unit_rows >> (step + 1)
        away = aligned((1 - bit_of(step + 1)) * rows, rows)
        source = mine.at[0, slot, :, away] if step == 0 else side.at[step - 1, slot, :, away]
        return remote(source, side_land.at[step, four, :, :rows], side_send.at[step, four], side_recv.at[step, four],
                      across(step + 1))

    def side_sum(step, chunk):
        slot, four = lax.rem(chunk, ring), lax.rem(chunk, 4)
        rows = unit_rows >> (step + 1)
        kept = bit_of(step + 1) * rows
        copy = side_copy(step, chunk)
        copy.wait_recv()
        copy.wait_send()

        @pl.loop(0, shards)
        def _(shard):
            def add(part):
                source = mine[0, slot, shard, shifted(part, kept)] if step == 0 else side[
                    step - 1, slot, shard, shifted(part, kept)]
                side[step, slot, shard, part] = (
                    source.astype(F32) + side_land[step, four, shard, part].astype(F32)).astype(BF16)
            by_rows(rows, add)
        if step + 1 < others:
            side_copy(step + 1, chunk).start()

    def base(path, slot, shard, rows):
        return (side[others - 1, slot, shard, rows] if path == 0 else mine[1, slot, shard, rows]).astype(F32)

    def hop(path, way, chunk, shard):
        slot = lax.rem(chunk, depth)
        ref = chains[path].at[way, slot, shard]
        return remote(ref, ref, chain_send.at[path, way, slot, shard], chain_recv.at[path, way, slot, shard],
                      above if way == 0 else below)

    def onward(path, way, chunk):
        slot, from_base = lax.rem(chunk, depth), lax.rem(chunk, ring)
        arrives = here > 0 if way == 0 else here < shards - 1

        @pl.loop(0, shards - 1 - here if way == 0 else here)
        def _(index):
            shard = shards - 1 - index if way == 0 else index
            copy = hop(path, way, chunk, shard)
            on(arrives, lambda: copy.wait_recv())
            source = jnp.where(arrives, slot, depth)

            def add(rows):
                chains[path][way, slot, shard, rows] = (
                    chains[path][way, source, shard, rows].astype(F32) + base(path, from_base, shard, rows)
                ).astype(BF16)
            by_rows(chain_rows[path], add)
            copy.start()

    def sent(path, way, chunk):
        @pl.loop(0, shards - 1 - here if way == 0 else here)
        def _(index):
            hop(path, way, chunk, shards - 1 - index if way == 0 else index).wait_send()

    def last_hop(path, chunk):
        from_base, slot = lax.rem(chunk, ring), lax.rem(chunk, depth)
        on(here > 0, lambda: hop(path, 0, chunk, here).wait_recv())
        on(here < shards - 1, lambda: hop(path, 1, chunk, here).wait_recv())
        from_below = jnp.where(here > 0, slot, depth)
        from_above = jnp.where(here < shards - 1, slot, depth)

        def total(rows, offset):
            rows = shifted(rows, offset)
            return (
                base(path, from_base, here, rows)
                + chains[path][0, from_below, here, rows].astype(F32)
                + chains[path][1, from_above, here, rows].astype(F32)
            )
        if path == 0:
            finish(path, chunk, total)
        else:
            share(0, chunk, total)

    def rest_copy(step, chunk):
        slot, rows = lax.rem(chunk, 4), pl.ds(0, unit_rows >> (step + 1))
        return remote(rest_send.at[step, slot, rows], rest_land.at[step, slot, rows], rest_ssem.at[step, slot],
                      rest_rsem.at[step, slot], across(step + 1))

    def share(step, chunk, total):
        slot, rows = lax.rem(chunk, 4), unit_rows >> (step + 1)
        bit = bit_of(step + 1)

        def give(part):
            rest_send[step, slot, part] = total(part, (1 - bit) * rows).astype(BF16)
        by_rows(rows, give)
        rest_copy(step, chunk).start()

        def keep(part):
            rest_keep[step, slot, part] = total(part, bit * rows)
        by_rows(rows, keep)

    def rest_sum(step, chunk):
        slot = lax.rem(chunk, 4)
        copy = rest_copy(step, chunk)
        copy.wait_recv()
        copy.wait_send()

        def total(part, offset):
            part = shifted(part, offset)
            return rest_keep[step, slot, part] + rest_land[step, slot, part].astype(F32)
        if step + 1 < others:
            share(step + 1, chunk, total)
        else:
            finish(1, chunk, total)

    def finish(path, chunk, total):
        def put(part):
            piece[path, lax.rem(chunk, 4), part] = total(part, 0).astype(BF16)
        by_rows(final_rows, put)
        spread(path, 0, chunk)

    def place(which, row, block, path, bit, offset, rows):
        if split_rows(which):
            row0, column = (2 * row + bit) * unit_rows, block * (2 * width) + path * width
        else:
            row0, column = row * unit_rows, block * (4 * width) + bit * (2 * width) + path * width
        return outs[which].at[aligned(row0 + offset, rows), aligned(column, width)]

    def seat_row(steps):
        row = 0
        for step in range(steps):
            row = row + bit_of(step + 1) * (unit_rows >> (step + 1))
        return row

    def store(path, chunk, target):
        slot = lax.rem(chunk, 4)
        return pltpu.make_async_copy(piece.at[path, slot], target, store_sem.at[path, slot])

    def gather(path, step, other, chunk, target):
        slot = lax.rem(chunk, 4)
        source = piece.at[path, slot] if step == 0 else target
        return remote(source, target, gather_send.at[path, step, other, slot], gather_recv.at[path, step, other, slot],
                      across(0 if step == 0 else bits - step))

    def spread(path, step, chunk):
        steps = others - max(step - 1, 0)
        rows = unit_rows >> steps

        def each(which, row, block):
            for other in range(1 if step == 0 else 2):
                bit = half if other == 0 else 1 - half
                target = place(which, row, block, path, bit, seat_row(steps), rows)
                if step == 0:
                    store(path, chunk, target).start()
                gather(path, step, other, chunk, target).start()
        each_array(chunk, each)

    def gathered(path, step, chunk):
        rows = unit_rows >> (others - max(step - 1, 0))
        target = outs[0].at[pl.ds(0, rows), pl.ds(0, width)]
        for other in range(1 if step == 0 else 2):
            copy = gather(path, step, other, chunk, target)
            copy.wait_recv()
            copy.wait_send()
        if step == 0:
            store(path, chunk, target).wait()
        if step + 1 < bits:
            spread(path, step + 1, chunk)

    def work():
        barrier = pltpu.get_barrier_semaphore()

        @pl.loop(1, peers)
        def _(step):
            pl.semaphore_signal(barrier, inc=1, device_id=peer(step)[1], device_id_type=MESH)
        pl.semaphore_wait(barrier, peers - 1)
        send_right(0)
        loads(0, lambda copy: copy.start())

        @pl.loop(1, peers)
        def _(step):
            vector_copy(*peer(step)).start()

        for path in range(2):
            for way in range(2):
                @pl.loop(0, shards)
                def _(shard):
                    def clear(rows):
                        chains[path][way, depth, shard, rows] = jnp.zeros((rows.size, width), BF16)
                    by_rows(chain_rows[path], clear)

        line = shards - 1

        @pl.loop(0, units + line + others + bits + 2)
        def _(turn):
            on(turn + 1 < units, lambda: send_right(turn + 1))
            if late:
                late_turn(turn)
            on(turn + 1 < units, lambda: loads(turn + 1, lambda copy: copy.start()))

            def opening():
                multiply(turn)
                side_copy(0, turn).start()
            on(turn < units, opening)
            for step in range(others):
                on(valid(turn - 1 - step), lambda step=step: side_sum(step, turn - 1 - step))
            for path in range(2):
                for way in range(2):
                    chunk = turn - (others if path == 0 else 0) - (here if way == 0 else line - here)
                    on(valid(chunk - 2), lambda path=path, way=way, chunk=chunk: sent(path, way, chunk - 2))
                    on(valid(chunk), lambda path=path, way=way, chunk=chunk: onward(path, way, chunk))
            on(valid(turn - line), lambda: last_hop(1, turn - line))
            on(valid(turn - line - others), lambda: last_hop(0, turn - line - others))
            for step in range(others):
                on(valid(turn - line - 1 - step), lambda step=step: rest_sum(step, turn - line - 1 - step))
            for step in range(bits):
                for path in range(2):
                    chunk = turn - line - others - 1 - step
                    on(valid(chunk), lambda path=path, step=step, chunk=chunk: gathered(path, step, chunk))

        vector_finish()

    if section is None:
        work()
    else:
        pl.when(sec == section)(work)


def exchange(pairs, vector, shards, group, section, collective_id, unit_width, previous=None, unit_rows_max=256,
             name="exchange"):
    bits = group.bit_length() - 1
    arrays = len(pairs)
    lefts, rights = [pair[0][0] for pair in pairs], [pair[1] for pair in pairs]
    layers = tuple(pair[0][1] for pair in pairs)
    left_others = [pair[2] for pair in pairs]
    late = left_others[-1] is None
    if late:
        left_others = left_others[:-1]
    tokens = lefts[0].shape[-2]
    rows_of = [left.shape[-1] // shards for left in lefts]
    unit_rows = min([unit_rows_max] + rows_of[:-1])
    width = unit_width // 4
    seats = []
    for index, (rows, right) in enumerate(zip(rows_of, rights)):
        tall, wide = (2 * unit_rows, 2 * width) if index == arrays - 1 else (unit_rows, 4 * width)
        inner = right.shape[2] // wide
        seats.append((rows // tall * right.shape[0] * inner, right.shape[0] * inner, inner, rows))
    units = sum(seat[0] for seat in seats)
    others = bits - 1
    final_rows = unit_rows >> others
    depth, ring = shards + 3, shards + 2
    late_rows = rows_of[-1] // (2 * unit_rows)
    peers, lanes = shards * group, vector.shape[1] // shards
    dma = pltpu.SemaphoreType.DMA
    scratch = [
        pltpu.VMEM((peers, vector.shape[0], lanes), F32),
        pltpu.VMEM((vector.shape[0], lanes), F32),
        dma((peers,)), dma((peers,)), dma,
        pltpu.VMEM((2, 2 * tokens, shards * unit_rows), BF16),
        pltpu.VMEM((5, 2 * tokens, 2 * width), BF16),
        dma((2, 2, shards)), dma((5,)), dma((5,)),
        dma((5,)), dma((5,)),
        dma((late_rows, shards)), dma((late_rows, shards)),
        pltpu.VMEM((2, ring, shards, unit_rows, width), BF16),
        pltpu.VMEM((others, 4, shards, unit_rows // 2, width), BF16),
        pltpu.VMEM((others, ring, shards, unit_rows // 2, width), BF16),
        dma((others, 4)), dma((others, 4)),
        pltpu.VMEM((2, depth + 1, shards, final_rows, width), BF16),
        pltpu.VMEM((2, depth + 1, shards, unit_rows, width), BF16),
        dma((2, 2, depth, shards)), dma((2, 2, depth, shards)),
        pltpu.VMEM((others, 4, unit_rows // 2, width), BF16),
        pltpu.VMEM((others, 4, unit_rows // 2, width), BF16),
        pltpu.VMEM((others, 4, unit_rows // 2, width), F32),
        dma((others, 4)), dma((others, 4)),
        pltpu.VMEM((2, 4, final_rows, width), BF16),
        dma((2, 4)),
        dma((2, bits, 2, 4)), dma((2, bits, 2, 4)),
    ]
    cfg = (shards, bits, tuple(seats), unit_rows, width, section, previous is not None, late, layers)
    operands = lefts + rights + left_others + [pairs[-1][3], vector] + list(previous or [])
    first = len(operands) - len(previous or [])
    results = [jax.ShapeDtypeStruct((r, g.shape[0] * g.shape[2]), BF16) for r, g in zip(rows_of, rights)]
    results.append(jax.ShapeDtypeStruct((vector.shape[0], lanes), F32))
    if late:
        results.append(jax.ShapeDtypeStruct((tokens, lefts[-1].shape[-1] // 2), BF16))
    hbm, vmem = pl.BlockSpec(memory_space=pl.ANY), pl.BlockSpec(memory_space=pltpu.VMEM)
    in_specs = [vmem if index == first - 1 else hbm for index in range(len(operands))]
    return pl.pallas_call(
        functools.partial(exchange_kernel, cfg),
        out_shape=results,
        in_specs=in_specs,
        out_specs=[hbm] * len(results),
        scratch_shapes=scratch,
        input_output_aliases={first + index: index for index in range(len(previous or []))},
        name=name,
        cost_estimate=pl.CostEstimate(
            flops=4 * tokens * units * shards * unit_rows * 2 * width, bytes_accessed=100 * 2 ** 20,
            transcendentals=0),
        compiler_params=pltpu.CompilerParams(
            collective_id=collective_id, has_side_effects=True, vmem_limit_bytes=56 * 1024 * 1024),
    )(*operands)[:arrays + 1]


UNIT_WIDTH = 512


def body(
    ends_in,
    lengths,
    norm_gain_a,
    norm_bias_a,
    w_qkv,
    w_out,
    norm_gain_f,
    norm_bias_f,
    w_gate_up,
    w_down,
):
    section = lax.axis_index("section")
    shards, group = lax.axis_size("shard"), lax.axis_size("group")
    is_first = section == 0
    first, second = ((section == which).astype(jnp.int32).reshape(1) for which in range(2))
    tokens, features = ends_in.shape[1:]
    size = features // HEADS
    rows = ends_in[0]
    weight_qkv, weight_out, weight_gu, weight_down = w_qkv[0], w_out[0], w_gate_up[0], w_down[0]
    cosine, sine = tables(lengths, tokens // lengths.shape[0], size)
    nothing = jnp.zeros((4, features), F32)
    unit_rows = min(256, features // shards)
    partner_bit = (1 - lax.axis_index("group") % 2).astype(jnp.int32).reshape(1)

    def beside(which, array):
        pairs = [(which * group + index, which * group + (index ^ 1)) for index in range(group)]
        return lax.ppermute(array, ("section", "group"), pairs)

    def attend(active, values):
        return attention(active, lengths, values, norm_gain_a, norm_bias_a, norm_gain_f, norm_bias_f, weight_qkv,
                         weight_out, cosine, sine)

    def back(active, middle, lefts, qkv, values, grad):
        result, hidden, grad_gu, grad_middle, gain_f, bias_f = feed_both(
            active, middle, lefts, grad, norm_gain_f, weight_gu, weight_down)
        branch, grad_qkv, grad_in, grad_in_low, gain_a, bias_a = attention_back(
            active, lengths, grad_middle, values, norm_gain_a, qkv, weight_qkv, weight_out, cosine, sine)
        vectors = jnp.concatenate([gain_a, bias_a, gain_f, bias_f, nothing], axis=0)
        return result, grad_in, grad_in_low, hidden, (grad_gu, branch[None], grad_qkv, grad[None]), vectors

    def sum_all(which, lefts, lefts_beside, hidden, hidden_beside, rights, right_beside, vectors, **more):
        pairs = [((lefts, at), right, lefts_beside) for at, right in zip((2, 1, 0), rights)]
        pairs.append(((hidden, None), rights[3], hidden_beside, right_beside))
        return exchange(pairs, vectors, shards, group, which, which + 1, UNIT_WIDTH * features // 1024, **more)

    rows_beside = beside(1, rows)
    middle_0, lefts_0, qkv_0 = attend(first, rows)
    passed, hidden_half_0 = feed(
        jnp.concatenate([first, partner_bit]), middle_0, lefts_0, weight_gu, weight_down, unit_rows)
    arrived = lax.ppermute(passed, "section", [(0, 1)])
    lefts_beside_0, hidden_beside_0 = beside(0, lefts_0), beside(0, hidden_half_0)
    middle_1, lefts_1, qkv_1 = attend(second, arrived)
    lefts_beside_1 = beside(1, lefts_1)
    result, _, returned, hidden_1, rights_1, vectors_1 = back(second, middle_1, lefts_1, qkv_1, arrived, rows)
    returned = lax.ppermute(returned, "section", [(1, 0)])
    sums = sum_all(1, lefts_1, lefts_beside_1, hidden_1, None, rights_1, rows_beside, vectors_1,
                   name="exchange_second")
    returned, _, lefts_beside_0, hidden_beside_0 = lax.optimization_barrier(
        (returned, sums[4], lefts_beside_0, hidden_beside_0))
    returned_beside = beside(0, returned)
    _, grad_in, _, hidden_0, rights_0, vectors_0 = back(first, middle_0, lefts_0, qkv_0, rows, returned)
    sums = sum_all(0, lefts_0, lefts_beside_0, hidden_0, hidden_beside_0, rights_0, returned_beside, vectors_0,
                   previous=sums, name="exchange_first")
    ends_out = jnp.where(is_first, grad_in, result)[None]
    grad_gate_up, grad_out, grad_qkv, grad_down = (item.astype(F32)[None] for item in sums[:4])
    vectors = sums[4]
    return (
        ends_out,
        vectors[0:1],
        vectors[1:2],
        grad_qkv,
        grad_out,
        vectors[2:3],
        vectors[3:4],
        grad_gate_up,
        grad_down,
    )


def solution(mesh):
    placed = (
        P("section", ("shard", "group"), None),
        P(("shard", "group"), None),
        P("section", None),
        P("section", None),
        P("section", None, None),
        P("section", None, None),
        P("section", None),
        P("section", None),
        P("section", None, None),
        P("section", None, None),
    )
    return jax.shard_map(
        body,
        mesh=mesh,
        in_specs=placed,
        out_specs=(
            P("section", ("shard", "group"), None),
            P("section", "shard"),
            P("section", "shard"),
            P("section", "shard", None),
            P("section", "shard", None),
            P("section", "shard"),
            P("section", "shard"),
            P("section", "shard", None),
            P("section", "shard", None),
        ),
        check_vma=False,
    )
```

time: 471 us -> 450 us (0.955)
  waiting for transfers between devices: 63.1 us -> 46.5 us
  Pallas kernels: 373 us -> 359 us
  starting transfers between devices: 2.8 us -> 16.6 us
    ppermute x1, waiting for transfers between devices: 60.9 us -> 44.5 us  [body(): returned = lax.ppermute(returned, 'section', [(1, 0)])]
    ppermute x0 -> x5, starting transfers between devices: none -> 13.9 us  [beside(): return lax.ppermute(array, ('section', 'group'), pairs)]
    pallas_call x2, Pallas kernels: 249 us -> 236 us  [exchange(): pl.pallas_call(functools.partial(exchange_kernel, cfg), out_shape=results...]
  transfers between devices with their start and end apart: 2 -> 7, of which waited for: 2 -> 2; matrix products, arithmetic and copies ran while one was open for 0% -> 1% of each run, Pallas kernels for 1% -> 14%
where the time goes in v5:
time: 450 us; the launch traced here: 448 us
  Pallas kernels  359 us (80%)
  waiting for transfers between devices  46.5 us (10%)
  other arithmetic  18.5 us (4%)
  starting transfers between devices  16.6 us (4%)
  local copies, waits for them, and re-layouts  6.3 us (1%)
    pallas_call x2, Pallas kernels, exchange(): pl.pallas_call(functools.partial(exchange_kernel, cfg), out_shape=results...  236 us
    pallas_call x7, Pallas kernels, local_call(): pl.pallas_call(kernel, grid_spec=pltpu.PrefetchScalarGridSpec(num_scalar_...  124 us
    ppermute x1, waiting for transfers between devices, body(): returned = lax.ppermute(returned, 'section', [(1, 0)])  44.5 us
    ppermute x5, starting transfers between devices, beside(): return lax.ppermute(array, ('section', 'group'), pairs)  13.9 us
    broadcast_in_dim x4, other arithmetic, body(): item.astype(F32)[None]  11.5 us
  transfers between devices with their start and end apart: 7, of which 2 were waited for; matrix products, arithmetic and copies ran while one was open for 1% of the time, Pallas kernels for 14%

profile of v5, /device:TPU:0, one launch (start us, length us, event | category | flops | bytes accessed | tf_op | source)
XLA Modules:
  0.0 448.4 jit_solution(6802706509161800097)
XLA Ops:
  0.7 1.0 fusion.7
  1.7 0.1 broadcast_bitcast_fusion.4
  2.0 1.8 multiply_sine_fusion
  3.8 0.6 pad_add_fusion.act_ref
  4.4 19.9 %attention.2 = (f32[512,1024]{1,0:T(8,128)}, bf16[3,512,1024]{2,1,0:T(8,128)(2,1)}, bf16[3,512,1024]{2,1,0:T(8,128)(2,1)}) custom-call(s32[1]{0:T(128)} %bitcast.act_ref, s32[2,3]{1,0:T(2,128)} %lengths_ref.7, bf16[512,1024]{1,0:T(8,128)(2,1)} %bitcast.59, f32[1,1024]{1,0:T(1,128)} %gain_ref.11, f32[1,1024]{1,0:T(1,128)} %bias_ref.3, f32[1,1024]{1,0:T(1,128)} %gain_ref.10, ...), custom_call_target="tpu_custom_call" | custom-call | flops 4294967296 | bytes 41943040 | tf_op jit(solution)/shard_map/attention/pallas_call | solution.py:306
  24.3 20.7 %feed.1 = (bf16[512,1024]{1,0:T(8,128)(2,1)}, bf16[512,2048]{1,0:T(8,128)(2,1)}) custom-call(s32[2]{0:T(128)} %pad_add_fusion.act_ref, f32[512,1024]{1,0:T(8,128)} %get-tuple-element.51.mid_ref, bf16[3,512,1024]{2,1,0:T(8,128)(2,1)} %get-tuple-element.52.low_ref.refs_0_.refs_1_.refs_2_, bf16[1024,8192]{1,0:T(8,128)(2,1)} %bitcast.69, ...), custom_call_target="tpu_custom_call" | custom-call | flops 12884901888 | bytes 41943040 | tf_op jit(solution)/shard_map/feed/pallas_call | solution.py:306
  45.0 1.3 collective-permute-start
  46.4 0.7 collective-permute-start.3
  47.1 4.8 %collective-permute-start.4 = (bf16[3,512,1024]{2,1,0:T(8,128)(2,1)}, bf16[3,512,1024]{2,1,0:T(8,128)(2,1)}, u32[]{:S(2)}, u32[]{:S(2)}) collective-permute-start(bf16[3,512,1024]{2,1,0:T(8,128)(2,1)} %get-tuple-element.52.low_ref.refs_0_.refs_1_.refs_2_), channel_id=1, source_target_pairs={{0,1},{1,0},{2,3},{3,2},{4,5},{5,4},{6,7},{7,6},{8,9},{9,8},{10,11... | collective-permute-start | bytes 9437192 | tf_op jit(solution)/shard_map/ppermute | solution.py:939
  52.0 2.2 collective-permute-start.5
  54.2 1.0 copy-done.4
  55.1 6.7 %attention.3 = (f32[512,1024]{1,0:T(8,128)}, bf16[3,512,1024]{2,1,0:T(8,128)(2,1)}, bf16[3,512,1024]{2,1,0:T(8,128)(2,1)}) custom-call(s32[1]{0:T(128)} %bitcast.4.act_ref, s32[2,3]{1,0:T(2,128)} %lengths_ref.7, bf16[512,1024]{1,0:T(8,128)(2,1)} %copy-done.4, f32[1,1024]{1,0:T(1,128)} %gain_ref.11, f32[1,1024]{1,0:T(1,128)} %bias_ref.3, ...), custom_call_target="tpu_custom_call" | custom-call | flops 4294967296 | bytes 41943040 | tf_op jit(solution)/shard_map/attention/pallas_call | solution.py:306
  61.9 2.3 collective-permute-start.2
  64.1 5.7 %feed_both.2 = (f32[512,1024]{1,0:T(8,128)}, bf16[512,4096]{1,0:T(8,128)(2,1)}, bf16[2,512,4096]{2,1,0:T(8,128)(2,1)}, f32[512,1024]{1,0:T(8,128)}, f32[1,1024]{1,0:T(1,128)}, /*index=5*/f32[1,1024]{1,0:T(1,128)}) custom-call(s32[1]{0:T(128)} %bitcast.4.act_ref, f32[512,1024]{1,0:T(8,128)} %get-tuple-element.54.mid_ref, ...), custom_call_target="tpu_custom_call" | custom-call | flops 25769803776 | bytes 41943040 | tf_op jit(solution)/shard_map/feed_both/pallas_call | solution.py:306
  69.8 7.3 %attention_back.2 = (bf16[512,1024]{1,0:T(8,128)(2,1)}, bf16[3,512,1024]{2,1,0:T(8,128)(2,1)}, f32[512,1024]{1,0:T(8,128)}, bf16[512,1024]{1,0:T(8,128)(2,1)}, f32[1,1024]{1,0:T(1,128)}, /*index=5*/f32[1,1024]{1,0:T(1,128)}) custom-call(s32[1]{0:T(128)} %bitcast.4.act_ref, s32[2,3]{1,0:T(2,128)} %lengths_ref.7, f32[512,1024]{1,0:T(8,128)} %get-tuple-element.56.grad_ref, ...), custom_call_target="tpu_custom_call" | custom-call | flops 10737418240 | bytes 41943040 | tf_op jit(solution)/shard_map/attention_back/pallas_call | solution.py:306
  77.1 1.3 collective-permute-start.1
  78.4 1.3 concatenate.10.refs_12_
  79.7 1.0 copy-done.11
  80.7 16.5 %exchange_second.1 = (bf16[256,8192]{1,0:T(8,128)(2,1)}, bf16[256,1024]{1,0:T(8,128)(2,1)}, bf16[256,3072]{1,0:T(8,128)(2,1)}, bf16[1024,1024]{1,0:T(8,128)(2,1)...) custom-call(bf16[3,512,1024]{2,1,0:T(8,128)(2,1)} %get-tuple-element.55.low_ref.refs_0_.refs_1_.refs_2_, ...), custom_call_target="tpu_custom_call" | custom-call | flops 17179869184 | bytes 104857600 | tf_op jit(solution)/shard_map/exchange_second/pallas_call | solution.py:893
  97.2 44.5 %collective-permute-done.1.grad_ref = bf16[512,1024]{1,0:T(8,128)(2,1)S(1)} collective-permute-done((bf16[512,1024]{1,0:T(8,128)(2,1)}, bf16[512,1024]{1,0:T(8,128)(2,1)S(1)}, u32[]{:S(2)}, u32[]{:S(2)}) %collective-permute-start.1) | collective-permute-done | bytes 1048608 | tf_op jit(solution)/shard_map/ppermute | solution.py:967
  141.7 2.0 collective-permute-done.5.refs_11_
  143.7 37.6 %feed_both.3 = (f32[512,1024]{1,0:T(8,128)}, bf16[512,4096]{1,0:T(8,128)(2,1)}, bf16[2,512,4096]{2,1,0:T(8,128)(2,1)}, f32[512,1024]{1,0:T(8,128)}, f32[1,1024]{1,0:T(1,128)}, /*index=5*/f32[1,1024]{1,0:T(1,128)}) custom-call(s32[1]{0:T(128)} %bitcast.act_ref, f32[512,1024]{1,0:T(8,128)} %get-tuple-element.51.mid_ref, ...), custom_call_target="tpu_custom_call" | custom-call | flops 25769803776 | bytes 41943040 | tf_op jit(solution)/shard_map/feed_both/pallas_call | solution.py:306
  181.3 3.9 collective-permute-start.6
  185.3 26.0 %attention_back.3 = (bf16[512,1024]{1,0:T(8,128)(2,1)}, bf16[3,512,1024]{2,1,0:T(8,128)(2,1)}, f32[512,1024]{1,0:T(8,128)}, bf16[512,1024]{1,0:T(8,128)(2,1)}, f32[1,1024]{1,0:T(1,128)}, /*index=5*/f32[1,1024]{1,0:T(1,128)}) custom-call(s32[1]{0:T(128)} %bitcast.act_ref, s32[2,3]{1,0:T(2,128)} %lengths_ref.7, f32[512,1024]{1,0:T(8,128)} %get-tuple-element.70.grad_ref, ...), custom_call_target="tpu_custom_call" | custom-call | flops 10737418240 | bytes 41943040 | tf_op jit(solution)/shard_map/attention_back/pallas_call | solution.py:306
  211.3 1.3 concatenate.11.refs_13_
  212.6 3.5 select_bitcast_fusion
  216.1 219.1 %exchange_first.1 = (bf16[256,8192]{1,0:T(8,128)(2,1)}, bf16[256,1024]{1,0:T(8,128)(2,1)}, bf16[256,3072]{1,0:T(8,128)(2,1)}, bf16[1024,1024]{1,0:T(8,128)(2,1)}, f32[8,256]{1,0:T(8,128)}) custom-call(bf16[3,512,1024]{2,1,0:T(8,128)(2,1)} %get-tuple-element.52.low_ref.refs_0_.refs_1_.r, ...), custom_call_target="tpu_custom_call", output_to_operand_aliasing={{0}: (14, {}), {1}: (15, {}), {2}: (16, {}), {3}: (17, {}),... | custom-call | flops 17179869184 | bytes 104857600 | tf_op jit(solution)/shard_map/exchange_first/pallas_call | solution.py:893
  435.2 1.4 fusion.8
  436.6 3.6 bitcast_convert_fusion.2
  440.2 1.1 bitcast_convert_fusion.3
  441.3 4.4 bitcast_convert_fusion
  445.7 2.5 bitcast_convert_fusion.1
  (39 shorter events, 0.2 us)
Async XLA Ops:
  24.3 22.0 %copy-start.3 = (bf16[1,512,1024]{2,1,0:T(8,128)(2,1)S(1)}, bf16[1,512,1024]{2,1,0:T(8,128)(2,1)}, u32[]{:S(2)}) copy-start(bf16[1,512,1024]{2,1,0:T(8,128)(2,1)} %refs_7_.1) | copy-start | bytes 3145732
  45.0 9.1 %collective-permute-start = (bf16[512,1024]{1,0:T(8,128)(2,1)}, bf16[512,1024]{1,0:T(8,128)(2,1)S(1)}, u32[]{:S(2)}, u32[]{:S(2)}) collective-permute-start(bf16[512,1024]{1,0:T(8,128)(2,1)} %get-tuple-element.53), channel_id=1, source_target_pairs={{0,16},{1,17},{2,18},{3,19},{4,20},{5,21},{6,22},{7,23},{8,24},{9,... | collective-permute-start | bytes 3145736 | tf_op jit(solution)/shard_map/ppermute | solution.py:962
  46.4 33.3 %collective-permute-start.3 = (bf16[512,1024]{1,0:T(8,128)(2,1)S(1)}, bf16[512,1024]{1,0:T(8,128)(2,1)S(1)}, u32[]{:S(2)}, u32[]{:S(2)}) collective-permute-start(bf16[512,1024]{1,0:T(8,128)(2,1)S(1)} %bitcast.62), channel_id=1, source_target_pairs={{16,17},{17,16},{18,19},{19,18},{20,21},{21,20},{22,23},{23,22},{2... | collective-permute-start | bytes 3145736 | tf_op jit(solution)/shard_map/ppermute | solution.py:939
  47.1 96.6 %collective-permute-start.4 = (bf16[3,512,1024]{2,1,0:T(8,128)(2,1)}, bf16[3,512,1024]{2,1,0:T(8,128)(2,1)}, u32[]{:S(2)}, u32[]{:S(2)}) collective-permute-start(bf16[3,512,1024]{2,1,0:T(8,128)(2,1)} %get-tuple-element.52.low_ref.refs_0_.refs_1_.refs_2_), channel_id=1, source_target_pairs={{0,1},{1,0},{2,3},{3,2},{4,5},{5,4},{6,7},{7,6},{8,9},{9,8},{10,11... | collective-permute-start | bytes 9437192 | tf_op jit(solution)/shard_map/ppermute | solution.py:939
  52.0 91.7 %collective-permute-start.5 = (bf16[512,2048]{1,0:T(8,128)(2,1)}, bf16[512,2048]{1,0:T(8,128)(2,1)}, u32[]{:S(2)}, u32[]{:S(2)}) collective-permute-start(bf16[512,2048]{1,0:T(8,128)(2,1)} %get-tuple-element.68), channel_id=1, source_target_pairs={{0,1},{1,0},{2,3},{3,2},{4,5},{5,4},{6,7},{7,6},{8,9},{9,8},{10,11... | collective-permute-start | bytes 6291464 | tf_op jit(solution)/shard_map/ppermute | solution.py:939
  54.2 1.0 copy-start.4
  61.9 17.9 %collective-permute-start.2 = (bf16[3,512,1024]{2,1,0:T(8,128)(2,1)}, bf16[3,512,1024]{2,1,0:T(8,128)(2,1)}, u32[]{:S(2)}, u32[]{:S(2)}) collective-permute-start(bf16[3,512,1024]{2,1,0:T(8,128)(2,1)} %get-tuple-element.55.low_ref.refs_0_.refs_1_.refs_2_), channel_id=1, source_target_pairs={{16,17},{17,16},{18,19},{19,18},{20,21},{21,20},{22,23},{23,22},{2... | collective-permute-start | bytes 9437192 | tf_op jit(solution)/shard_map/ppermute | solution.py:939
  69.8 8.6 %copy-start.6 = (f32[1,1024]{1,0:T(1,128)S(1)}, f32[1,1024]{1,0:T(1,128)}, u32[]{:S(2)}) copy-start(f32[1,1024]{1,0:T(1,128)} %get-tuple-element.65) | copy-start | bytes 12292
  69.8 8.6 %copy-start.7 = (f32[1,1024]{1,0:T(1,128)S(1)}, f32[1,1024]{1,0:T(1,128)}, u32[]{:S(2)}) copy-start(f32[1,1024]{1,0:T(1,128)} %get-tuple-element.66) | copy-start | bytes 12292
  77.1 64.7 %collective-permute-start.1 = (bf16[512,1024]{1,0:T(8,128)(2,1)}, bf16[512,1024]{1,0:T(8,128)(2,1)S(1)}, u32[]{:S(2)}, u32[]{:S(2)}) collective-permute-start(bf16[512,1024]{1,0:T(8,128)(2,1)} %get-tuple-element.58), channel_id=1, source_target_pairs={{16,0},{17,1},{18,2},{19,3},{20,4},{21,5},{22,6},{23,7},{24,8},{25... | collective-permute-start | bytes 3145736 | tf_op jit(solution)/shard_map/ppermute | solution.py:967
  79.7 1.0 copy-start.11
  141.7 2.0 copy-start.10
  181.3 34.8 %collective-permute-start.6 = (bf16[512,1024]{1,0:T(8,128)(2,1)}, bf16[512,1024]{1,0:T(8,128)(2,1)}, u32[]{:S(2)}, u32[]{:S(2)}) collective-permute-start(bf16[512,1024]{1,0:T(8,128)(2,1)} %copy-done.10), channel_id=1, source_target_pairs={{0,1},{1,0},{2,3},{3,2},{4,5},{5,4},{6,7},{7,6},{8,9},{9,8},{10,11... | collective-permute-start | bytes 3145736 | tf_op jit(solution)/shard_map/ppermute | solution.py:939
  185.2 26.0 %copy-start.8 = (f32[1,1024]{1,0:T(1,128)S(1)}, f32[1,1024]{1,0:T(1,128)}, u32[]{:S(2)}) copy-start(f32[1,1024]{1,0:T(1,128)} %get-tuple-element.82) | copy-start | bytes 12292
  185.2 26.0 %copy-start.9 = (f32[1,1024]{1,0:T(1,128)S(1)}, f32[1,1024]{1,0:T(1,128)}, u32[]{:S(2)}) copy-start(f32[1,1024]{1,0:T(1,128)} %get-tuple-element.83) | copy-start | bytes 12292
  185.3 27.3 %copy-start.1 = (f32[512,1024]{1,0:T(8,128)S(1)}, f32[512,1024]{1,0:T(8,128)}, u32[]{:S(2)}) copy-start(f32[512,1024]{1,0:T(8,128)} %get-tuple-element.73) | copy-start | bytes 6291460
  435.2 5.0 %copy-start.5 = (bf16[256,1024]{1,0:T(8,128)(2,1)S(1)}, bf16[256,1024]{1,0:T(8,128)(2,1)}, u32[]{:S(2)}) copy-start(bf16[256,1024]{1,0:T(8,128)(2,1)} %get-tuple-element.90) | copy-start | bytes 1572868
  436.6 4.7 %copy-start = (bf16[256,8192]{1,0:T(8,128)(2,1)S(1)}, bf16[256,8192]{1,0:T(8,128)(2,1)}, u32[]{:S(2)}) copy-start(bf16[256,8192]{1,0:T(8,128)(2,1)} %get-tuple-element.91) | copy-start | bytes 12582916
  441.3 4.4 copy-start.2

commit v6 on v5

--- a/solution.py
+++ b/solution.py
@@ -403,7 +403,7 @@
 
 
 def exchange_kernel(cfg, *refs):
-    shards, bits, seats, unit_rows, width, section, aliased, late, layers = cfg
+    shards, bits, seats, unit_rows, width, section, aliased, late, layers, lag = cfg
     arrays = len(seats)
     refs = list(refs)
 
@@ -434,6 +434,7 @@
     chain_rows = (final_rows, unit_rows)
     depth = chain_a.shape[1] - 1
     ring = mine.shape[1]
+    slots, right_slots = piece.shape[1], right.shape[0]
     sec = lax.axis_index("section")
     here = lax.axis_index("shard")
     seat = lax.axis_index("group")
@@ -534,31 +535,43 @@
         return outer, aligned((block - outer * inner) * (4 * width) + bit * (2 * width), 2 * width)
 
     def loads(chunk, run):
-        two, four = lax.rem(chunk, 2), lax.rem(chunk, 5)
-
+        slot = lax.rem(chunk, right_slots)
+
+        def each(which, row, block):
+            outer, columns = right_columns(which, block, half)
+            run(pltpu.make_async_copy(
+                rights[which].at[outer, :, columns], right.at[slot, :tokens], right_sem.at[slot]))
+            if split_rows(which):
+                run(pltpu.make_async_copy(
+                    right_others[0].at[:, columns], right.at[slot, tokens:], other_sem.at[slot]))
+        each_array(chunk, each)
+
+    def load_left(chunk):
         def each(which, row, block):
             rows = seats[which][3]
-            outer, columns = right_columns(which, block, half)
-            run(pltpu.make_async_copy(
-                rights[which].at[outer, :, columns], right.at[four, :tokens], right_sem.at[four]))
-            if split_rows(which):
-                run(pltpu.make_async_copy(
-                    right_others[0].at[:, columns], right.at[four, tokens:], other_sem.at[four]))
+            kind = int(split_rows(which))
+            copies = []
             for shard in range(shards):
                 if split_rows(which):
                     offsets = (shard * rows + (2 * row + half) * unit_rows, shard * (rows // 2) + row * unit_rows)
                 else:
                     offsets = (shard * rows + row * unit_rows,) * 2
-                for which_side, source in enumerate((lefts[which], left_others[which])):
-                    run(pltpu.make_async_copy(
-                        source.at[:, aligned(offsets[which_side], unit_rows)],
-                        left.at[two, which_side * tokens:(which_side + 1) * tokens,
-                                shard * unit_rows:(shard + 1) * unit_rows],
-                        left_sem.at[two, which_side, shard]))
+                for side, source in enumerate((lefts[which], left_others[which])):
+                    copies.append(pltpu.make_async_copy(
+                        source.at[:, aligned(offsets[side], unit_rows)],
+                        left.at[kind, side * tokens:(side + 1) * tokens, shard * unit_rows:(shard + 1) * unit_rows],
+                        left_sem.at[kind, side, shard]))
+
+            def fetch():
+                for copy in copies:
+                    copy.start()
+                for copy in copies:
+                    copy.wait()
+            on(block == 0, fetch)
         each_array(chunk, each)
 
     def right_copy(chunk, source):
-        four = lax.rem(chunk, 5)
+        four = lax.rem(chunk, right_slots)
         return remote(source, right.at[four, tokens:], right_send.at[four], right_recv.at[four], across(0))
 
     def send_right(chunk):
@@ -594,22 +607,24 @@
             begin = need
 
     def multiply(chunk):
-        two, four, slot = lax.rem(chunk, 2), lax.rem(chunk, 5), lax.rem(chunk, ring)
+        four, slot = lax.rem(chunk, right_slots), lax.rem(chunk, ring)
+        load_left(chunk)
         loads(chunk, lambda copy: copy.wait())
+        last = seat_of(chunk)[0]
 
         def arrived():
             copy = right_copy(chunk, right.at[four, tokens:])
             copy.wait_recv()
             copy.wait_send()
-        on(jnp.logical_not(seat_of(chunk)[0]), arrived)
-        result = lax.dot_general(left[two], right[four], (((0,), (0,)), ((), ())), preferred_element_type=F32)
+        on(jnp.logical_not(last), arrived)
+        result = lax.dot_general(left[last.astype(jnp.int32)], right[four], (((0,), (0,)), ((), ())), preferred_element_type=F32)
         for shard in range(shards):
             for path in range(2):
                 mine[path, slot, shard] = result[
                     shard * unit_rows:(shard + 1) * unit_rows, path * width:(path + 1) * width].astype(BF16)
 
     def side_copy(step, chunk):
-        slot, four = lax.rem(chunk, ring), lax.rem(chunk, 4)
+        slot, four = lax.rem(chunk, ring), lax.rem(chunk, slots)
         rows = unit_rows >> (step + 1)
         away = aligned((1 - bit_of(step + 1)) * rows, rows)
         source = mine.at[0, slot, :, away] if step == 0 else side.at[step - 1, slot, :, away]
@@ -617,7 +632,7 @@
                       across(step + 1))
 
     def side_sum(step, chunk):
-        slot, four = lax.rem(chunk, ring), lax.rem(chunk, 4)
+        slot, four = lax.rem(chunk, ring), lax.rem(chunk, slots)
         rows = unit_rows >> (step + 1)
         kept = bit_of(step + 1) * rows
         copy = side_copy(step, chunk)
@@ -687,12 +702,12 @@
             share(0, chunk, total)
 
     def rest_copy(step, chunk):
-        slot, rows = lax.rem(chunk, 4), pl.ds(0, unit_rows >> (step + 1))
+        slot, rows = lax.rem(chunk, slots), pl.ds(0, unit_rows >> (step + 1))
         return remote(rest_send.at[step, slot, rows], rest_land.at[step, slot, rows], rest_ssem.at[step, slot],
                       rest_rsem.at[step, slot], across(step + 1))
 
     def share(step, chunk, total):
-        slot, rows = lax.rem(chunk, 4), unit_rows >> (step + 1)
+        slot, rows = lax.rem(chunk, slots), unit_rows >> (step + 1)
         bit = bit_of(step + 1)
 
         def give(part):
@@ -705,7 +720,7 @@
         by_rows(rows, keep)
 
     def rest_sum(step, chunk):
-        slot = lax.rem(chunk, 4)
+        slot = lax.rem(chunk, slots)
         copy = rest_copy(step, chunk)
         copy.wait_recv()
         copy.wait_send()
@@ -720,7 +735,7 @@
 
     def finish(path, chunk, total):
         def put(part):
-            piece[path, lax.rem(chunk, 4), part] = total(part, 0).astype(BF16)
+            piece[path, lax.rem(chunk, slots), part] = total(part, 0).astype(BF16)
         by_rows(final_rows, put)
         spread(path, 0, chunk)
 
@@ -738,11 +753,11 @@
         return row
 
     def store(path, chunk, target):
-        slot = lax.rem(chunk, 4)
+        slot = lax.rem(chunk, slots)
         return pltpu.make_async_copy(piece.at[path, slot], target, store_sem.at[path, slot])
 
     def gather(path, step, other, chunk, target):
-        slot = lax.rem(chunk, 4)
+        slot = lax.rem(chunk, slots)
         source = piece.at[path, slot] if step == 0 else target
         return remote(source, target, gather_send.at[path, step, other, slot], gather_recv.at[path, step, other, slot],
                       across(0 if step == 0 else bits - step))
@@ -779,7 +794,8 @@
         def _(step):
             pl.semaphore_signal(barrier, inc=1, device_id=peer(step)[1], device_id_type=MESH)
         pl.semaphore_wait(barrier, peers - 1)
-        send_right(0)
+        for chunk in range(lag):
+            send_right(chunk)
         loads(0, lambda copy: copy.start())
 
         @pl.loop(1, peers)
@@ -796,9 +812,9 @@
 
         line = shards - 1
 
-        @pl.loop(0, units + line + others + bits + 2)
+        @pl.loop(0, units + lag * (line + others + bits) + 2)
         def _(turn):
-            on(turn + 1 < units, lambda: send_right(turn + 1))
+            on(turn + lag < units, lambda: send_right(turn + lag))
             if late:
                 late_turn(turn)
             on(turn + 1 < units, lambda: loads(turn + 1, lambda copy: copy.start()))
@@ -808,19 +824,21 @@
                 side_copy(0, turn).start()
             on(turn < units, opening)
             for step in range(others):
-                on(valid(turn - 1 - step), lambda step=step: side_sum(step, turn - 1 - step))
+                chunk = turn - lag * (1 + step)
+                on(valid(chunk), lambda step=step, chunk=chunk: side_sum(step, chunk))
             for path in range(2):
                 for way in range(2):
-                    chunk = turn - (others if path == 0 else 0) - (here if way == 0 else line - here)
+                    chunk = turn - lag * ((others if path == 0 else 0) + (here if way == 0 else line - here))
                     on(valid(chunk - 2), lambda path=path, way=way, chunk=chunk: sent(path, way, chunk - 2))
                     on(valid(chunk), lambda path=path, way=way, chunk=chunk: onward(path, way, chunk))
-            on(valid(turn - line), lambda: last_hop(1, turn - line))
-            on(valid(turn - line - others), lambda: last_hop(0, turn - line - others))
+            on(valid(turn - lag * line), lambda: last_hop(1, turn - lag * line))
+            on(valid(turn - lag * (line + others)), lambda: last_hop(0, turn - lag * (line + others)))
             for step in range(others):
-                on(valid(turn - line - 1 - step), lambda step=step: rest_sum(step, turn - line - 1 - step))
+                chunk = turn - lag * (line + 1 + step)
+                on(valid(chunk), lambda step=step, chunk=chunk: rest_sum(step, chunk))
             for step in range(bits):
                 for path in range(2):
-                    chunk = turn - line - others - 1 - step
+                    chunk = turn - lag * (line + others + 1 + step)
                     on(valid(chunk), lambda path=path, step=step, chunk=chunk: gathered(path, step, chunk))
 
         vector_finish()
@@ -831,7 +849,7 @@
         pl.when(sec == section)(work)
 
 
-def exchange(pairs, vector, shards, group, section, collective_id, unit_width, previous=None, unit_rows_max=256,
+def exchange(pairs, vector, shards, group, section, collective_id, unit_width, previous=None, lag=2, unit_rows_max=256,
              name="exchange"):
     bits = group.bit_length() - 1
     arrays = len(pairs)
@@ -853,7 +871,8 @@
     units = sum(seat[0] for seat in seats)
     others = bits - 1
     final_rows = unit_rows >> others
-    depth, ring = shards + 3, shards + 2
+    slots, right_slots = 2 * lag + 2, 2 * lag + 3
+    depth, ring = lag * shards + 3, lag * (shards - 1) + 2
     late_rows = rows_of[-1] // (2 * unit_rows)
     peers, lanes = shards * group, vector.shape[1] // shards
     dma = pltpu.SemaphoreType.DMA
@@ -862,26 +881,26 @@
         pltpu.VMEM((vector.shape[0], lanes), F32),
         dma((peers,)), dma((peers,)), dma,
         pltpu.VMEM((2, 2 * tokens, shards * unit_rows), BF16),
-        pltpu.VMEM((5, 2 * tokens, 2 * width), BF16),
-        dma((2, 2, shards)), dma((5,)), dma((5,)),
-        dma((5,)), dma((5,)),
+        pltpu.VMEM((right_slots, 2 * tokens, 2 * width), BF16),
+        dma((2, 2, shards)), dma((right_slots,)), dma((right_slots,)),
+        dma((right_slots,)), dma((right_slots,)),
         dma((late_rows, shards)), dma((late_rows, shards)),
         pltpu.VMEM((2, ring, shards, unit_rows, width), BF16),
-        pltpu.VMEM((others, 4, shards, unit_rows // 2, width), BF16),
+        pltpu.VMEM((others, slots, shards, unit_rows // 2, width), BF16),
         pltpu.VMEM((others, ring, shards, unit_rows // 2, width), BF16),
-        dma((others, 4)), dma((others, 4)),
+        dma((others, slots)), dma((others, slots)),
         pltpu.VMEM((2, depth + 1, shards, final_rows, width), BF16),
         pltpu.VMEM((2, depth + 1, shards, unit_rows, width), BF16),
         dma((2, 2, depth, shards)), dma((2, 2, depth, shards)),
-        pltpu.VMEM((others, 4, unit_rows // 2, width), BF16),
-        pltpu.VMEM((others, 4, unit_rows // 2, width), BF16),
-        pltpu.VMEM((others, 4, unit_rows // 2, width), F32),
-        dma((others, 4)), dma((others, 4)),
-        pltpu.VMEM((2, 4, final_rows, width), BF16),
-        dma((2, 4)),
-        dma((2, bits, 2, 4)), dma((2, bits, 2, 4)),
+        pltpu.VMEM((others, slots, unit_rows // 2, width), BF16),
+        pltpu.VMEM((others, slots, unit_rows // 2, width), BF16),
+        pltpu.VMEM((others, slots, unit_rows // 2, width), F32),
+        dma((others, slots)), dma((others, slots)),
+        pltpu.VMEM((2, slots, final_rows, width), BF16),
+        dma((2, slots)),
+        dma((2, bits, 2, slots)), dma((2, bits, 2, slots)),
     ]
-    cfg = (shards, bits, tuple(seats), unit_rows, width, section, previous is not None, late, layers)
+    cfg = (shards, bits, tuple(seats), unit_rows, width, section, previous is not None, late, layers, lag)
     operands = lefts + rights + left_others + [pairs[-1][3], vector] + list(previous or [])
     first = len(operands) - len(previous or [])
     results = [jax.ShapeDtypeStruct((r, g.shape[0] * g.shape[2]), BF16) for r, g in zip(rows_of, rights)]
@@ -966,13 +985,13 @@
     result, _, returned, hidden_1, rights_1, vectors_1 = back(second, middle_1, lefts_1, qkv_1, arrived, rows)
     returned = lax.ppermute(returned, "section", [(1, 0)])
     sums = sum_all(1, lefts_1, lefts_beside_1, hidden_1, None, rights_1, rows_beside, vectors_1,
-                   name="exchange_second")
+                   name="exchange_second", lag=1)
     returned, _, lefts_beside_0, hidden_beside_0 = lax.optimization_barrier(
         (returned, sums[4], lefts_beside_0, hidden_beside_0))
     returned_beside = beside(0, returned)
     _, grad_in, _, hidden_0, rights_0, vectors_0 = back(first, middle_0, lefts_0, qkv_0, rows, returned)
     sums = sum_all(0, lefts_0, lefts_beside_0, hidden_0, hidden_beside_0, rights_0, returned_beside, vectors_0,
-                   previous=sums, name="exchange_first")
+                   previous=sums, name="exchange_first", lag=2)
     ends_out = jnp.where(is_first, grad_in, result)[None]
     grad_gate_up, grad_out, grad_qkv, grad_down = (item.astype(F32)[None] for item in sums[:4])
     vectors = sums[4]

time: 450 us -> 443 us (0.984)
  Pallas kernels: 359 us -> 352 us
    pallas_call x2, Pallas kernels: 236 us -> 228 us  [exchange(): pl.pallas_call(functools.partial(exchange_kernel, cfg), out_shape=results...]
where the time goes in v6:
time: 443 us; the launch traced here: 442 us
  Pallas kernels  352 us (79%)
  waiting for transfers between devices  47.9 us (11%)
  other arithmetic  18.5 us (4%)
  starting transfers between devices  16.6 us (4%)
  local copies, waits for them, and re-layouts  6.3 us (1%)
    pallas_call x2, Pallas kernels, exchange(): pl.pallas_call(functools.partial(exchange_kernel, cfg), out_shape=results...  228 us
    pallas_call x7, Pallas kernels, local_call(): pl.pallas_call(kernel, grid_spec=pltpu.PrefetchScalarGridSpec(num_scalar_...  124 us
    ppermute x1, waiting for transfers between devices, body(): returned = lax.ppermute(returned, 'section', [(1, 0)])  45.9 us
    ppermute x5, starting transfers between devices, beside(): return lax.ppermute(array, ('section', 'group'), pairs)  13.9 us
    broadcast_in_dim x4, other arithmetic, body(): item.astype(F32)[None]  11.5 us
  transfers between devices with their start and end apart: 7, of which 2 were waited for; matrix products, arithmetic and copies ran while one was open for 1% of the time, Pallas kernels for 14%

profile of v6, /device:TPU:0, one launch (start us, length us, event | category | flops | bytes accessed | tf_op | source)
XLA Modules:
  0.0 442.4 jit_solution(4911116015322776701)
XLA Ops:
  0.7 1.0 fusion.7
  1.7 0.1 broadcast_bitcast_fusion.4
  2.0 1.8 multiply_sine_fusion
  3.8 0.6 pad_add_fusion.act_ref
  4.4 19.9 %attention.2 = (f32[512,1024]{1,0:T(8,128)}, bf16[3,512,1024]{2,1,0:T(8,128)(2,1)}, bf16[3,512,1024]{2,1,0:T(8,128)(2,1)}) custom-call(s32[1]{0:T(128)} %bitcast.act_ref, s32[2,3]{1,0:T(2,128)} %lengths_ref.7, bf16[512,1024]{1,0:T(8,128)(2,1)} %bitcast.59, f32[1,1024]{1,0:T(1,128)} %gain_ref.11, f32[1,1024]{1,0:T(1,128)} %bias_ref.3, f32[1,1024]{1,0:T(1,128)} %gain_ref.10, ...), custom_call_target="tpu_custom_call" | custom-call | flops 4294967296 | bytes 41943040 | tf_op jit(solution)/shard_map/attention/pallas_call | solution.py:306
  24.3 20.7 %feed.1 = (bf16[512,1024]{1,0:T(8,128)(2,1)}, bf16[512,2048]{1,0:T(8,128)(2,1)}) custom-call(s32[2]{0:T(128)} %pad_add_fusion.act_ref, f32[512,1024]{1,0:T(8,128)} %get-tuple-element.51.mid_ref, bf16[3,512,1024]{2,1,0:T(8,128)(2,1)} %get-tuple-element.52.low_ref.refs_0_.refs_1_.refs_2_, bf16[1024,8192]{1,0:T(8,128)(2,1)} %bitcast.69, ...), custom_call_target="tpu_custom_call" | custom-call | flops 12884901888 | bytes 41943040 | tf_op jit(solution)/shard_map/feed/pallas_call | solution.py:306
  45.0 1.3 collective-permute-start
  46.4 0.7 collective-permute-start.3
  47.1 4.8 %collective-permute-start.4 = (bf16[3,512,1024]{2,1,0:T(8,128)(2,1)}, bf16[3,512,1024]{2,1,0:T(8,128)(2,1)}, u32[]{:S(2)}, u32[]{:S(2)}) collective-permute-start(bf16[3,512,1024]{2,1,0:T(8,128)(2,1)} %get-tuple-element.52.low_ref.refs_0_.refs_1_.refs_2_), channel_id=1, source_target_pairs={{0,1},{1,0},{2,3},{3,2},{4,5},{5,4},{6,7},{7,6},{8,9},{9,8},{10,11... | collective-permute-start | bytes 9437192 | tf_op jit(solution)/shard_map/ppermute | solution.py:958
  52.0 2.2 collective-permute-start.5
  54.2 1.0 copy-done.4
  55.1 6.7 %attention.3 = (f32[512,1024]{1,0:T(8,128)}, bf16[3,512,1024]{2,1,0:T(8,128)(2,1)}, bf16[3,512,1024]{2,1,0:T(8,128)(2,1)}) custom-call(s32[1]{0:T(128)} %bitcast.4.act_ref, s32[2,3]{1,0:T(2,128)} %lengths_ref.7, bf16[512,1024]{1,0:T(8,128)(2,1)} %copy-done.4, f32[1,1024]{1,0:T(1,128)} %gain_ref.11, f32[1,1024]{1,0:T(1,128)} %bias_ref.3, ...), custom_call_target="tpu_custom_call" | custom-call | flops 4294967296 | bytes 41943040 | tf_op jit(solution)/shard_map/attention/pallas_call | solution.py:306
  61.9 2.3 collective-permute-start.2
  64.1 5.7 %feed_both.2 = (f32[512,1024]{1,0:T(8,128)}, bf16[512,4096]{1,0:T(8,128)(2,1)}, bf16[2,512,4096]{2,1,0:T(8,128)(2,1)}, f32[512,1024]{1,0:T(8,128)}, f32[1,1024]{1,0:T(1,128)}, /*index=5*/f32[1,1024]{1,0:T(1,128)}) custom-call(s32[1]{0:T(128)} %bitcast.4.act_ref, f32[512,1024]{1,0:T(8,128)} %get-tuple-element.54.mid_ref, ...), custom_call_target="tpu_custom_call" | custom-call | flops 25769803776 | bytes 41943040 | tf_op jit(solution)/shard_map/feed_both/pallas_call | solution.py:306
  69.8 7.3 %attention_back.2 = (bf16[512,1024]{1,0:T(8,128)(2,1)}, bf16[3,512,1024]{2,1,0:T(8,128)(2,1)}, f32[512,1024]{1,0:T(8,128)}, bf16[512,1024]{1,0:T(8,128)(2,1)}, f32[1,1024]{1,0:T(1,128)}, /*index=5*/f32[1,1024]{1,0:T(1,128)}) custom-call(s32[1]{0:T(128)} %bitcast.4.act_ref, s32[2,3]{1,0:T(2,128)} %lengths_ref.7, f32[512,1024]{1,0:T(8,128)} %get-tuple-element.56.grad_ref, ...), custom_call_target="tpu_custom_call" | custom-call | flops 10737418240 | bytes 41943040 | tf_op jit(solution)/shard_map/attention_back/pallas_call | solution.py:306
  77.1 1.3 collective-permute-start.1
  78.4 1.3 concatenate.10.refs_12_
  79.7 1.0 copy-done.11
  80.7 15.1 %exchange_second.1 = (bf16[256,8192]{1,0:T(8,128)(2,1)}, bf16[256,1024]{1,0:T(8,128)(2,1)}, bf16[256,3072]{1,0:T(8,128)(2,1)}, bf16[1024,1024]{1,0:T(8,128)(2,1)...) custom-call(bf16[3,512,1024]{2,1,0:T(8,128)(2,1)} %get-tuple-element.55.low_ref.refs_0_.refs_1_.refs_2_, ...), custom_call_target="tpu_custom_call" | custom-call | flops 17179869184 | bytes 104857600 | tf_op jit(solution)/shard_map/exchange_second/pallas_call | solution.py:912
  95.8 45.9 %collective-permute-done.1.grad_ref = bf16[512,1024]{1,0:T(8,128)(2,1)S(1)} collective-permute-done((bf16[512,1024]{1,0:T(8,128)(2,1)}, bf16[512,1024]{1,0:T(8,128)(2,1)S(1)}, u32[]{:S(2)}, u32[]{:S(2)}) %collective-permute-start.1) | collective-permute-done | bytes 1048608 | tf_op jit(solution)/shard_map/ppermute | solution.py:986
  141.7 2.0 collective-permute-done.5.refs_11_
  143.7 37.6 %feed_both.3 = (f32[512,1024]{1,0:T(8,128)}, bf16[512,4096]{1,0:T(8,128)(2,1)}, bf16[2,512,4096]{2,1,0:T(8,128)(2,1)}, f32[512,1024]{1,0:T(8,128)}, f32[1,1024]{1,0:T(1,128)}, /*index=5*/f32[1,1024]{1,0:T(1,128)}) custom-call(s32[1]{0:T(128)} %bitcast.act_ref, f32[512,1024]{1,0:T(8,128)} %get-tuple-element.51.mid_ref, ...), custom_call_target="tpu_custom_call" | custom-call | flops 25769803776 | bytes 41943040 | tf_op jit(solution)/shard_map/feed_both/pallas_call | solution.py:306
  181.3 3.9 collective-permute-start.6
  185.3 26.0 %attention_back.3 = (bf16[512,1024]{1,0:T(8,128)(2,1)}, bf16[3,512,1024]{2,1,0:T(8,128)(2,1)}, f32[512,1024]{1,0:T(8,128)}, bf16[512,1024]{1,0:T(8,128)(2,1)}, f32[1,1024]{1,0:T(1,128)}, /*index=5*/f32[1,1024]{1,0:T(1,128)}) custom-call(s32[1]{0:T(128)} %bitcast.act_ref, s32[2,3]{1,0:T(2,128)} %lengths_ref.7, f32[512,1024]{1,0:T(8,128)} %get-tuple-element.70.grad_ref, ...), custom_call_target="tpu_custom_call" | custom-call | flops 10737418240 | bytes 41943040 | tf_op jit(solution)/shard_map/attention_back/pallas_call | solution.py:306
  211.3 1.3 concatenate.11.refs_13_
  212.6 3.5 select_bitcast_fusion
  216.1 213.2 %exchange_first.1 = (bf16[256,8192]{1,0:T(8,128)(2,1)}, bf16[256,1024]{1,0:T(8,128)(2,1)}, bf16[256,3072]{1,0:T(8,128)(2,1)}, bf16[1024,1024]{1,0:T(8,128)(2,1)}, f32[8,256]{1,0:T(8,128)}) custom-call(bf16[3,512,1024]{2,1,0:T(8,128)(2,1)} %get-tuple-element.52.low_ref.refs_0_.refs_1_.r, ...), custom_call_target="tpu_custom_call", output_to_operand_aliasing={{0}: (14, {}), {1}: (15, {}), {2}: (16, {}), {3}: (17, {}),... | custom-call | flops 17179869184 | bytes 104857600 | tf_op jit(solution)/shard_map/exchange_first/pallas_call | solution.py:912
  429.3 1.4 fusion.8
  430.7 3.6 bitcast_convert_fusion.2
  434.3 1.1 bitcast_convert_fusion.3
  435.4 4.4 bitcast_convert_fusion
  439.7 2.5 bitcast_convert_fusion.1
  (39 shorter events, 0.2 us)
Async XLA Ops:
  24.3 22.0 %copy-start.3 = (bf16[1,512,1024]{2,1,0:T(8,128)(2,1)S(1)}, bf16[1,512,1024]{2,1,0:T(8,128)(2,1)}, u32[]{:S(2)}) copy-start(bf16[1,512,1024]{2,1,0:T(8,128)(2,1)} %refs_7_.1) | copy-start | bytes 3145732
  45.0 9.1 %collective-permute-start = (bf16[512,1024]{1,0:T(8,128)(2,1)}, bf16[512,1024]{1,0:T(8,128)(2,1)S(1)}, u32[]{:S(2)}, u32[]{:S(2)}) collective-permute-start(bf16[512,1024]{1,0:T(8,128)(2,1)} %get-tuple-element.53), channel_id=1, source_target_pairs={{0,16},{1,17},{2,18},{3,19},{4,20},{5,21},{6,22},{7,23},{8,24},{9,... | collective-permute-start | bytes 3145736 | tf_op jit(solution)/shard_map/ppermute | solution.py:981
  46.4 33.3 %collective-permute-start.3 = (bf16[512,1024]{1,0:T(8,128)(2,1)S(1)}, bf16[512,1024]{1,0:T(8,128)(2,1)S(1)}, u32[]{:S(2)}, u32[]{:S(2)}) collective-permute-start(bf16[512,1024]{1,0:T(8,128)(2,1)S(1)} %bitcast.62), channel_id=1, source_target_pairs={{16,17},{17,16},{18,19},{19,18},{20,21},{21,20},{22,23},{23,22},{2... | collective-permute-start | bytes 3145736 | tf_op jit(solution)/shard_map/ppermute | solution.py:958
  47.1 96.6 %collective-permute-start.4 = (bf16[3,512,1024]{2,1,0:T(8,128)(2,1)}, bf16[3,512,1024]{2,1,0:T(8,128)(2,1)}, u32[]{:S(2)}, u32[]{:S(2)}) collective-permute-start(bf16[3,512,1024]{2,1,0:T(8,128)(2,1)} %get-tuple-element.52.low_ref.refs_0_.refs_1_.refs_2_), channel_id=1, source_target_pairs={{0,1},{1,0},{2,3},{3,2},{4,5},{5,4},{6,7},{7,6},{8,9},{9,8},{10,11... | collective-permute-start | bytes 9437192 | tf_op jit(solution)/shard_map/ppermute | solution.py:958
  52.0 91.7 %collective-permute-start.5 = (bf16[512,2048]{1,0:T(8,128)(2,1)}, bf16[512,2048]{1,0:T(8,128)(2,1)}, u32[]{:S(2)}, u32[]{:S(2)}) collective-permute-start(bf16[512,2048]{1,0:T(8,128)(2,1)} %get-tuple-element.68), channel_id=1, source_target_pairs={{0,1},{1,0},{2,3},{3,2},{4,5},{5,4},{6,7},{7,6},{8,9},{9,8},{10,11... | collective-permute-start | bytes 6291464 | tf_op jit(solution)/shard_map/ppermute | solution.py:958
  54.2 1.0 copy-start.4
  61.9 17.9 %collective-permute-start.2 = (bf16[3,512,1024]{2,1,0:T(8,128)(2,1)}, bf16[3,512,1024]{2,1,0:T(8,128)(2,1)}, u32[]{:S(2)}, u32[]{:S(2)}) collective-permute-start(bf16[3,512,1024]{2,1,0:T(8,128)(2,1)} %get-tuple-element.55.low_ref.refs_0_.refs_1_.refs_2_), channel_id=1, source_target_pairs={{16,17},{17,16},{18,19},{19,18},{20,21},{21,20},{22,23},{23,22},{2... | collective-permute-start | bytes 9437192 | tf_op jit(solution)/shard_map/ppermute | solution.py:958
  69.8 8.6 %copy-start.6 = (f32[1,1024]{1,0:T(1,128)S(1)}, f32[1,1024]{1,0:T(1,128)}, u32[]{:S(2)}) copy-start(f32[1,1024]{1,0:T(1,128)} %get-tuple-element.65) | copy-start | bytes 12292
  69.8 8.6 %copy-start.7 = (f32[1,1024]{1,0:T(1,128)S(1)}, f32[1,1024]{1,0:T(1,128)}, u32[]{:S(2)}) copy-start(f32[1,1024]{1,0:T(1,128)} %get-tuple-element.66) | copy-start | bytes 12292
  77.1 64.7 %collective-permute-start.1 = (bf16[512,1024]{1,0:T(8,128)(2,1)}, bf16[512,1024]{1,0:T(8,128)(2,1)S(1)}, u32[]{:S(2)}, u32[]{:S(2)}) collective-permute-start(bf16[512,1024]{1,0:T(8,128)(2,1)} %get-tuple-element.58), channel_id=1, source_target_pairs={{16,0},{17,1},{18,2},{19,3},{20,4},{21,5},{22,6},{23,7},{24,8},{25... | collective-permute-start | bytes 3145736 | tf_op jit(solution)/shard_map/ppermute | solution.py:986
  79.7 1.0 copy-start.11
  141.7 2.0 copy-start.10
  181.3 34.8 %collective-permute-start.6 = (bf16[512,1024]{1,0:T(8,128)(2,1)}, bf16[512,1024]{1,0:T(8,128)(2,1)}, u32[]{:S(2)}, u32[]{:S(2)}) collective-permute-start(bf16[512,1024]{1,0:T(8,128)(2,1)} %copy-done.10), channel_id=1, source_target_pairs={{0,1},{1,0},{2,3},{3,2},{4,5},{5,4},{6,7},{7,6},{8,9},{9,8},{10,11... | collective-permute-start | bytes 3145736 | tf_op jit(solution)/shard_map/ppermute | solution.py:958
  185.2 26.0 %copy-start.8 = (f32[1,1024]{1,0:T(1,128)S(1)}, f32[1,1024]{1,0:T(1,128)}, u32[]{:S(2)}) copy-start(f32[1,1024]{1,0:T(1,128)} %get-tuple-element.82) | copy-start | bytes 12292
  185.2 26.0 %copy-start.9 = (f32[1,1024]{1,0:T(1,128)S(1)}, f32[1,1024]{1,0:T(1,128)}, u32[]{:S(2)}) copy-start(f32[1,1024]{1,0:T(1,128)} %get-tuple-element.83) | copy-start | bytes 12292
  185.3 27.3 %copy-start.1 = (f32[512,1024]{1,0:T(8,128)S(1)}, f32[512,1024]{1,0:T(8,128)}, u32[]{:S(2)}) copy-start(f32[512,1024]{1,0:T(8,128)} %get-tuple-element.73) | copy-start | bytes 6291460
  429.2 5.0 %copy-start.5 = (bf16[256,1024]{1,0:T(8,128)(2,1)S(1)}, bf16[256,1024]{1,0:T(8,128)(2,1)}, u32[]{:S(2)}) copy-start(bf16[256,1024]{1,0:T(8,128)(2,1)} %get-tuple-element.90) | copy-start | bytes 1572868
  430.7 4.7 %copy-start = (bf16[256,8192]{1,0:T(8,128)(2,1)S(1)}, bf16[256,8192]{1,0:T(8,128)(2,1)}, u32[]{:S(2)}) copy-start(bf16[256,8192]{1,0:T(8,128)(2,1)} %get-tuple-element.91) | copy-start | bytes 12582916
  435.4 4.4 copy-start.2

commit v7 on v6

--- a/solution.py
+++ b/solution.py
@@ -119,8 +119,9 @@
                 qkv_ref[which, :, lanes] = values.astype(BF16)
 
         first = lanes_of((row_tokens, pair)) < size
-        for row in range(tokens // row_tokens):
-            rows = pl.ds(row * row_tokens, row_tokens)
+        @pl.loop(0, tokens // row_tokens)
+        def _(row):
+            rows = pl.ds(pl.multiple_of(row * row_tokens, row_tokens), row_tokens)
             allowed = same_window(lengths_ref, row, row_tokens)
             for start in range(0, block // pair, 2):
                 work = []
@@ -149,86 +150,150 @@
             in_rows(tokens, 64, close)
 
 
-def attention_back_kernel(size, row_tokens, act_ref, lengths_ref, grad_ref, x_ref, gain_ref, qkv_ref, wq_ref, wk_ref,
-                          wv_ref, wo_ref, cos_ref, sin_ref, branch_ref, proj_ref, input_ref, input_low_ref,
-                          dgain_ref, dbias_ref, gm_ref, total_ref):
-    tokens = x_ref.shape[0]
-    part = pl.program_id(0)
-    block = wq_ref.shape[1]
+def attention_back_kernel(size, row_tokens, parts, act_ref, lengths_ref, grad_in, x_in, qkv_in, wqkv_in, wo_in, cos_in,
+                          sin_in, branch_out, proj_out, input_out, input_low_out, vectors_out, grad_ref, x_ref, qkv_ref,
+                          wqkv_ref, wo_ref, cos_ref, sin_ref, branch_ref, proj_ref, input_low_ref, vectors_ref, gm_ref,
+                          total_ref, load_sem, part_sem, store_sem):
+    tokens, features = x_ref.shape
+    block = features // parts
     pair = 2 * size
     scale = size ** -0.5
-
-    @pl.when(act_ref[0] == 1)
+    copy = pltpu.make_async_copy
+
+    def work():
+        loads = [
+            copy(source, target, load_sem.at[index]) for index, (source, target) in enumerate(
+                ((grad_in, grad_ref), (cos_in, cos_ref), (sin_in, sin_ref), (x_in, x_ref)))]
+        part_loads = []
+        for part in range(parts):
+            lanes = pl.ds(part * block, block)
+            part_loads.append([copy(wo_in.at[lanes], wo_ref.at[lanes], part_sem.at[part, 0]),
+                               copy(qkv_in.at[:, :, lanes], qkv_ref.at[:, :, lanes], part_sem.at[part, 1])] + [
+                copy(wqkv_in.at[:, pl.ds(which * features + part * block, block)],
+                     wqkv_ref.at[:, pl.ds(which * features + part * block, block)], part_sem.at[part, 2 + which])
+                for which in range(3)])
+        for item in loads[:1] + part_loads[0][:2] + loads[1:3] + part_loads[0][2:] + loads[3:]:
+            item.start()
+        for items in part_loads[1:]:
+            for item in items:
+                item.start()
+        loads[0].wait()
+
+        def begin(rows):
+            branch_ref[rows] = grad_ref[rows].astype(BF16)
+        in_rows(tokens, 64, begin)
+        branch_store = copy(branch_ref, branch_out, store_sem.at[0])
+        branch_store.start()
+        stores = [branch_store]
+        for part in range(parts):
+            columns = slice(part * block, (part + 1) * block)
+            part_loads[part][0].wait()
+            gm_ref[...] = dot_cols(branch_ref[...], wo_ref[columns]).astype(BF16)
+            part_loads[part][1].wait()
+            if part == 0:
+                loads[1].wait()
+                loads[2].wait()
+            first = lanes_of((row_tokens, pair)) < size
+            @pl.loop(0, tokens // row_tokens)
+            def _(row):
+                rows = pl.ds(pl.multiple_of(row * row_tokens, row_tokens), row_tokens)
+                allowed = same_window(lengths_ref, row, row_tokens)
+                cosine, sine = cos_ref[rows], sin_ref[rows]
+                for start in range(0, block // pair, 2):
+                    work = []
+                    for at in range(start, start + 2):
+                        lanes = pl.ds(part * block + at * pair, pair)
+                        query, key, value = (qkv_ref[which, rows, lanes] for which in range(3))
+                        grad_mix = gm_ref[rows, pl.ds(at * pair, pair)]
+                        scaled = query * scale
+                        for head in range(2):
+                            mine = first if head == 0 else jnp.logical_not(first)
+                            work.append((
+                                query, key, grad_mix,
+                                dot_cols(jnp.where(mine, scaled, jnp.zeros_like(scaled)), key),
+                                dot_cols(jnp.where(mine, grad_mix, jnp.zeros_like(grad_mix)), value)))
+                    results = []
+                    for query, key, grad_mix, scores, grad_probs in work:
+                        probs = softmax(scores, allowed)
+                        weighted = probs * grad_probs
+                        grad_scores = (weighted - probs * jnp.sum(weighted, axis=-1, keepdims=True)).astype(BF16)
+                        results.append((query, key, grad_mix, grad_scores, probs.astype(BF16)))
+                    results = [
+                        (dot(grad_scores, key), dot_rows(grad_scores, query), dot_rows(probs, grad_mix))
+                        for query, key, grad_mix, grad_scores, probs in results]
+                    for at in range(2):
+                        lanes = pl.ds(part * block + (start + at) * pair, pair)
+                        grad_query, grad_key, grad_value = (
+                            jnp.where(first, a, b) for a, b in zip(results[2 * at], results[2 * at + 1]))
+                        proj_ref[0, rows, lanes] = unrotated(grad_query * scale, cosine, sine, size).astype(BF16)
+                        proj_ref[1, rows, lanes] = unrotated(grad_key * scale, cosine, sine, size).astype(BF16)
+                        proj_ref[2, rows, lanes] = grad_value.astype(BF16)
+            lanes = pl.ds(part * block, block)
+            stores.append(copy(proj_ref.at[:, :, lanes], proj_out.at[:, :, lanes], store_sem.at[1 + part]))
+            stores[-1].start()
+            added = 0.0
+            for which in range(3):
+                part_loads[part][2 + which].wait()
+                weights = wqkv_ref[:, which * features + part * block:which * features + (part + 1) * block]
+                added = added + dot_cols(proj_ref[which, :, columns], weights)
+            total_ref[...] = added if part == 0 else total_ref[...] + added
+        loads[3].wait()
+        vectors_ref[...] = jnp.zeros_like(vectors_ref)
+
+        def finish(rows):
+            grad = total_ref[rows]
+            through, by_gain = norm_back(grad, x_ref[rows].astype(F32), grad_ref[tokens:tokens + 1])
+            result = grad_ref[rows] + through
+            total_ref[rows] = result
+            input_low_ref[rows] = result.astype(BF16)
+            vectors_ref[0:1] += jnp.sum(by_gain, axis=0, keepdims=True)
+            vectors_ref[1:2] += jnp.sum(grad, axis=0, keepdims=True)
+        in_rows(tokens, 64, finish)
+        for index, (source, target) in enumerate(
+                ((input_low_ref, input_low_out), (total_ref, input_out), (vectors_ref, vectors_out))):
+            stores.append(copy(source, target, store_sem.at[1 + parts + index]))
+            stores[-1].start()
+        for item in stores:
+            item.wait()
+
+    pl.when(act_ref[0] == 1)(work)
+
+
+def places():
+    section, shard, seat = (lax.axis_index(name) for name in ("section", "shard", "group"))
+    stride = 2 - section
+    bit = lax.rem(lax.div(seat, stride), 2)
+    return section, bit, (section, shard, seat + (1 - 2 * bit) * stride), (1 - section, shard, seat)
+
+
+def remote(source, target, sems, index, device):
+    return pltpu.make_async_remote_copy(
+        src_ref=source, dst_ref=target, send_sem=sems.at[0, index], recv_sem=sems.at[1, index], device_id=device,
+        device_id_type=pl.DeviceIdType.MESH)
+
+
+def meet(*devices):
+    barrier = pltpu.get_barrier_semaphore()
+    for device in devices:
+        pl.semaphore_signal(barrier, inc=1, device_id=device, device_id_type=pl.DeviceIdType.MESH)
+    pl.semaphore_wait(barrier, len(devices))
+
+
+def feed_kernel(unit_rows, mid_ref, low_ref, wg_ref, wu_ref, wd_ref, lefts_ref, rows_ref, out_ref, half_ref,
+                arrived_ref, lefts_land, rows_land, total_ref, sems):
+    part = pl.program_id(0)
+    section, bit, beside, above = places()
+    lefts_copy = remote(lefts_ref.at[0:2], lefts_land, sems, 0, beside)
+    rows_copy = remote(rows_ref, rows_land, sems, 0, beside)
+    out_copy = remote(out_ref, arrived_ref, sems, 1, above)
+
+    @pl.when(part == 0)
     def _():
-        @pl.when(part == 0)
-        def _():
-            def begin(rows):
-                branch_ref[rows] = grad_ref[rows].astype(BF16)
-            in_rows(tokens, 64, begin)
-
-        gm_ref[...] = dot_cols(branch_ref[...], wo_ref[...]).astype(BF16)
-        first = lanes_of((row_tokens, pair)) < size
-        for row in range(tokens // row_tokens):
-            rows = pl.ds(row * row_tokens, row_tokens)
-            allowed = same_window(lengths_ref, row, row_tokens)
-            cosine, sine = cos_ref[rows], sin_ref[rows]
-            for start in range(0, block // pair, 2):
-                work = []
-                for at in range(start, start + 2):
-                    lanes = pl.ds(at * pair, pair)
-                    query, key, value = (qkv_ref[which, rows, lanes] for which in range(3))
-                    grad_mix = gm_ref[rows, lanes]
-                    scaled = query * scale
-                    for head in range(2):
-                        mine = first if head == 0 else jnp.logical_not(first)
-                        work.append((
-                            query, key, grad_mix,
-                            dot_cols(jnp.where(mine, scaled, jnp.zeros_like(scaled)), key),
-                            dot_cols(jnp.where(mine, grad_mix, jnp.zeros_like(grad_mix)), value)))
-                results = []
-                for query, key, grad_mix, scores, grad_probs in work:
-                    probs = softmax(scores, allowed)
-                    weighted = probs * grad_probs
-                    grad_scores = (weighted - probs * jnp.sum(weighted, axis=-1, keepdims=True)).astype(BF16)
-                    results.append((query, key, grad_mix, grad_scores, probs.astype(BF16)))
-                results = [
-                    (dot(grad_scores, key), dot_rows(grad_scores, query), dot_rows(probs, grad_mix))
-                    for query, key, grad_mix, grad_scores, probs in results]
-                for at in range(2):
-                    lanes = pl.ds((start + at) * pair, pair)
-                    grad_query, grad_key, grad_value = (
-                        jnp.where(first, a, b) for a, b in zip(results[2 * at], results[2 * at + 1]))
-                    proj_ref[0, rows, lanes] = unrotated(grad_query * scale, cosine, sine, size).astype(BF16)
-                    proj_ref[1, rows, lanes] = unrotated(grad_key * scale, cosine, sine, size).astype(BF16)
-                    proj_ref[2, rows, lanes] = grad_value.astype(BF16)
-
-        added = (
-            dot_cols(proj_ref[0], wq_ref[...])
-            + dot_cols(proj_ref[1], wk_ref[...])
-            + dot_cols(proj_ref[2], wv_ref[...])
-        )
-        total_ref[...] = jnp.where(part == 0, added, total_ref[...] + added)
-
-        @pl.when(part == pl.num_programs(0) - 1)
-        def _():
-            dgain_ref[...] = jnp.zeros_like(dgain_ref)
-            dbias_ref[...] = jnp.zeros_like(dbias_ref)
-
-            def finish(rows):
-                grad = total_ref[rows]
-                through, by_gain = norm_back(grad, x_ref[rows].astype(F32), gain_ref[...])
-                result = grad_ref[rows] + through
-                input_ref[rows] = result
-                input_low_ref[rows] = result.astype(BF16)
-                dgain_ref[...] += jnp.sum(by_gain, axis=0, keepdims=True)
-                dbias_ref[...] += jnp.sum(grad, axis=0, keepdims=True)
-            in_rows(tokens, 64, finish)
-
-
-def feed_kernel(unit_rows, act_ref, mid_ref, low_ref, wg_ref, wu_ref, wd_ref, out_ref, half_ref, total_ref):
-    part = pl.program_id(0)
-
-    @pl.when(act_ref[0] == 1)
+        meet(beside, above)
+        pl.when(section == 0)(lefts_copy.start)
+        pl.when(section == 1)(rows_copy.start)
+
+    @pl.when(section == 0)
     def _():
         @pl.when(part == 0)
         def _():
@@ -240,20 +305,68 @@
         hidden = (gate / (1.0 + jnp.exp(-gate)) * up).astype(BF16)
         for at in range(half_ref.shape[1] // unit_rows):
             rows = [hidden[:, (2 * at + side) * unit_rows:(2 * at + side + 1) * unit_rows] for side in range(2)]
-            half_ref[:, at * unit_rows:(at + 1) * unit_rows] = jnp.where(act_ref[1] == 0, rows[0], rows[1])
+            half_ref[:, at * unit_rows:(at + 1) * unit_rows] = jnp.where(bit == 0, rows[1], rows[0])
         total_ref[...] += dot(hidden, wd_ref[...])
 
-        @pl.when(part == pl.num_programs(0) - 1)
+    @pl.when(part == pl.num_programs(0) - 1)
+    def _():
+        @pl.when(section == 0)
         def _():
             out_ref[...] = total_ref[...].astype(BF16)
-
-
-def feed_both_kernel(act_ref, mid_ref, low_ref, grad_ref, gain_ref, wg_ref, wu_ref, wd_ref, out_ref,
-                     hidden_ref, ggu_ref, grad_mid_ref, dgain_ref, dbias_ref, total_ref):
+            out_copy.start()
+            out_copy.wait_send()
+            lefts_copy.wait()
+
+        @pl.when(section == 1)
+        def _():
+            out_copy.wait_recv()
+            rows_copy.wait()
+
+
+def feed_both_kernel(active, mid_ref, low_ref, grad_ref, gain_ref, gain_a_ref, wg_ref, wu_ref, wd_ref, *refs):
+    sends, refs = refs[:6 if active else 1], refs[6 if active else 1:]
+    out_ref, hidden_ref, ggu_ref, grad_mid_ref, vectors_ref = refs[:5]
+    lands = refs[5:5 + (6 if active else 1)]
+    total_ref, sems = refs[-2:]
     tokens = mid_ref.shape[0]
     part = pl.program_id(0)
-
-    @pl.when(act_ref[0] == 1)
+    section, _, beside, other = places()
+    pieces = 4
+    step = tokens // pieces
+    if active:
+        lefts_ref, qkv_ref, wqkv_ref, wo_ref, lefts_first, hidden_first = sends
+        lefts_land, qkv_land, wqkv_land, wo_land, hidden_land, grad_land = lands
+        working = [
+            remote(lefts_ref, lefts_land, sems, 0, beside), remote(qkv_ref, qkv_land, sems, 1, other),
+            remote(wqkv_ref, wqkv_land, sems, 2, other), remote(wo_ref, wo_land, sems, 3, other)]
+        waiting = [
+            remote(lefts_first.at[2], lefts_land.at[2], sems, 4, beside),
+            remote(hidden_first, hidden_land, sems, 5, beside)]
+
+        def grad_copy(piece):
+            rows = pl.ds(piece * step, step + (8 if piece == pieces - 1 else 0))
+            return remote(grad_mid_ref.at[rows], grad_land.at[rows], sems, 6 + piece, other)
+    else:
+        working = [remote(sends[0], lands[0], sems, 0, beside)]
+
+    @pl.when(part == 0)
+    def _():
+        if active:
+            meet(beside, other)
+
+            @pl.when(section != active)
+            def _():
+                for copy in waiting:
+                    copy.start()
+
+        @pl.when(section == active)
+        def _():
+            if not active:
+                meet(beside)
+            for copy in working:
+                copy.start()
+
+    @pl.when(section == active)
     def _():
         @pl.when(part == 0)
         def _():
@@ -272,18 +385,40 @@
         added = dot_cols(ggu_ref[0], wg_ref[...]) + dot_cols(ggu_ref[1], wu_ref[...])
         total_ref[...] = jnp.where(part == 0, added, total_ref[...] + added)
 
-        @pl.when(part == pl.num_programs(0) - 1)
+    @pl.when(part == pl.num_programs(0) - 1)
+    def _():
+        @pl.when(section == active)
         def _():
-            dgain_ref[...] = jnp.zeros_like(dgain_ref)
-            dbias_ref[...] = jnp.zeros_like(dbias_ref)
+            vectors_ref[...] = jnp.zeros_like(vectors_ref)
+            grad_mid_ref[pl.ds(tokens, 8)] = jnp.broadcast_to(gain_a_ref[...], (8, gain_a_ref.shape[1]))
 
             def finish(rows):
                 grad = total_ref[rows]
                 through, by_gain = norm_back(grad, mid_ref[rows], gain_ref[...])
                 grad_mid_ref[rows] = grad_ref[rows].astype(F32) + through
-                dgain_ref[...] += jnp.sum(by_gain, axis=0, keepdims=True)
-                dbias_ref[...] += jnp.sum(grad, axis=0, keepdims=True)
-            in_rows(tokens, 64, finish)
+                vectors_ref[2:3] += jnp.sum(by_gain, axis=0, keepdims=True)
+                vectors_ref[3:4] += jnp.sum(grad, axis=0, keepdims=True)
+            for piece in range(pieces):
+                for at in range(2):
+                    finish(pl.ds(piece * step + at * (step // 2), step // 2))
+                if active:
+                    grad_copy(piece).start()
+            if active:
+                for piece in range(pieces):
+                    grad_copy(piece).wait_send()
+                for copy in working[1:]:
+                    copy.wait_send()
+            working[0].wait()
+
+        if active:
+            @pl.when(section != active)
+            def _():
+                for piece in range(pieces):
+                    grad_copy(piece).wait_recv()
+                for copy in working[1:]:
+                    copy.wait_recv()
+                for copy in waiting:
+                    copy.wait()
 
 
 def whole(shape):
@@ -291,15 +426,15 @@
 
 
 def column(rows, wide, offset=0):
-    return pl.BlockSpec((rows, wide), lambda part, act, *_: (0, (part + offset) * act[0]))
+    return pl.BlockSpec((rows, wide), lambda part, *act: (0, (part + offset) * (act[0][0] if act else 1)))
 
 
 def stacked(count, rows, wide):
-    return pl.BlockSpec((count, rows, wide), lambda part, act, *_: (0, 0, part * act[0]))
+    return pl.BlockSpec((count, rows, wide), lambda part, *act: (0, 0, part * (act[0][0] if act else 1)))
 
 
 def lower(rows, wide):
-    return pl.BlockSpec((rows, wide), lambda part, act, *_: (part * act[0], 0))
+    return pl.BlockSpec((rows, wide), lambda part, *act: (part * (act[0][0] if act else 1), 0))
 
 
 def local_call(kernel, name, grid, scalars, args, in_specs, outs, out_specs, scratch, flops, limit=56):
@@ -333,59 +468,87 @@
         [pltpu.VMEM((tokens, wide), BF16)], 8 * tokens * features ** 2)
 
 
-def attention_back(active, lengths, grad_mid, x, gain, qkv, w_qkv, w_out, cosine, sine, parts=2):
+def attention_back(active, lengths, grad_mid, x, qkv, w_qkv, w_out, cosine, sine, parts=2):
     tokens, features = x.shape
     row_tokens = tokens // lengths.shape[0]
     size = features // HEADS
-    wide = features // parts
-    vector = jax.ShapeDtypeStruct((1, features), F32)
-    return local_call(
-        functools.partial(attention_back_kernel, size, row_tokens), "attention_back", parts, (active, lengths),
-        (grad_mid, x, gain, qkv, w_qkv, w_qkv, w_qkv, w_out, cosine, sine),
-        [whole((tokens, features)), whole((tokens, features)), whole((1, features)), stacked(3, tokens, wide),
-         column(features, wide), column(features, wide, parts), column(features, wide, 2 * parts),
-         lower(wide, features), whole(cosine.shape), whole(sine.shape)],
-        (jax.ShapeDtypeStruct((tokens, features), BF16), jax.ShapeDtypeStruct((3, tokens, features), BF16),
-         jax.ShapeDtypeStruct((tokens, features), F32), jax.ShapeDtypeStruct((tokens, features), BF16),
-         vector, vector),
-        (whole((tokens, features)), stacked(3, tokens, wide), whole((tokens, features)), whole((tokens, features)),
-         whole((1, features)), whole((1, features))),
-        [pltpu.VMEM((tokens, wide), BF16), pltpu.VMEM((tokens, features), F32)], 20 * tokens * features ** 2)
+    low = jax.ShapeDtypeStruct((tokens, features), BF16)
+    stack = jax.ShapeDtypeStruct((3, tokens, features), BF16)
+    full = jax.ShapeDtypeStruct((tokens, features), F32)
+    vectors = jax.ShapeDtypeStruct((8, features), F32)
+    outs = (low, stack, full, low, vectors)
+    hbm, smem, dma = pl.BlockSpec(memory_space=pl.ANY), pl.BlockSpec(memory_space=pltpu.SMEM), pltpu.SemaphoreType.DMA
+    held = [grad_mid, x, qkv, w_qkv, w_out, cosine, sine, low, stack, low, vectors]
+    return pl.pallas_call(
+        functools.partial(attention_back_kernel, size, row_tokens, parts),
+        out_shape=outs,
+        in_specs=[smem, smem] + [hbm] * 7,
+        out_specs=[hbm] * len(outs),
+        scratch_shapes=[pltpu.VMEM(item.shape, item.dtype) for item in held] + [
+            pltpu.VMEM((tokens, features // parts), BF16), pltpu.VMEM((tokens, features), F32),
+            dma((4,)), dma((parts, 5)), dma((4 + parts,))],
+        name="attention_back",
+        cost_estimate=pl.CostEstimate(
+            flops=20 * tokens * features ** 2, bytes_accessed=40 * 2 ** 20, transcendentals=0),
+        compiler_params=pltpu.CompilerParams(vmem_limit_bytes=56 * 1024 * 1024),
+    )(active, lengths, grad_mid, x, qkv, w_qkv, w_out, cosine, sine)
 
 
 def third(tokens, features):
     return pl.BlockSpec((1, tokens, features), lambda part, *_: (2, 0, 0))
 
 
-def feed(active, mid, lefts, w_gate_up, w_down, unit_rows, parts=8):
+def meeting_call(kernel, name, parts, args, in_specs, outs, out_specs, scratch, flops, collective_id):
+    return pl.pallas_call(
+        kernel,
+        grid=(parts,),
+        in_specs=in_specs,
+        out_specs=out_specs,
+        out_shape=outs,
+        scratch_shapes=scratch,
+        name=name,
+        cost_estimate=pl.CostEstimate(flops=flops, bytes_accessed=40 * 2 ** 20, transcendentals=0),
+        compiler_params=pltpu.CompilerParams(
+            dimension_semantics=("arbitrary",), vmem_limit_bytes=56 * 1024 * 1024, collective_id=collective_id,
+            has_side_effects=True),
+    )(*args)
+
+
+def feed(mid, lefts, rows, w_gate_up, w_down, unit_rows, collective_id, parts=8):
     tokens, features = mid.shape
     wide = w_down.shape[0] // parts
-    return local_call(
-        functools.partial(feed_kernel, unit_rows), "feed", parts, (active,),
-        (mid, lefts, w_gate_up, w_gate_up, w_down),
+    hbm = pl.BlockSpec(memory_space=pl.ANY)
+    low = jax.ShapeDtypeStruct((tokens, features), BF16)
+    return meeting_call(
+        functools.partial(feed_kernel, unit_rows), "feed", parts,
+        (mid, lefts, w_gate_up, w_gate_up, w_down, lefts, rows),
         [whole((tokens, features)), third(tokens, features), column(features, wide), column(features, wide, parts),
-         lower(wide, features)],
-        (jax.ShapeDtypeStruct((tokens, features), BF16), jax.ShapeDtypeStruct((tokens, w_down.shape[0] // 2), BF16)),
-        (whole((tokens, features)), column(tokens, wide // 2)),
-        [pltpu.VMEM((tokens, features), F32)], 6 * tokens * features * w_down.shape[0])
-
-
-def feed_both(active, mid, lefts, grad, gain, w_gate_up, w_down, parts=8):
+         lower(wide, features), hbm, hbm],
+        (low, jax.ShapeDtypeStruct((tokens, w_down.shape[0] // 2), BF16), low,
+         jax.ShapeDtypeStruct((2, tokens, features), BF16), low),
+        (whole((tokens, features)), column(tokens, wide // 2), hbm, hbm, hbm),
+        [pltpu.VMEM((tokens, features), F32), pltpu.SemaphoreType.DMA((2, 2))],
+        6 * tokens * features * w_down.shape[0], collective_id)
+
+
+def feed_both(active, mid, lefts, grad, gain, gain_a, w_gate_up, w_down, sends, lands, collective_id, parts=8):
     tokens, features = mid.shape
     hidden = w_down.shape[0]
     wide = hidden // parts
-    vector = jax.ShapeDtypeStruct((1, features), F32)
-    return local_call(
-        feed_both_kernel, "feed_both", parts, (active,),
-        (mid, lefts, grad, gain, w_gate_up, w_gate_up, w_down),
+    hbm = pl.BlockSpec(memory_space=pl.ANY)
+    return meeting_call(
+        functools.partial(feed_both_kernel, active), "feed_both", parts,
+        (mid, lefts, grad, gain, gain_a, w_gate_up, w_gate_up, w_down, *sends),
         [whole((tokens, features)), third(tokens, features), whole((tokens, features)), whole((1, features)),
-         column(features, wide), column(features, wide, parts), lower(wide, features)],
+         whole((1, features)), column(features, wide), column(features, wide, parts), lower(wide, features)]
+        + [hbm] * len(sends),
         (jax.ShapeDtypeStruct((tokens, features), F32), jax.ShapeDtypeStruct((tokens, hidden), BF16),
-         jax.ShapeDtypeStruct((2, tokens, hidden), BF16), jax.ShapeDtypeStruct((tokens, features), F32),
-         vector, vector),
+         jax.ShapeDtypeStruct((2, tokens, hidden), BF16), jax.ShapeDtypeStruct((tokens + 8, features), F32),
+         jax.ShapeDtypeStruct((8, features), F32), *lands),
         (whole((tokens, features)), column(tokens, wide), stacked(2, tokens, wide),
-         whole((tokens, features)), whole((1, features)), whole((1, features))),
-        [pltpu.VMEM((tokens, features), F32)], 12 * tokens * features * hidden)
+         whole((tokens + 8, features)), whole((8, features))) + (hbm,) * len(lands),
+        [pltpu.VMEM((tokens, features), F32), pltpu.SemaphoreType.DMA((2, 10))],
+        12 * tokens * features * hidden, collective_id)
 
 
 def tables(lengths, row_tokens, size):
@@ -403,7 +566,7 @@
 
 
 def exchange_kernel(cfg, *refs):
-    shards, bits, seats, unit_rows, width, section, aliased, late, layers, lag = cfg
+    shards, bits, seats, unit_rows, width, section, aliased, late, layers, other_layers, lag, supply, order = cfg
     arrays = len(seats)
     refs = list(refs)
 
@@ -415,13 +578,17 @@
     lefts, rights = take(arrays), take(arrays)
     left_others, right_others = take(arrays - (1 if late else 0)), take(1)
     lefts = [ref if at is None else ref.at[at] for ref, at in zip(lefts, layers)]
-    left_others = [ref if at is None else ref.at[at] for ref, at in zip(left_others, layers)]
+    left_others = [ref if at is None else ref.at[at] for ref, at in zip(left_others, other_layers)]
     (vector,) = take(1)
+    vector_given = take(1) if supply else []
     take(arrays + 1 if aliased else 0)
     outs, (vector_out,) = take(arrays), take(1)
     if late:
         left_others = left_others + take(1)
-    (vector_land, vector_sum, vector_send, vector_recv, vector_store, left, right, left_sem, right_sem, other_sem,
+    given = [rights[index] for index in supply]
+    for index in supply:
+        rights[index] = take(1)[0]
+    (given_send, given_recv, vector_far, vector_full, vector_land, vector_sum, vector_send, vector_recv, vector_store, left, right, left_sem, right_sem, other_sem,
      right_send, right_recv, late_send, late_recv, mine, side_land, side, side_send, side_recv, chain_a, chain_b,
      chain_send, chain_recv, rest_send, rest_land, rest_keep, rest_ssem, rest_rsem, piece, store_sem, gather_send,
      gather_recv) = refs
@@ -444,10 +611,10 @@
     part = vector_out.shape[1]
 
     def bit_of(index):
-        return lax.rem(lax.div(seat, 1 << index), 2)
+        return lax.rem(lax.div(seat, 1 << order[index]), 2)
 
     def across(index):
-        return (sec, here, seat + (1 - 2 * bit_of(index)) * (1 << index))
+        return (sec, here, seat + (1 - 2 * bit_of(index)) * (1 << order[index]))
 
     above = (sec, jnp.minimum(here + 1, shards - 1), seat)
     below = (sec, jnp.maximum(here - 1, 0), seat)
@@ -467,11 +634,18 @@
         return index, (sec, lax.div(index, group), lax.rem(index, group))
 
     def vector_copy(index, device):
-        return remote(vector.at[:, aligned(device[1] * part, part)], vector_land.at[me], vector_send.at[index],
+        return remote(vector_full.at[:, aligned(device[1] * part, part)], vector_land.at[me], vector_send.at[index],
                       vector_recv.at[me], device)
 
     def vector_finish():
-        vector_sum[...] = vector[:, aligned(here * part, part)]
+        vector_full[...] = vector[...]
+        if supply:
+            vector_full[...] += vector_far[...]
+
+        @pl.loop(1, peers)
+        def _(step):
+            vector_copy(*peer(step)).start()
+        vector_sum[...] = vector_full[:, aligned(here * part, part)]
 
         @pl.loop(1, peers)
         def _(step):
@@ -787,8 +961,30 @@
         if step + 1 < bits:
             spread(path, step + 1, chunk)
 
+    def given_copies():
+        device = (section, here, seat)
+        targets = [rights[index] for index in supply] + [vector_far]
+        return [remote(source, target, given_send.at[index], given_recv.at[index], device)
+                for index, (source, target) in enumerate(zip(given + vector_given, targets))]
+
+    def hand_over():
+        pl.semaphore_wait(pltpu.get_barrier_semaphore(), 1)
+        for copy in given_copies():
+            copy.start()
+        for copy in given_copies():
+            copy.wait_send()
+
+    def take_over():
+        for copy in given_copies():
+            copy.wait_recv()
+
+    def unit_of(index):
+        return index if index < lead else lead + (index - lead) // pace * (pace + 1) + 1 + (index - lead) % pace
+
     def work():
         barrier = pltpu.get_barrier_semaphore()
+        if supply:
+            pl.semaphore_signal(barrier, inc=1, device_id=(1 - section, here, seat), device_id_type=MESH)
 
         @pl.loop(1, peers)
         def _(step):
@@ -798,10 +994,6 @@
             send_right(chunk)
         loads(0, lambda copy: copy.start())
 
-        @pl.loop(1, peers)
-        def _(step):
-            vector_copy(*peer(step)).start()
-
         for path in range(2):
             for way in range(2):
                 @pl.loop(0, shards)
@@ -814,6 +1006,8 @@
 
         @pl.loop(0, units + lag * (line + others + bits) + 2)
         def _(turn):
+            if supply:
+                on(turn == unit_of(sum(seat[0] for seat in seats[:supply[0]])) - lag, take_over)
             on(turn + lag < units, lambda: send_right(turn + lag))
             if late:
                 late_turn(turn)
@@ -847,16 +1041,20 @@
         work()
     else:
         pl.when(sec == section)(work)
-
-
-def exchange(pairs, vector, shards, group, section, collective_id, unit_width, previous=None, lag=2, unit_rows_max=256,
+        if supply:
+            pl.when(sec != section)(hand_over)
+
+
+def exchange(pairs, vector, shards, group, section, collective_id, unit_width, previous=None, lag=2, supply=(), vector_given=None, first_bit=0, unit_rows_max=256,
              name="exchange"):
     bits = group.bit_length() - 1
     arrays = len(pairs)
+    order = (first_bit,) + tuple(bit for bit in range(bits) if bit != first_bit)
     lefts, rights = [pair[0][0] for pair in pairs], [pair[1] for pair in pairs]
     layers = tuple(pair[0][1] for pair in pairs)
-    left_others = [pair[2] for pair in pairs]
-    late = left_others[-1] is None
+    left_others = [pair[2] and pair[2][0] for pair in pairs]
+    other_layers = tuple(pair[2] and pair[2][1] for pair in pairs)
+    late = pairs[-1][2] is None
     if late:
         left_others = left_others[:-1]
     tokens = lefts[0].shape[-2]
@@ -877,6 +1075,8 @@
     peers, lanes = shards * group, vector.shape[1] // shards
     dma = pltpu.SemaphoreType.DMA
     scratch = [
+        dma((len(supply) + 1,)), dma((len(supply) + 1,)),
+        pltpu.VMEM(vector.shape, F32), pltpu.VMEM(vector.shape, F32),
         pltpu.VMEM((peers, vector.shape[0], lanes), F32),
         pltpu.VMEM((vector.shape[0], lanes), F32),
         dma((peers,)), dma((peers,)), dma,
@@ -900,15 +1100,17 @@
         dma((2, slots)),
         dma((2, bits, 2, slots)), dma((2, bits, 2, slots)),
     ]
-    cfg = (shards, bits, tuple(seats), unit_rows, width, section, previous is not None, late, layers, lag)
-    operands = lefts + rights + left_others + [pairs[-1][3], vector] + list(previous or [])
+    cfg = (shards, bits, tuple(seats), unit_rows, width, section, previous is not None, late, layers, other_layers, lag, supply, order)
+    vectors = [vector] + ([vector_given] if supply else [])
+    operands = lefts + rights + left_others + [pairs[-1][3]] + vectors + list(previous or [])
     first = len(operands) - len(previous or [])
     results = [jax.ShapeDtypeStruct((r, g.shape[0] * g.shape[2]), BF16) for r, g in zip(rows_of, rights)]
     results.append(jax.ShapeDtypeStruct((vector.shape[0], lanes), F32))
     if late:
         results.append(jax.ShapeDtypeStruct((tokens, lefts[-1].shape[-1] // 2), BF16))
+    results.extend(jax.ShapeDtypeStruct(rights[index].shape, BF16) for index in supply)
     hbm, vmem = pl.BlockSpec(memory_space=pl.ANY), pl.BlockSpec(memory_space=pltpu.VMEM)
-    in_specs = [vmem if index == first - 1 else hbm for index in range(len(operands))]
+    in_specs = [vmem if first - len(vectors) <= index < first else hbm for index in range(len(operands))]
     return pl.pallas_call(
         functools.partial(exchange_kernel, cfg),
         out_shape=results,
@@ -949,49 +1151,50 @@
     rows = ends_in[0]
     weight_qkv, weight_out, weight_gu, weight_down = w_qkv[0], w_out[0], w_gate_up[0], w_down[0]
     cosine, sine = tables(lengths, tokens // lengths.shape[0], size)
-    nothing = jnp.zeros((4, features), F32)
     unit_rows = min(256, features // shards)
-    partner_bit = (1 - lax.axis_index("group") % 2).astype(jnp.int32).reshape(1)
-
-    def beside(which, array):
-        pairs = [(which * group + index, which * group + (index ^ 1)) for index in range(group)]
-        return lax.ppermute(array, ("section", "group"), pairs)
+    low = jax.ShapeDtypeStruct((tokens, features), BF16)
+    stack = jax.ShapeDtypeStruct((3, tokens, features), BF16)
+
+    def like(array):
+        return jax.ShapeDtypeStruct(array.shape, array.dtype)
 
     def attend(active, values):
         return attention(active, lengths, values, norm_gain_a, norm_bias_a, norm_gain_f, norm_bias_f, weight_qkv,
                          weight_out, cosine, sine)
 
-    def back(active, middle, lefts, qkv, values, grad):
-        result, hidden, grad_gu, grad_middle, gain_f, bias_f = feed_both(
-            active, middle, lefts, grad, norm_gain_f, weight_gu, weight_down)
-        branch, grad_qkv, grad_in, grad_in_low, gain_a, bias_a = attention_back(
-            active, lengths, grad_middle, values, norm_gain_a, qkv, weight_qkv, weight_out, cosine, sine)
-        vectors = jnp.concatenate([gain_a, bias_a, gain_f, bias_f, nothing], axis=0)
-        return result, grad_in, grad_in_low, hidden, (grad_gu, branch[None], grad_qkv, grad[None]), vectors
+    def feed_back(active, middle, lefts, grad, sends, lands, collective_id):
+        return feed_both(active, middle, lefts, grad, norm_gain_f, norm_gain_a, weight_gu, weight_down, sends, lands,
+                         collective_id)
+
+    def attend_back(grad_middle, values, qkv, weight_qkv, weight_out):
+        return attention_back(first, lengths, grad_middle, values, qkv, weight_qkv, weight_out, cosine, sine)
 
     def sum_all(which, lefts, lefts_beside, hidden, hidden_beside, rights, right_beside, vectors, **more):
-        pairs = [((lefts, at), right, lefts_beside) for at, right in zip((2, 1, 0), rights)]
+        pairs = [((lefts, at), right, other) for at, right, other in zip((2, 1, 0), rights, lefts_beside)]
         pairs.append(((hidden, None), rights[3], hidden_beside, right_beside))
-        return exchange(pairs, vectors, shards, group, which, which + 1, UNIT_WIDTH * features // 1024, **more)
-
-    rows_beside = beside(1, rows)
+        return exchange(pairs, vectors, shards, group, which, which + 1, UNIT_WIDTH * features // 1024,
+                        first_bit=1 - which, **more)
+
     middle_0, lefts_0, qkv_0 = attend(first, rows)
-    passed, hidden_half_0 = feed(
-        jnp.concatenate([first, partner_bit]), middle_0, lefts_0, weight_gu, weight_down, unit_rows)
-    arrived = lax.ppermute(passed, "section", [(0, 1)])
-    lefts_beside_0, hidden_beside_0 = beside(0, lefts_0), beside(0, hidden_half_0)
+    passed, hidden_half_0, arrived, early_beside, rows_beside = feed(
+        middle_0, lefts_0, rows, weight_gu, weight_down, unit_rows, 3)
     middle_1, lefts_1, qkv_1 = attend(second, arrived)
-    lefts_beside_1 = beside(1, lefts_1)
-    result, _, returned, hidden_1, rights_1, vectors_1 = back(second, middle_1, lefts_1, qkv_1, arrived, rows)
-    returned = lax.ppermute(returned, "section", [(1, 0)])
-    sums = sum_all(1, lefts_1, lefts_beside_1, hidden_1, None, rights_1, rows_beside, vectors_1,
-                   name="exchange_second", lag=1)
-    returned, _, lefts_beside_0, hidden_beside_0 = lax.optimization_barrier(
-        (returned, sums[4], lefts_beside_0, hidden_beside_0))
-    returned_beside = beside(0, returned)
-    _, grad_in, _, hidden_0, rights_0, vectors_0 = back(first, middle_0, lefts_0, qkv_0, rows, returned)
-    sums = sum_all(0, lefts_0, lefts_beside_0, hidden_0, hidden_beside_0, rights_0, returned_beside, vectors_0,
-                   previous=sums, name="exchange_first", lag=2)
+    result, hidden_1, grad_gu_1, _, vectors_1, lefts_beside, qkv_there, qkv_weight, out_weight, hidden_beside, \
+        grad_middle = feed_back(
+            1, middle_1, lefts_1, rows,
+            (lefts_1, qkv_1, weight_qkv, weight_out, lefts_0, hidden_half_0),
+            (stack, stack, like(weight_qkv), like(weight_out), like(hidden_half_0), jax.ShapeDtypeStruct((tokens + 8, features), F32)), 4)
+    branch, grad_qkv, _, returned, vectors_far = attend_back(grad_middle, passed, qkv_there, qkv_weight, out_weight)
+    sums = sum_all(1, lefts_1, [(lefts_beside, at) for at in (2, 1, 0)], hidden_1, None,
+                   (grad_gu_1, branch[None], grad_qkv, rows[None]), rows_beside, vectors_1, vector_given=vectors_far,
+                   lag=1, supply=(1, 2), name="exchange_second")
+    returned, _ = lax.optimization_barrier((returned, sums[4]))
+    _, hidden_0, grad_gu_0, grad_middle, vectors_0, returned_beside = feed_back(
+        0, middle_0, lefts_0, returned, (returned,), (low,), 5)
+    branch, grad_qkv, grad_in, _, vectors_near = attend_back(grad_middle, rows, qkv_0, weight_qkv, weight_out)
+    sums = sum_all(0, lefts_0, [(lefts_beside, 2), (early_beside, 1), (early_beside, 0)], hidden_0,
+                   (hidden_beside, None), (grad_gu_0, branch[None], grad_qkv, returned[None]), returned_beside,
+                   vectors_0 + vectors_near, previous=sums, lag=2, name="exchange_first")
     ends_out = jnp.where(is_first, grad_in, result)[None]
     grad_gate_up, grad_out, grad_qkv, grad_down = (item.astype(F32)[None] for item in sums[:4])
     vectors = sums[4]

time: 443 us -> 411 us (0.928); the launches traced: 442 us -> 403 us
  waiting for transfers between devices: 47.9 us -> 0 us
  Pallas kernels: 352 us -> 379 us
  starting transfers between devices: 16.6 us -> 0 us
    pallas_call x0 -> x5, Pallas kernels: none -> 173 us  [the longest x3 120 us: meeting_call(): pl.pallas_call(kernel, grid=(parts,), in_specs=in_specs, out_specs=out_sp...]
    pallas_call x7 -> x2, Pallas kernels: 124 us -> 26.6 us  [local_call(): pl.pallas_call(kernel, grid_spec=pltpu.PrefetchScalarGridSpec(num_scalar_...]
    pallas_call x2, Pallas kernels: 228 us -> 179 us  [exchange(): pl.pallas_call(functools.partial(exchange_kernel, cfg), out_shape=results...]
    ppermute x7 -> x0, waiting for transfers between devices: 47.9 us -> none  [the longest x1 45.9 us: body(): returned = lax.ppermute(returned, 'section', [(1, 0)])]
    ppermute x7 -> x0, starting transfers between devices: 16.6 us -> none  [the longest x5 13.9 us: beside(): return lax.ppermute(array, ('section', 'group'), pairs)]
  transfers between devices with their start and end apart: 7 -> 0, of which waited for: 2 -> 0; matrix products, arithmetic and copies ran while one was open for 1% -> 0% of each run, Pallas kernels for 14% -> 0%
where the time goes in v7:
time: 411 us; the launch traced here: 403 us
  Pallas kernels  379 us (92%)
  other arithmetic  20.5 us (5%)
    pallas_call x2, Pallas kernels, exchange(): pl.pallas_call(functools.partial(exchange_kernel, cfg), out_shape=results...  179 us
    pallas_call x3, Pallas kernels, meeting_call(): pl.pallas_call(kernel, grid=(parts,), in_specs=in_specs, out_specs=out_sp...  120 us
    pallas_call x2, Pallas kernels, attention_back(): pl.pallas_call(functools.partial(attention_back_kernel, size, row_tokens,...  53.2 us
    pallas_call x2, Pallas kernels, local_call(): pl.pallas_call(kernel, grid_spec=pltpu.PrefetchScalarGridSpec(num_scalar_...  26.6 us
    broadcast_in_dim x4, other arithmetic, body(): item.astype(F32)[None]  12.7 us

profile of v7, /device:TPU:0, one launch (start us, length us, event | category | flops | bytes accessed | tf_op | source)
XLA Modules:
  0.0 403.4 jit_solution(11308425283296734091)
XLA Ops:
  0.7 1.0 fusion.7
  1.7 0.1 broadcast_bitcast_fusion.4
  1.8 0.1 broadcast_bitcast_fusion.2
  1.9 0.1 broadcast_bitcast_fusion
  2.0 1.9 multiply_sine_fusion
  3.8 19.8 %attention.2 = (f32[512,1024]{1,0:T(8,128)}, bf16[3,512,1024]{2,1,0:T(8,128)(2,1)}, bf16[3,512,1024]{2,1,0:T(8,128)(2,1)}) custom-call(s32[1]{0:T(128)} %bitcast.act_ref, s32[2,3]{1,0:T(2,128)} %lengths_ref.7, bf16[512,1024]{1,0:T(8,128)(2,1)} %bitcast.63, f32[1,1024]{1,0:T(1,128)} %gain_a_ref.3, f32[1,1024]{1,0:T(1,128)} %bias_ref.3, f32[1,1024]{1,0:T(1,128)} %gain_ref.7, ...), custom_call_target="tpu_custom_call" | custom-call | flops 4294967296 | bytes 41943040 | tf_op jit(solution)/shard_map/attention/pallas_call | solution.py:441
  23.7 31.6 %feed.1 = (bf16[512,1024]{1,0:T(8,128)(2,1)}, bf16[512,2048]{1,0:T(8,128)(2,1)}, bf16[512,1024]{1,0:T(8,128)(2,1)}, bf16[2,512,1024]{2,1,0:T(8,128)(2,1)}, bf16[512,1024]{1,0:T(8,128)(2,1)}) custom-call(f32[512,1024]{1,0:T(8,128)} %get-tuple-element.54.mid_ref, bf16[3,512,1024]{2,1,0:T(8,128)(2,1)} %get-tuple-element.55.low_ref.lefts_ref.refs_4_.refs_0_.refs_1_.refs_2_, ...), custom_call_target="tpu_custom_call" | custom-call | flops 12884901888 | bytes 41943040 | tf_op jit(solution)/shard_map/feed/pallas_call | solution.py:502
  55.3 6.7 %attention.3 = (f32[512,1024]{1,0:T(8,128)}, bf16[3,512,1024]{2,1,0:T(8,128)(2,1)}, bf16[3,512,1024]{2,1,0:T(8,128)(2,1)}) custom-call(s32[1]{0:T(128)} %bitcast.4.act_ref, s32[2,3]{1,0:T(2,128)} %lengths_ref.7, bf16[512,1024]{1,0:T(8,128)(2,1)} %get-tuple-element.56.x_ref, f32[1,1024]{1,0:T(1,128)} %gain_a_ref.3, f32[1,1024]{1,0:T(1,128)} %bias_ref.3, ...), custom_call_target="tpu_custom_call" | custom-call | flops 4294967296 | bytes 41943040 | tf_op jit(solution)/shard_map/attention/pallas_call | solution.py:441
  62.1 49.5 %feed_both.2 = (f32[512,1024]{1,0:T(8,128)}, bf16[512,4096]{1,0:T(8,128)(2,1)}, bf16[2,512,4096]{2,1,0:T(8,128)(2,1)}, f32[520,1024]{1,0:T(8,128)}, f32[8,1024]{...) custom-call(f32[512,1024]{1,0:T(8,128)} %get-tuple-element.57.mid_re, ...), custom_call_target="tpu_custom_call" | custom-call | flops 25769803776 | bytes 41943040 | tf_op jit(solution)/shard_map/feed_both/pallas_call | solution.py:502
  111.5 26.5 %attention_back.2 = (bf16[512,1024]{1,0:T(8,128)(2,1)}, bf16[3,512,1024]{2,1,0:T(8,128)(2,1)}, f32[512,1024]{1,0:T(8,128)}, bf16[512,1024]{1,0:T(8,128)(2,1)}, f32[8,1024]{1,0:T(8,128)}) custom-call(s32[1]{0:T(128)} %bitcast.act_ref, s32[2,3]{1,0:T(2,128)} %lengths_ref.7, f32[520,1024]{1,0:T(8,128)} %get-tuple-element.61.grad_in, ...), custom_call_target="tpu_custom_call" | custom-call | flops 10737418240 | bytes 41943040 | tf_op jit(solution)/shard_map/attention_back/pallas_call | solution.py:482
  138.0 11.6 %exchange_second.1 = (bf16[256,8192]{1,0:T(8,128)(2,1)}, bf16[256,1024]{1,0:T(8,128)(2,1)}, bf16[256,3072]{1,0:T(8,128)(2,1)}, bf16[1024,1024]{1,0:T(8,128)(2,1)...) custom-call(bf16[3,512,1024]{2,1,0:T(8,128)(2,1)} %get-tuple-element, ...), custom_call_target="tpu_custom_call" | custom-call | flops 17179869184 | bytes 104857600 | tf_op jit(solution)/shard_map/exchange_second/pallas_call | solution.py:1114
  149.7 39.0 %feed_both.3 = (f32[512,1024]{1,0:T(8,128)}, bf16[512,4096]{1,0:T(8,128)(2,1)}, bf16[2,512,4096]{2,1,0:T(8,128)(2,1)}, f32[520,1024]{1,0:T(8,128)}, f32[8,1024]{1,0:T(8,128)}, /*index=5*/bf16[512,1024]{1,0:T(8,128)(2,1)}) custom-call(f32[512,1024]{1,0:T(8,128)} %get-tuple-element.54.mid_ref, ...), custom_call_target="tpu_custom_call" | custom-call | flops 25769803776 | bytes 41943040 | tf_op jit(solution)/shard_map/feed_both/pallas_call | solution.py:502
  188.7 0.0 copy-start.3
  188.7 0.0 copy-start.1
  188.7 26.7 %attention_back.3 = (bf16[512,1024]{1,0:T(8,128)(2,1)}, bf16[3,512,1024]{2,1,0:T(8,128)(2,1)}, f32[512,1024]{1,0:T(8,128)}, bf16[512,1024]{1,0:T(8,128)(2,1)}, f32[8,1024]{1,0:T(8,128)}) custom-call(s32[1]{0:T(128)} %bitcast.act_ref, s32[2,3]{1,0:T(2,128)} %lengths_ref.7, f32[520,1024]{1,0:T(8,128)} %get-tuple-element.77.grad_in, ...), custom_call_target="tpu_custom_call" | custom-call | flops 10737418240 | bytes 41943040 | tf_op jit(solution)/shard_map/attention_back/pallas_call | solution.py:482
  215.4 0.0 copy-done.3
  215.4 1.4 add.38.refs_13_
  216.8 0.0 copy-done.1
  216.8 3.5 select_bitcast_fusion
  220.2 167.7 %exchange_first.1 = (bf16[256,8192]{1,0:T(8,128)(2,1)}, bf16[256,1024]{1,0:T(8,128)(2,1)}, bf16[256,3072]{1,0:T(8,128)(2,1)}, bf16[1024,1024]{1,0:T(8,128)(2,1)}, f32[8,256]{1,0:T(8,128)}) custom-call(bf16[3,512,1024]{2,1,0:T(8,128)(2,1)} %get-tuple-element.55.low_ref.lefts_ref.refs_4_, ...), custom_call_target="tpu_custom_call", output_to_operand_aliasing={{0}: (14, {}), {1}: (15, {}), {2}: (16, {}), {3}: (17, {}),... | custom-call | flops 17179869184 | bytes 104857600 | tf_op jit(solution)/shard_map/exchange_first/pallas_call | solution.py:1114
  387.9 1.4 fusion.8
  389.4 0.0 copy-start.2
  389.4 2.3 bitcast_convert_fusion.3
  391.6 3.4 bitcast_convert_fusion.2
  395.1 0.0 copy-done.2
  395.1 0.0 copy-start
  395.1 2.6 bitcast_convert_fusion.1
  397.7 1.1 copy-done
  398.8 4.4 %bitcast_convert_fusion = f32[1,256,8192]{2,1,0:T(8,128)} fusion(bf16[256,8192]{1,0:T(8,128)(2,1)S(1)} %copy-done), kind=kLoop, calls=%fused_computation | loop fusion | flops 2097152 | bytes 12582912 | tf_op jit(solution)/shard_map/broadcast_in_dim | solution.py:1199
  (9 shorter events, 0.0 us)
Async XLA Ops:
  188.7 26.7 %copy-start.3 = (f32[8,1024]{1,0:T(8,128)S(1)}, f32[8,1024]{1,0:T(8,128)}, u32[]{:S(2)}) copy-start(f32[8,1024]{1,0:T(8,128)} %get-tuple-element.88) | copy-start | bytes 98308
  188.7 28.1 %copy-start.1 = (f32[512,1024]{1,0:T(8,128)S(1)}, f32[512,1024]{1,0:T(8,128)}, u32[]{:S(2)}) copy-start(f32[512,1024]{1,0:T(8,128)} %get-tuple-element.80) | copy-start | bytes 6291460
  389.4 5.7 %copy-start.2 = (bf16[1024,1024]{1,0:T(8,128)(2,1)S(1)}, bf16[1024,1024]{1,0:T(8,128)(2,1)}, u32[]{:S(2)}) copy-start(bf16[1024,1024]{1,0:T(8,128)(2,1)} %get-tuple-element.98) | copy-start | bytes 6291460
  395.1 3.7 copy-start

commit v8 on v7

--- a/solution.py
+++ b/solution.py
@@ -150,115 +150,6 @@
             in_rows(tokens, 64, close)
 
 
-def attention_back_kernel(size, row_tokens, parts, act_ref, lengths_ref, grad_in, x_in, qkv_in, wqkv_in, wo_in, cos_in,
-                          sin_in, branch_out, proj_out, input_out, input_low_out, vectors_out, grad_ref, x_ref, qkv_ref,
-                          wqkv_ref, wo_ref, cos_ref, sin_ref, branch_ref, proj_ref, input_low_ref, vectors_ref, gm_ref,
-                          total_ref, load_sem, part_sem, store_sem):
-    tokens, features = x_ref.shape
-    block = features // parts
-    pair = 2 * size
-    scale = size ** -0.5
-    copy = pltpu.make_async_copy
-
-    def work():
-        loads = [
-            copy(source, target, load_sem.at[index]) for index, (source, target) in enumerate(
-                ((grad_in, grad_ref), (cos_in, cos_ref), (sin_in, sin_ref), (x_in, x_ref)))]
-        part_loads = []
-        for part in range(parts):
-            lanes = pl.ds(part * block, block)
-            part_loads.append([copy(wo_in.at[lanes], wo_ref.at[lanes], part_sem.at[part, 0]),
-                               copy(qkv_in.at[:, :, lanes], qkv_ref.at[:, :, lanes], part_sem.at[part, 1])] + [
-                copy(wqkv_in.at[:, pl.ds(which * features + part * block, block)],
-                     wqkv_ref.at[:, pl.ds(which * features + part * block, block)], part_sem.at[part, 2 + which])
-                for which in range(3)])
-        for item in loads[:1] + part_loads[0][:2] + loads[1:3] + part_loads[0][2:] + loads[3:]:
-            item.start()
-        for items in part_loads[1:]:
-            for item in items:
-                item.start()
-        loads[0].wait()
-
-        def begin(rows):
-            branch_ref[rows] = grad_ref[rows].astype(BF16)
-        in_rows(tokens, 64, begin)
-        branch_store = copy(branch_ref, branch_out, store_sem.at[0])
-        branch_store.start()
-        stores = [branch_store]
-        for part in range(parts):
-            columns = slice(part * block, (part + 1) * block)
-            part_loads[part][0].wait()
-            gm_ref[...] = dot_cols(branch_ref[...], wo_ref[columns]).astype(BF16)
-            part_loads[part][1].wait()
-            if part == 0:
-                loads[1].wait()
-                loads[2].wait()
-            first = lanes_of((row_tokens, pair)) < size
-            @pl.loop(0, tokens // row_tokens)
-            def _(row):
-                rows = pl.ds(pl.multiple_of(row * row_tokens, row_tokens), row_tokens)
-                allowed = same_window(lengths_ref, row, row_tokens)
-                cosine, sine = cos_ref[rows], sin_ref[rows]
-                for start in range(0, block // pair, 2):
-                    work = []
-                    for at in range(start, start + 2):
-                        lanes = pl.ds(part * block + at * pair, pair)
-                        query, key, value = (qkv_ref[which, rows, lanes] for which in range(3))
-                        grad_mix = gm_ref[rows, pl.ds(at * pair, pair)]
-                        scaled = query * scale
-                        for head in range(2):
-                            mine = first if head == 0 else jnp.logical_not(first)
-                            work.append((
-                                query, key, grad_mix,
-                                dot_cols(jnp.where(mine, scaled, jnp.zeros_like(scaled)), key),
-                                dot_cols(jnp.where(mine, grad_mix, jnp.zeros_like(grad_mix)), value)))
-                    results = []
-                    for query, key, grad_mix, scores, grad_probs in work:
-                        probs = softmax(scores, allowed)
-                        weighted = probs * grad_probs
-                        grad_scores = (weighted - probs * jnp.sum(weighted, axis=-1, keepdims=True)).astype(BF16)
-                        results.append((query, key, grad_mix, grad_scores, probs.astype(BF16)))
-                    results = [
-                        (dot(grad_scores, key), dot_rows(grad_scores, query), dot_rows(probs, grad_mix))
-                        for query, key, grad_mix, grad_scores, probs in results]
-                    for at in range(2):
-                        lanes = pl.ds(part * block + (start + at) * pair, pair)
-                        grad_query, grad_key, grad_value = (
-                            jnp.where(first, a, b) for a, b in zip(results[2 * at], results[2 * at + 1]))
-                        proj_ref[0, rows, lanes] = unrotated(grad_query * scale, cosine, sine, size).astype(BF16)
-                        proj_ref[1, rows, lanes] = unrotated(grad_key * scale, cosine, sine, size).astype(BF16)
-                        proj_ref[2, rows, lanes] = grad_value.astype(BF16)
-            lanes = pl.ds(part * block, block)
-            stores.append(copy(proj_ref.at[:, :, lanes], proj_out.at[:, :, lanes], store_sem.at[1 + part]))
-            stores[-1].start()
-            added = 0.0
-            for which in range(3):
-                part_loads[part][2 + which].wait()
-                weights = wqkv_ref[:, which * features + part * block:which * features + (part + 1) * block]
-                added = added + dot_cols(proj_ref[which, :, columns], weights)
-            total_ref[...] = added if part == 0 else total_ref[...] + added
-        loads[3].wait()
-        vectors_ref[...] = jnp.zeros_like(vectors_ref)
-
-        def finish(rows):
-            grad = total_ref[rows]
-            through, by_gain = norm_back(grad, x_ref[rows].astype(F32), grad_ref[tokens:tokens + 1])
-            result = grad_ref[rows] + through
-            total_ref[rows] = result
-            input_low_ref[rows] = result.astype(BF16)
-            vectors_ref[0:1] += jnp.sum(by_gain, axis=0, keepdims=True)
-            vectors_ref[1:2] += jnp.sum(grad, axis=0, keepdims=True)
-        in_rows(tokens, 64, finish)
-        for index, (source, target) in enumerate(
-                ((input_low_ref, input_low_out), (total_ref, input_out), (vectors_ref, vectors_out))):
-            stores.append(copy(source, target, store_sem.at[1 + parts + index]))
-            stores[-1].start()
-        for item in stores:
-            item.wait()
-
-    pl.when(act_ref[0] == 1)(work)
-
-
 def places():
     section, shard, seat = (lax.axis_index(name) for name in ("section", "shard", "group"))
     stride = 2 - section
@@ -468,32 +359,6 @@
         [pltpu.VMEM((tokens, wide), BF16)], 8 * tokens * features ** 2)
 
 
-def attention_back(active, lengths, grad_mid, x, qkv, w_qkv, w_out, cosine, sine, parts=2):
-    tokens, features = x.shape
-    row_tokens = tokens // lengths.shape[0]
-    size = features // HEADS
-    low = jax.ShapeDtypeStruct((tokens, features), BF16)
-    stack = jax.ShapeDtypeStruct((3, tokens, features), BF16)
-    full = jax.ShapeDtypeStruct((tokens, features), F32)
-    vectors = jax.ShapeDtypeStruct((8, features), F32)
-    outs = (low, stack, full, low, vectors)
-    hbm, smem, dma = pl.BlockSpec(memory_space=pl.ANY), pl.BlockSpec(memory_space=pltpu.SMEM), pltpu.SemaphoreType.DMA
-    held = [grad_mid, x, qkv, w_qkv, w_out, cosine, sine, low, stack, low, vectors]
-    return pl.pallas_call(
-        functools.partial(attention_back_kernel, size, row_tokens, parts),
-        out_shape=outs,
-        in_specs=[smem, smem] + [hbm] * 7,
-        out_specs=[hbm] * len(outs),
-        scratch_shapes=[pltpu.VMEM(item.shape, item.dtype) for item in held] + [
-            pltpu.VMEM((tokens, features // parts), BF16), pltpu.VMEM((tokens, features), F32),
-            dma((4,)), dma((parts, 5)), dma((4 + parts,))],
-        name="attention_back",
-        cost_estimate=pl.CostEstimate(
-            flops=20 * tokens * features ** 2, bytes_accessed=40 * 2 ** 20, transcendentals=0),
-        compiler_params=pltpu.CompilerParams(vmem_limit_bytes=56 * 1024 * 1024),
-    )(active, lengths, grad_mid, x, qkv, w_qkv, w_out, cosine, sine)
-
-
 def third(tokens, features):
     return pl.BlockSpec((1, tokens, features), lambda part, *_: (2, 0, 0))
 
@@ -565,8 +430,8 @@
     return jnp.cos(angles), jnp.sin(angles)
 
 
-def exchange_kernel(cfg, *refs):
-    shards, bits, seats, unit_rows, width, section, aliased, late, layers, other_layers, lag, supply, order = cfg
+def exchange_kernel(cfg, back_sizes, *refs):
+    shards, bits, seats, unit_rows, width, section, aliased, late, layers, other_layers, lag, supply, order, backs = cfg
     arrays = len(seats)
     refs = list(refs)
 
@@ -575,19 +440,25 @@
         del refs[:count]
         return taken
 
-    lefts, rights = take(arrays), take(arrays)
+    lefts, rights = take(arrays), take(arrays - len(supply))
+    for index in supply:
+        rights.insert(index, None)
     left_others, right_others = take(arrays - (1 if late else 0)), take(1)
     lefts = [ref if at is None else ref.at[at] for ref, at in zip(lefts, layers)]
     left_others = [ref if at is None else ref.at[at] for ref, at in zip(left_others, other_layers)]
     (vector,) = take(1)
-    vector_given = take(1) if supply else []
-    take(arrays + 1 if aliased else 0)
+    back_in = take(7)
+    (lengths_ref,) = take(1)
+    take(arrays + 2 if aliased else 0)
     outs, (vector_out,) = take(arrays), take(1)
     if late:
         left_others = left_others + take(1)
-    given = [rights[index] for index in supply]
     for index in supply:
         rights[index] = take(1)[0]
+    (back_out,) = take(1)
+    back_refs, (back_load, back_store) = take(12), take(2)
+    (grad_ref, x_ref, qkv_ref, wqkv_ref, wo_ref, cos_ref, sin_ref, branch_ref, proj_ref, vectors_ref, gm_ref,
+     total_ref) = back_refs
     (given_send, given_recv, vector_far, vector_full, vector_land, vector_sum, vector_send, vector_recv, vector_store, left, right, left_sem, right_sem, other_sem,
      right_send, right_recv, late_send, late_recv, mine, side_land, side, side_send, side_recv, chain_a, chain_b,
      chain_send, chain_recv, rest_send, rest_land, rest_keep, rest_ssem, rest_rsem, piece, store_sem, gather_send,
@@ -638,9 +509,7 @@
                       vector_recv.at[me], device)
 
     def vector_finish():
-        vector_full[...] = vector[...]
-        if supply:
-            vector_full[...] += vector_far[...]
+        vector_full[...] = vector[...] + (vectors_ref[...] if backs else vector_far[...])
 
         @pl.loop(1, peers)
         def _(step):
@@ -961,29 +830,166 @@
         if step + 1 < bits:
             spread(path, step + 1, chunk)
 
-    def given_copies():
-        device = (section, here, seat)
-        targets = [rights[index] for index in supply] + [vector_far]
-        return [remote(source, target, given_send.at[index], given_recv.at[index], device)
-                for index, (source, target) in enumerate(zip(given + vector_given, targets))]
+    size, row_tokens, parts = back_sizes
+    features = x_ref.shape[1]
+    block, pair, scale = features // parts, 2 * size, size ** -0.5
+    groups = block // pair // 2
+    part_steps = 2 + tokens // row_tokens * groups
+    back_steps = 2 + parts * part_steps
+
+    def back_loads():
+        return [pltpu.make_async_copy(source, target, back_load.at[index])
+                for index, (source, target) in enumerate(zip(back_in, back_refs))]
+
+    def back_start():
+        copies = back_loads()
+        for index in (0, 4, 2, 5, 6, 3, 1):
+            copies[index].start()
+
+    def back_lanes(part):
+        return aligned(part * block, block)
+
+    def deliver(index, source, target):
+        if backs:
+            return pltpu.make_async_copy(source, target, back_store.at[index])
+        return remote(source, target, given_send.at[index], given_recv.at[index], (section, here, seat))
+
+    def deliver_branch():
+        return deliver(0, branch_ref, rights[supply[0]].at[0])
+
+    def deliver_part(part):
+        lanes = back_lanes(part)
+        return deliver(1 + part, proj_ref.at[:, :, lanes], rights[supply[1]].at[:, :, lanes])
+
+    def deliver_vectors():
+        return deliver(1 + parts, vectors_ref, vector_far)
+
+    def back_store_last():
+        return pltpu.make_async_copy(total_ref if backs else branch_ref, back_out, back_store.at[1 + parts])
+
+    def back_begin():
+        back_loads()[0].wait()
+
+        def put(rows):
+            branch_ref[rows] = grad_ref[rows].astype(BF16)
+        by_rows(tokens, put)
+        deliver_branch().start()
+
+    def back_open(part):
+        @pl.when(part == 0)
+        def _():
+            for index in (4, 2, 5, 6):
+                back_loads()[index].wait()
+        gm_ref[...] = dot_cols(branch_ref[...], wo_ref[back_lanes(part)]).astype(BF16)
+
+    def back_heads(part, row, group):
+        rows = aligned(row * row_tokens, row_tokens)
+        first = lanes_of((row_tokens, pair)) < size
+        allowed = same_window(lengths_ref, row, row_tokens)
+        cosine, sine = cos_ref[rows], sin_ref[rows]
+        lanes = [aligned(part * block + (2 * group + at) * pair, pair) for at in range(2)]
+        work = []
+        for at in range(2):
+            query, key, value = (qkv_ref[which, rows, lanes[at]] for which in range(3))
+            grad_mix = gm_ref[rows, aligned((2 * group + at) * pair, pair)]
+            scaled = query * scale
+            for head in range(2):
+                own = first if head == 0 else jnp.logical_not(first)
+                work.append((
+                    query, key, grad_mix,
+                    dot_cols(jnp.where(own, scaled, jnp.zeros_like(scaled)), key),
+                    dot_cols(jnp.where(own, grad_mix, jnp.zeros_like(grad_mix)), value)))
+        results = []
+        for query, key, grad_mix, scores, grad_probs in work:
+            probs = softmax(scores, allowed)
+            weighted = probs * grad_probs
+            grad_scores = (weighted - probs * jnp.sum(weighted, axis=-1, keepdims=True)).astype(BF16)
+            results.append((query, key, grad_mix, grad_scores, probs.astype(BF16)))
+        results = [
+            (dot(grad_scores, key), dot_rows(grad_scores, query), dot_rows(probs, grad_mix))
+            for query, key, grad_mix, grad_scores, probs in results]
+        for at in range(2):
+            grad_query, grad_key, grad_value = (
+                jnp.where(first, a, b) for a, b in zip(results[2 * at], results[2 * at + 1]))
+            proj_ref[0, rows, lanes[at]] = unrotated(grad_query * scale, cosine, sine, size).astype(BF16)
+            proj_ref[1, rows, lanes[at]] = unrotated(grad_key * scale, cosine, sine, size).astype(BF16)
+            proj_ref[2, rows, lanes[at]] = grad_value.astype(BF16)
+
+    def back_close(part):
+        deliver_part(part).start()
+
+        @pl.when(part == 0)
+        def _():
+            back_loads()[3].wait()
+        added = 0.0
+        for which in range(3):
+            added = added + dot_cols(
+                proj_ref[which, :, back_lanes(part)], wqkv_ref[:, aligned(which * features + part * block, block)])
+        total_ref[...] = jnp.where(part == 0, added, total_ref[...] + added)
+
+    def back_end():
+        back_loads()[1].wait()
+        vectors_ref[...] = jnp.zeros_like(vectors_ref)
+        if not backs:
+            deliver_branch().wait_send()
+
+        def end(rows):
+            grad = total_ref[rows]
+            through, by_gain = norm_back(grad, x_ref[rows].astype(F32), grad_ref[tokens:tokens + 1])
+            result = grad_ref[rows] + through
+            if backs:
+                total_ref[rows] = result
+            else:
+                branch_ref[rows] = result.astype(BF16)
+            vectors_ref[0:1] += jnp.sum(by_gain, axis=0, keepdims=True)
+            vectors_ref[1:2] += jnp.sum(grad, axis=0, keepdims=True)
+        by_rows(tokens, end)
+        back_store_last().start()
+        if backs:
+            deliver_branch().wait()
+        else:
+            deliver_vectors().start()
+            deliver_vectors().wait_send()
+        for part in range(parts):
+            if backs:
+                deliver_part(part).wait()
+            else:
+                deliver_part(part).wait_send()
+        back_store_last().wait()
+
+    def back_step(step):
+        on(step == 0, back_begin)
+        inner = jnp.maximum(step - 1, 0)
+        part = lax.div(inner, part_steps)
+        at = inner - part * part_steps
+        within = (step > 0) & (step < back_steps - 1)
+        on(within & (at == 0), lambda: back_open(part))
+        head = at - 1
+        row = lax.div(jnp.maximum(head, 0), groups)
+        on(within & (at > 0) & (at < part_steps - 1), lambda: back_heads(part, row, head - row * groups))
+        on(within & (at == part_steps - 1), lambda: back_close(part))
+        on(step == back_steps - 1, back_end)
 
     def hand_over():
+        back_start()
         pl.semaphore_wait(pltpu.get_barrier_semaphore(), 1)
-        for copy in given_copies():
-            copy.start()
-        for copy in given_copies():
-            copy.wait_send()
+
+        @pl.loop(0, back_steps)
+        def _(step):
+            back_step(step)
 
     def take_over():
-        for copy in given_copies():
-            copy.wait_recv()
+        deliver_branch().wait_recv()
+        for part in range(parts):
+            deliver_part(part).wait_recv()
+        deliver_vectors().wait_recv()
 
     def unit_of(index):
         return index if index < lead else lead + (index - lead) // pace * (pace + 1) + 1 + (index - lead) % pace
 
     def work():
         barrier = pltpu.get_barrier_semaphore()
-        if supply:
+        if not backs:
             pl.semaphore_signal(barrier, inc=1, device_id=(1 - section, here, seat), device_id_type=MESH)
 
         @pl.loop(1, peers)
@@ -993,6 +999,8 @@
         for chunk in range(lag):
             send_right(chunk)
         loads(0, lambda copy: copy.start())
+        if backs:
+            back_start()
 
         for path in range(2):
             for way in range(2):
@@ -1006,7 +1014,9 @@
 
         @pl.loop(0, units + lag * (line + others + bits) + 2)
         def _(turn):
-            if supply:
+            if backs:
+                back_step(turn - 1)
+            else:
                 on(turn == unit_of(sum(seat[0] for seat in seats[:supply[0]])) - lag, take_over)
             on(turn + lag < units, lambda: send_right(turn + lag))
             if late:
@@ -1041,11 +1051,11 @@
         work()
     else:
         pl.when(sec == section)(work)
-        if supply:
+        if not backs:
             pl.when(sec != section)(hand_over)
 
 
-def exchange(pairs, vector, shards, group, section, collective_id, unit_width, previous=None, lag=2, supply=(), vector_given=None, first_bit=0, unit_rows_max=256,
+def exchange(pairs, vector, shards, group, section, collective_id, unit_width, previous=None, lag=None, first_bit=0, supply=(1, 2), back=(), backs=False, parts=2, unit_rows_max=256,
              name="exchange"):
     bits = group.bit_length() - 1
     arrays = len(pairs)
@@ -1069,13 +1079,21 @@
     units = sum(seat[0] for seat in seats)
     others = bits - 1
     final_rows = unit_rows >> others
+    lag = lag or (2 if shards <= 4 else 1)
     slots, right_slots = 2 * lag + 2, 2 * lag + 3
     depth, ring = lag * shards + 3, lag * (shards - 1) + 2
     late_rows = rows_of[-1] // (2 * unit_rows)
     peers, lanes = shards * group, vector.shape[1] // shards
     dma = pltpu.SemaphoreType.DMA
+    *back, lengths = back
+    x = back[1]
+    previous = list(previous or [])
     scratch = [
-        dma((len(supply) + 1,)), dma((len(supply) + 1,)),
+        *(pltpu.VMEM(item.shape, item.dtype) for item in back),
+        pltpu.VMEM(x.shape, BF16), pltpu.VMEM((3,) + x.shape, BF16), pltpu.VMEM(vector.shape, F32),
+        pltpu.VMEM((tokens, x.shape[1] // parts), BF16), pltpu.VMEM(x.shape, F32),
+        dma((len(back),)), dma((2 + parts,)),
+        dma((2 + parts,)), dma((2 + parts,)),
         pltpu.VMEM(vector.shape, F32), pltpu.VMEM(vector.shape, F32),
         pltpu.VMEM((peers, vector.shape[0], lanes), F32),
         pltpu.VMEM((vector.shape[0], lanes), F32),
@@ -1100,31 +1118,37 @@
         dma((2, slots)),
         dma((2, bits, 2, slots)), dma((2, bits, 2, slots)),
     ]
-    cfg = (shards, bits, tuple(seats), unit_rows, width, section, previous is not None, late, layers, other_layers, lag, supply, order)
-    vectors = [vector] + ([vector_given] if supply else [])
-    operands = lefts + rights + left_others + [pairs[-1][3]] + vectors + list(previous or [])
-    first = len(operands) - len(previous or [])
+    cfg = (shards, bits, tuple(seats), unit_rows, width, section, len(previous) > 0, late, layers, other_layers, lag, supply, order, backs)
+    operands = lefts + [r for n, r in enumerate(rights) if n not in supply] + left_others + [
+        pairs[-1][3], vector] + back + [lengths] + previous
+    first = len(operands) - len(previous)
     results = [jax.ShapeDtypeStruct((r, g.shape[0] * g.shape[2]), BF16) for r, g in zip(rows_of, rights)]
     results.append(jax.ShapeDtypeStruct((vector.shape[0], lanes), F32))
     if late:
         results.append(jax.ShapeDtypeStruct((tokens, lefts[-1].shape[-1] // 2), BF16))
     results.extend(jax.ShapeDtypeStruct(rights[index].shape, BF16) for index in supply)
+    results.append(jax.ShapeDtypeStruct(x.shape, F32 if backs else BF16))
+    aliases = {first + index: index for index in range(len(previous))}
+    if previous:
+        aliases[len(operands) - 1] = len(results) - 1
     hbm, vmem = pl.BlockSpec(memory_space=pl.ANY), pl.BlockSpec(memory_space=pltpu.VMEM)
-    in_specs = [vmem if first - len(vectors) <= index < first else hbm for index in range(len(operands))]
+    in_specs = [hbm] * len(operands)
+    in_specs[first - 1] = pl.BlockSpec(memory_space=pltpu.SMEM)
+    in_specs[first - 2 - len(back)] = vmem
     return pl.pallas_call(
-        functools.partial(exchange_kernel, cfg),
+        functools.partial(exchange_kernel, cfg, (x.shape[1] // HEADS, tokens // lengths.shape[0], parts)),
         out_shape=results,
         in_specs=in_specs,
         out_specs=[hbm] * len(results),
         scratch_shapes=scratch,
-        input_output_aliases={first + index: index for index in range(len(previous or []))},
+        input_output_aliases=aliases,
         name=name,
         cost_estimate=pl.CostEstimate(
             flops=4 * tokens * units * shards * unit_rows * 2 * width, bytes_accessed=100 * 2 ** 20,
             transcendentals=0),
         compiler_params=pltpu.CompilerParams(
             collective_id=collective_id, has_side_effects=True, vmem_limit_bytes=56 * 1024 * 1024),
-    )(*operands)[:arrays + 1]
+    )(*operands)
 
 
 UNIT_WIDTH = 512
@@ -1144,7 +1168,6 @@
 ):
     section = lax.axis_index("section")
     shards, group = lax.axis_size("shard"), lax.axis_size("group")
-    is_first = section == 0
     first, second = ((section == which).astype(jnp.int32).reshape(1) for which in range(2))
     tokens, features = ends_in.shape[1:]
     size = features // HEADS
@@ -1166,14 +1189,12 @@
         return feed_both(active, middle, lefts, grad, norm_gain_f, norm_gain_a, weight_gu, weight_down, sends, lands,
                          collective_id)
 
-    def attend_back(grad_middle, values, qkv, weight_qkv, weight_out):
-        return attention_back(first, lengths, grad_middle, values, qkv, weight_qkv, weight_out, cosine, sine)
-
-    def sum_all(which, lefts, lefts_beside, hidden, hidden_beside, rights, right_beside, vectors, **more):
+    def sum_all(which, lefts, lefts_beside, hidden, hidden_beside, grad_gu, grad, grad_beside, vectors, back, **more):
+        rights = (grad_gu, jax.ShapeDtypeStruct((1, tokens, features), BF16), stack)
         pairs = [((lefts, at), right, other) for at, right, other in zip((2, 1, 0), rights, lefts_beside)]
-        pairs.append(((hidden, None), rights[3], hidden_beside, right_beside))
+        pairs.append(((hidden, None), grad[None], hidden_beside, grad_beside))
         return exchange(pairs, vectors, shards, group, which, which + 1, UNIT_WIDTH * features // 1024,
-                        first_bit=1 - which, **more)
+                        first_bit=1 - which, back=back + (cosine, sine, lengths), **more)
 
     middle_0, lefts_0, qkv_0 = attend(first, rows)
     passed, hidden_half_0, arrived, early_beside, rows_beside = feed(
@@ -1184,18 +1205,16 @@
             1, middle_1, lefts_1, rows,
             (lefts_1, qkv_1, weight_qkv, weight_out, lefts_0, hidden_half_0),
             (stack, stack, like(weight_qkv), like(weight_out), like(hidden_half_0), jax.ShapeDtypeStruct((tokens + 8, features), F32)), 4)
-    branch, grad_qkv, _, returned, vectors_far = attend_back(grad_middle, passed, qkv_there, qkv_weight, out_weight)
-    sums = sum_all(1, lefts_1, [(lefts_beside, at) for at in (2, 1, 0)], hidden_1, None,
-                   (grad_gu_1, branch[None], grad_qkv, rows[None]), rows_beside, vectors_1, vector_given=vectors_far,
-                   lag=1, supply=(1, 2), name="exchange_second")
-    returned, _ = lax.optimization_barrier((returned, sums[4]))
+    sums = sum_all(1, lefts_1, [(lefts_beside, at) for at in (2, 1, 0)], hidden_1, None, grad_gu_1, rows, rows_beside,
+                   vectors_1, (grad_middle, passed, qkv_there, qkv_weight, out_weight), name="exchange_second")
+    returned = sums[-1]
     _, hidden_0, grad_gu_0, grad_middle, vectors_0, returned_beside = feed_back(
         0, middle_0, lefts_0, returned, (returned,), (low,), 5)
-    branch, grad_qkv, grad_in, _, vectors_near = attend_back(grad_middle, rows, qkv_0, weight_qkv, weight_out)
     sums = sum_all(0, lefts_0, [(lefts_beside, 2), (early_beside, 1), (early_beside, 0)], hidden_0,
-                   (hidden_beside, None), (grad_gu_0, branch[None], grad_qkv, returned[None]), returned_beside,
-                   vectors_0 + vectors_near, previous=sums, lag=2, name="exchange_first")
-    ends_out = jnp.where(is_first, grad_in, result)[None]
+                   (hidden_beside, None), grad_gu_0, returned, returned_beside, vectors_0,
+                   (grad_middle, rows, qkv_0, weight_qkv, weight_out), backs=True, previous=[*sums[:5], result],
+                   name="exchange_first")
+    ends_out = sums[-1][None]
     grad_gate_up, grad_out, grad_qkv, grad_down = (item.astype(F32)[None] for item in sums[:4])
     vectors = sums[4]
     return (

time: 411 us -> 395 us (0.961); the launches traced: 403 us -> 394 us
  Pallas kernels: 379 us -> 374 us
  other arithmetic: 20.5 us -> 15.6 us
    pallas_call x4 -> x2, Pallas kernels: 233 us -> 227 us  [exchange(): pl.pallas_call(functools.partial(exchange_kernel, cfg, (x.shape[1] // HEA...]
where the time goes in v8:
time: 395 us; the launch traced here: 394 us
  Pallas kernels  374 us (95%)
  other arithmetic  15.6 us (4%)
  local copies, waits for them, and re-layouts  4.09 us (1%)
    pallas_call x2, Pallas kernels, exchange(): pl.pallas_call(functools.partial(exchange_kernel, cfg, (x.shape[1] // HEA...  227 us
    pallas_call x3, Pallas kernels, meeting_call(): pl.pallas_call(kernel, grid=(parts,), in_specs=in_specs, out_specs=out_sp...  120 us
    pallas_call x2, Pallas kernels, local_call(): pl.pallas_call(kernel, grid_spec=pltpu.PrefetchScalarGridSpec(num_scalar_...  26.4 us
    broadcast_in_dim x4, other arithmetic, body(): item.astype(F32)[None]  12.7 us

profile of v8, /device:TPU:0, one launch (start us, length us, event | category | flops | bytes accessed | tf_op | source)
XLA Modules:
  0.0 394.4 jit_solution(5607258958083116459)
XLA Ops:
  0.7 1.0 fusion.7
  1.7 0.1 broadcast_bitcast_fusion.4
  1.8 0.1 broadcast_bitcast_fusion.2
  1.9 0.1 broadcast_bitcast_fusion
  2.0 1.8 multiply_sine_fusion
  3.8 19.8 %attention.2 = (f32[512,1024]{1,0:T(8,128)}, bf16[3,512,1024]{2,1,0:T(8,128)(2,1)}, bf16[3,512,1024]{2,1,0:T(8,128)(2,1)}) custom-call(s32[1]{0:T(128)} %bitcast.act_ref, s32[2,3]{1,0:T(2,128)} %refs_19_.1, bf16[512,1024]{1,0:T(8,128)(2,1)} %bitcast.60, f32[1,1024]{1,0:T(1,128)} %gain_a_ref.3, f32[1,1024]{1,0:T(1,128)} %bias_ref.3, f32[1,1024]{1,0:T(1,128)} %gain_ref.7, ...), custom_call_target="tpu_custom_call" | custom-call | flops 4294967296 | bytes 41943040 | tf_op jit(solution)/shard_map/attention/pallas_call | solution.py:332
  23.6 31.6 %feed.1 = (bf16[512,1024]{1,0:T(8,128)(2,1)}, bf16[512,2048]{1,0:T(8,128)(2,1)}, bf16[512,1024]{1,0:T(8,128)(2,1)}, bf16[2,512,1024]{2,1,0:T(8,128)(2,1)}, bf16[512,1024]{1,0:T(8,128)(2,1)}) custom-call(f32[512,1024]{1,0:T(8,128)} %get-tuple-element.48.mid_ref, bf16[3,512,1024]{2,1,0:T(8,128)(2,1)} %get-tuple-element.47.low_ref.lefts_ref.refs_4_.refs_0_.refs_1_.refs_2_, ...), custom_call_target="tpu_custom_call" | custom-call | flops 12884901888 | bytes 41943040 | tf_op jit(solution)/shard_map/feed/pallas_call | solution.py:367
  55.3 6.6 %attention.3 = (f32[512,1024]{1,0:T(8,128)}, bf16[3,512,1024]{2,1,0:T(8,128)(2,1)}, bf16[3,512,1024]{2,1,0:T(8,128)(2,1)}) custom-call(s32[1]{0:T(128)} %bitcast.4.act_ref, s32[2,3]{1,0:T(2,128)} %refs_19_.1, bf16[512,1024]{1,0:T(8,128)(2,1)} %get-tuple-element.49.x_ref, f32[1,1024]{1,0:T(1,128)} %gain_a_ref.3, f32[1,1024]{1,0:T(1,128)} %bias_ref.3, ...), custom_call_target="tpu_custom_call" | custom-call | flops 4294967296 | bytes 41943040 | tf_op jit(solution)/shard_map/attention/pallas_call | solution.py:332
  61.9 49.5 %feed_both.2 = (f32[512,1024]{1,0:T(8,128)}, bf16[512,4096]{1,0:T(8,128)(2,1)}, bf16[2,512,4096]{2,1,0:T(8,128)(2,1)}, f32[520,1024]{1,0:T(8,128)}, f32[8,1024]{...) custom-call(f32[512,1024]{1,0:T(8,128)} %get-tuple-element.51.mid_re, ...), custom_call_target="tpu_custom_call" | custom-call | flops 25769803776 | bytes 41943040 | tf_op jit(solution)/shard_map/feed_both/pallas_call | solution.py:367
  111.3 30.9 %exchange_second.1 = (bf16[256,8192]{1,0:T(8,128)(2,1)}, bf16[256,1024]{1,0:T(8,128)(2,1)}, bf16[256,3072]{1,0:T(8,128)(2,1)}, bf16[1024,1024]{1,0:T(8,128)(2,1)...) custom-call(bf16[3,512,1024]{2,1,0:T(8,128)(2,1)} %get-tuple-element, ...), custom_call_target="tpu_custom_call" | custom-call | flops 17179869184 | bytes 104857600 | tf_op jit(solution)/shard_map/exchange_second/pallas_call | solution.py:1138
  142.3 39.2 %feed_both.3 = (f32[512,1024]{1,0:T(8,128)}, bf16[512,4096]{1,0:T(8,128)(2,1)}, bf16[2,512,4096]{2,1,0:T(8,128)(2,1)}, f32[520,1024]{1,0:T(8,128)}, f32[8,1024]{1,0:T(8,128)}, /*index=5*/bf16[512,1024]{1,0:T(8,128)(2,1)}) custom-call(f32[512,1024]{1,0:T(8,128)} %get-tuple-element.48.mid_ref, ...), custom_call_target="tpu_custom_call" | custom-call | flops 25769803776 | bytes 41943040 | tf_op jit(solution)/shard_map/feed_both/pallas_call | solution.py:367
  181.4 196.4 %exchange_first.1 = (bf16[256,8192]{1,0:T(8,128)(2,1)}, bf16[256,1024]{1,0:T(8,128)(2,1)}, bf16[256,3072]{1,0:T(8,128)(2,1)}, bf16[1024,1024]{1,0:T(8,128)(2,1)}...) custom-call(bf16[3,512,1024]{2,1,0:T(8,128)(2,1)} %get-tuple-element, ...), custom_call_target="tpu_custom_call", output_to_operand_aliasing={{0}: (20, {}), {1}: (21, {}), {2}: (22, {}), {3}: (23, {}),... | custom-call | flops 17179869184 | bytes 104857600 | tf_op jit(solution)/shard_map/exchange_first/pallas_call | solution.py:1138
  377.9 1.4 fusion.8
  379.3 0.0 copy-start.1
  379.3 2.3 bitcast_convert_fusion.3
  381.6 3.4 bitcast_convert_fusion.2
  385.0 0.0 copy-done.1
  385.0 0.0 copy-start
  385.0 2.6 bitcast_convert_fusion.1
  387.6 1.1 copy-done
  388.7 0.0 copy-start.2
  388.7 4.4 %bitcast_convert_fusion = f32[1,256,8192]{2,1,0:T(8,128)} fusion(bf16[256,8192]{1,0:T(8,128)(2,1)S(1)} %copy-done), kind=kLoop, calls=%fused_computation | loop fusion | flops 2097152 | bytes 12582912 | tf_op jit(solution)/shard_map/broadcast_in_dim | solution.py:1218
  393.1 0.0 copy-done.2
  393.1 1.3 copy.38
  (9 shorter events, 0.0 us)
Async XLA Ops:
  379.3 5.7 %copy-start.1 = (bf16[1024,1024]{1,0:T(8,128)(2,1)S(1)}, bf16[1024,1024]{1,0:T(8,128)(2,1)}, u32[]{:S(2)}) copy-start(bf16[1024,1024]{1,0:T(8,128)(2,1)} %get-tuple-element.84) | copy-start | bytes 6291460
  385.0 3.7 copy-start
  388.7 4.4 %copy-start.2 = (f32[512,1024]{1,0:T(8,128)S(1)}, f32[512,1024]{1,0:T(8,128)}, u32[]{:S(2)}) copy-start(f32[512,1024]{1,0:T(8,128)} %get-tuple-element.79) | copy-start | bytes 6291460

commit v9 on v8

--- a/solution.py
+++ b/solution.py
@@ -91,23 +91,32 @@
     return weights * (1.0 / jnp.sum(weights, axis=-1, keepdims=True))
 
 
-def attention_kernel(size, row_tokens, act_ref, lengths_ref, x_ref, gain_ref, bias_ref, gain_f_ref, bias_f_ref,
-                     wq_ref, wk_ref, wv_ref, wo_ref, cos_ref, sin_ref, mid_ref, lefts_ref, qkv_ref, mix_ref):
+def attention_kernel(size, row_tokens, active, x_ref, gain_ref, bias_ref, gain_f_ref, bias_f_ref, wq_ref, wk_ref,
+                     wv_ref, wo_ref, cos_ref, sin_ref, lengths_ref, mid_ref, lefts_ref, qkv_ref, low_land, mix_ref, sems):
     tokens = x_ref.shape[0]
     part = pl.program_id(0)
     block = wq_ref.shape[1]
     pair = 2 * size
 
-    @pl.when(act_ref[0] == 1)
+    section, _, beside, _ = places()
+    low_copy = remote(lefts_ref.at[0], low_land, sems, 0, beside)
+
+    @pl.when(section == active)
     def _():
         @pl.when(part == 0)
         def _():
+            if active:
+                greet(beside)
+
             def begin(rows):
                 values = x_ref[rows].astype(F32)
                 unit, _ = normalized(values)
                 lefts_ref[0, rows] = (unit * gain_ref[...] + bias_ref[...]).astype(BF16)
                 mid_ref[rows] = values
             in_rows(tokens, 64, begin)
+            if active:
+                await_greetings(1)
+                low_copy.start()
 
         for which, weight in enumerate((wq_ref, wk_ref, wv_ref)):
             projected = dot(lefts_ref[0], weight[...])
@@ -148,6 +157,8 @@
                 unit, _ = normalized(mid_ref[rows])
                 lefts_ref[2, rows] = (unit * gain_f_ref[...] + bias_f_ref[...]).astype(BF16)
             in_rows(tokens, 64, close)
+            if active:
+                low_copy.wait()
 
 
 def places():
@@ -163,11 +174,14 @@
         device_id_type=pl.DeviceIdType.MESH)
 
 
-def meet(*devices):
-    barrier = pltpu.get_barrier_semaphore()
+def greet(*devices):
     for device in devices:
-        pl.semaphore_signal(barrier, inc=1, device_id=device, device_id_type=pl.DeviceIdType.MESH)
-    pl.semaphore_wait(barrier, len(devices))
+        pl.semaphore_signal(
+            pltpu.get_barrier_semaphore(), inc=1, device_id=device, device_id_type=pl.DeviceIdType.MESH)
+
+
+def await_greetings(count):
+    pl.semaphore_wait(pltpu.get_barrier_semaphore(), count)
 
 
 def feed_kernel(unit_rows, mid_ref, low_ref, wg_ref, wu_ref, wd_ref, lefts_ref, rows_ref, out_ref, half_ref,
@@ -178,9 +192,11 @@
     rows_copy = remote(rows_ref, rows_land, sems, 0, beside)
     out_copy = remote(out_ref, arrived_ref, sems, 1, above)
 
-    @pl.when(part == 0)
+    pl.when(part == 0)(lambda: greet(beside, above))
+
+    @pl.when(part == 1)
     def _():
-        meet(beside, above)
+        await_greetings(2)
         pl.when(section == 0)(lefts_copy.start)
         pl.when(section == 1)(rows_copy.start)
 
@@ -216,8 +232,8 @@
 
 def feed_both_kernel(active, mid_ref, low_ref, grad_ref, gain_ref, gain_a_ref, wg_ref, wu_ref, wd_ref, *refs):
     sends, refs = refs[:6 if active else 1], refs[6 if active else 1:]
-    out_ref, hidden_ref, ggu_ref, grad_mid_ref, vectors_ref = refs[:5]
-    lands = refs[5:5 + (6 if active else 1)]
+    hidden_ref, ggu_ref, grad_mid_ref, vectors_ref = refs[:4]
+    lands = refs[4:4 + (6 if active else 1)]
     total_ref, sems = refs[-2:]
     tokens = mid_ref.shape[0]
     part = pl.program_id(0)
@@ -228,7 +244,7 @@
         lefts_ref, qkv_ref, wqkv_ref, wo_ref, lefts_first, hidden_first = sends
         lefts_land, qkv_land, wqkv_land, wo_land, hidden_land, grad_land = lands
         working = [
-            remote(lefts_ref, lefts_land, sems, 0, beside), remote(qkv_ref, qkv_land, sems, 1, other),
+            remote(lefts_ref.at[1:3], lefts_land.at[1:3], sems, 0, beside), remote(qkv_ref, qkv_land, sems, 1, other),
             remote(wqkv_ref, wqkv_land, sems, 2, other), remote(wo_ref, wo_land, sems, 3, other)]
         waiting = [
             remote(lefts_first.at[2], lefts_land.at[2], sems, 4, beside),
@@ -243,7 +259,14 @@
     @pl.when(part == 0)
     def _():
         if active:
-            meet(beside, other)
+            greet(beside, other)
+        else:
+            pl.when(section == active)(lambda: greet(beside))
+
+    @pl.when(part == 1)
+    def _():
+        if active:
+            await_greetings(2)
 
             @pl.when(section != active)
             def _():
@@ -253,16 +276,12 @@
         @pl.when(section == active)
         def _():
             if not active:
-                meet(beside)
+                await_greetings(1)
             for copy in working:
                 copy.start()
 
     @pl.when(section == active)
     def _():
-        @pl.when(part == 0)
-        def _():
-            out_ref[...] = mid_ref[...]
-
         low = low_ref[0]
         gate = dot(low, wg_ref[...])
         up = dot(low, wu_ref[...])
@@ -272,7 +291,6 @@
         hidden_ref[...] = (silu * up).astype(BF16)
         ggu_ref[0] = (grad_hidden * up * (sig * (1.0 + gate * (1.0 - sig)))).astype(BF16)
         ggu_ref[1] = (grad_hidden * silu).astype(BF16)
-        out_ref[...] += dot(hidden_ref[...], wd_ref[...])
         added = dot_cols(ggu_ref[0], wg_ref[...]) + dot_cols(ggu_ref[1], wu_ref[...])
         total_ref[...] = jnp.where(part == 0, added, total_ref[...] + added)
 
@@ -313,54 +331,23 @@
 
 
 def whole(shape):
-    return pl.BlockSpec(shape, lambda part, *_: (0,) * len(shape))
+    return pl.BlockSpec(shape, lambda part: (0,) * len(shape))
 
 
 def column(rows, wide, offset=0):
-    return pl.BlockSpec((rows, wide), lambda part, *act: (0, (part + offset) * (act[0][0] if act else 1)))
+    return pl.BlockSpec((rows, wide), lambda part: (0, part + offset))
 
 
 def stacked(count, rows, wide):
-    return pl.BlockSpec((count, rows, wide), lambda part, *act: (0, 0, part * (act[0][0] if act else 1)))
+    return pl.BlockSpec((count, rows, wide), lambda part: (0, 0, part))
 
 
 def lower(rows, wide):
-    return pl.BlockSpec((rows, wide), lambda part, *act: (part * (act[0][0] if act else 1), 0))
-
-
-def local_call(kernel, name, grid, scalars, args, in_specs, outs, out_specs, scratch, flops, limit=56):
-    return pl.pallas_call(
-        kernel,
-        grid_spec=pltpu.PrefetchScalarGridSpec(
-            num_scalar_prefetch=len(scalars), grid=(grid,), in_specs=in_specs, out_specs=out_specs,
-            scratch_shapes=scratch),
-        out_shape=outs,
-        name=name,
-        cost_estimate=pl.CostEstimate(flops=flops, bytes_accessed=40 * 2 ** 20, transcendentals=0),
-        compiler_params=pltpu.CompilerParams(
-            dimension_semantics=("arbitrary",), vmem_limit_bytes=limit * 1024 * 1024),
-    )(*scalars, *args)
-
-
-def attention(active, lengths, x, gain, bias, gain_f, bias_f, w_qkv, w_out, cosine, sine, parts=2):
-    tokens, features = x.shape
-    row_tokens = tokens // lengths.shape[0]
-    size = features // HEADS
-    wide = features // parts
-    stack = jax.ShapeDtypeStruct((3, tokens, features), BF16)
-    return local_call(
-        functools.partial(attention_kernel, size, row_tokens), "attention", parts, (active, lengths),
-        (x, gain, bias, gain_f, bias_f, w_qkv, w_qkv, w_qkv, w_out, cosine, sine),
-        [whole((tokens, features))] + [whole((1, features))] * 4 + [column(features, wide),
-         column(features, wide, parts), column(features, wide, 2 * parts), lower(wide, features),
-         whole(cosine.shape), whole(sine.shape)],
-        (jax.ShapeDtypeStruct((tokens, features), F32), stack, stack),
-        (whole((tokens, features)), whole(stack.shape), stacked(3, tokens, wide)),
-        [pltpu.VMEM((tokens, wide), BF16)], 8 * tokens * features ** 2)
+    return pl.BlockSpec((rows, wide), lambda part: (part, 0))
 
 
 def third(tokens, features):
-    return pl.BlockSpec((1, tokens, features), lambda part, *_: (2, 0, 0))
+    return pl.BlockSpec((1, tokens, features), lambda part: (2, 0, 0))
 
 
 def meeting_call(kernel, name, parts, args, in_specs, outs, out_specs, scratch, flops, collective_id):
@@ -375,8 +362,26 @@
         cost_estimate=pl.CostEstimate(flops=flops, bytes_accessed=40 * 2 ** 20, transcendentals=0),
         compiler_params=pltpu.CompilerParams(
             dimension_semantics=("arbitrary",), vmem_limit_bytes=56 * 1024 * 1024, collective_id=collective_id,
-            has_side_effects=True),
+            has_side_effects=collective_id is not None),
     )(*args)
+
+
+def attention(active, lengths, x, gain, bias, gain_f, bias_f, w_qkv, w_out, cosine, sine, collective_id, parts=2):
+    tokens, features = x.shape
+    row_tokens = tokens // lengths.shape[0]
+    size = features // HEADS
+    wide = features // parts
+    stack = jax.ShapeDtypeStruct((3, tokens, features), BF16)
+    hbm = pl.BlockSpec(memory_space=pl.ANY)
+    return meeting_call(
+        functools.partial(attention_kernel, size, row_tokens, active), "attention", parts,
+        (x, gain, bias, gain_f, bias_f, w_qkv, w_qkv, w_qkv, w_out, cosine, sine, lengths),
+        [whole((tokens, features))] + [whole((1, features))] * 4 + [column(features, wide),
+         column(features, wide, parts), column(features, wide, 2 * parts), lower(wide, features),
+         whole(cosine.shape), whole(sine.shape), pl.BlockSpec(memory_space=pltpu.SMEM)],
+        (jax.ShapeDtypeStruct((tokens, features), F32), stack, stack, jax.ShapeDtypeStruct((tokens, features), BF16)),
+        (whole((tokens, features)), whole(stack.shape), stacked(3, tokens, wide), hbm),
+        [pltpu.VMEM((tokens, wide), BF16), pltpu.SemaphoreType.DMA((2, 1))], 8 * tokens * features ** 2, collective_id)
 
 
 def feed(mid, lefts, rows, w_gate_up, w_down, unit_rows, collective_id, parts=8):
@@ -407,13 +412,53 @@
         [whole((tokens, features)), third(tokens, features), whole((tokens, features)), whole((1, features)),
          whole((1, features)), column(features, wide), column(features, wide, parts), lower(wide, features)]
         + [hbm] * len(sends),
-        (jax.ShapeDtypeStruct((tokens, features), F32), jax.ShapeDtypeStruct((tokens, hidden), BF16),
-         jax.ShapeDtypeStruct((2, tokens, hidden), BF16), jax.ShapeDtypeStruct((tokens + 8, features), F32),
+        (jax.ShapeDtypeStruct((tokens, hidden), BF16), jax.ShapeDtypeStruct((2, tokens, hidden), BF16), jax.ShapeDtypeStruct((tokens + 8, features), F32),
          jax.ShapeDtypeStruct((8, features), F32), *lands),
-        (whole((tokens, features)), column(tokens, wide), stacked(2, tokens, wide),
-         whole((tokens + 8, features)), whole((8, features))) + (hbm,) * len(lands),
+        (column(tokens, wide), stacked(2, tokens, wide), whole((tokens + 8, features)), whole((8, features))) + (hbm,) * len(lands),
         [pltpu.VMEM((tokens, features), F32), pltpu.SemaphoreType.DMA((2, 10))],
-        12 * tokens * features * hidden, collective_id)
+        10 * tokens * features * hidden, collective_id)
+
+
+def feed_out_kernel(parts, mid_in, hidden_in, weight_in, out, total_ref, hidden_ref, weight_ref, load_sem, store_sem):
+    wide = hidden_ref.shape[1] // parts
+    first = pltpu.make_async_copy(mid_in, total_ref, store_sem)
+    loads = []
+    for part in range(parts):
+        at = pl.ds(part * wide, wide)
+        loads.append((pltpu.make_async_copy(hidden_in.at[:, at], hidden_ref.at[:, at], load_sem.at[0, part]),
+                      pltpu.make_async_copy(weight_in.at[at], weight_ref.at[at], load_sem.at[1, part])))
+
+    @pl.when(lax.axis_index("section") == 1)
+    def _():
+        first.start()
+        for copies in loads:
+            for copy in copies:
+                copy.start()
+        first.wait()
+        for part, copies in enumerate(loads):
+            for copy in copies:
+                copy.wait()
+            at = slice(part * wide, (part + 1) * wide)
+            total_ref[...] += dot(hidden_ref[:, at], weight_ref[at])
+        last = pltpu.make_async_copy(total_ref, out, store_sem)
+        last.start()
+        last.wait()
+
+
+def feed_out(mid, hidden, w_down, parts=4):
+    hbm = pl.BlockSpec(memory_space=pl.ANY)
+    return pl.pallas_call(
+        functools.partial(feed_out_kernel, parts),
+        out_shape=jax.ShapeDtypeStruct(mid.shape, F32),
+        in_specs=[hbm] * 3,
+        out_specs=hbm,
+        scratch_shapes=[pltpu.VMEM(mid.shape, F32), pltpu.VMEM(hidden.shape, BF16), pltpu.VMEM(w_down.shape, BF16),
+                        pltpu.SemaphoreType.DMA((2, parts)), pltpu.SemaphoreType.DMA],
+        name="feed_out",
+        cost_estimate=pl.CostEstimate(
+            flops=2 * mid.shape[0] * w_down.size, bytes_accessed=16 * 2 ** 20, transcendentals=0),
+        compiler_params=pltpu.CompilerParams(vmem_limit_bytes=56 * 1024 * 1024),
+    )(mid, hidden, w_down)
 
 
 def tables(lengths, row_tokens, size):
@@ -431,7 +476,7 @@
 
 
 def exchange_kernel(cfg, back_sizes, *refs):
-    shards, bits, seats, unit_rows, width, section, aliased, late, layers, other_layers, lag, supply, order, backs = cfg
+    shards, bits, seats, unit_rows, width, section, aliased, late, layers, other_layers, lag, supply, order, backs, swapped = cfg
     arrays = len(seats)
     refs = list(refs)
 
@@ -636,10 +681,13 @@
         begin = 0
         for row in range(late_rows):
             need = max(lead + row * seats[-1][1] * (pace + 1) - 1, 0)
+            stride = max((need - begin) // shards, 1)
             at_once = -(-shards // max(need - begin, 1))
             for index in range(at_once):
-                shard = (turn - begin) * at_once + index
-                on((turn >= begin) & (shard < shards), lambda row=row, shard=shard: late_copy(row, shard).start())
+                passed = turn - begin
+                shard = lax.div(jnp.maximum(passed, 0), stride) * at_once + index
+                on((passed >= 0) & (passed - lax.div(jnp.maximum(passed, 0), stride) * stride == 0) & (shard < shards),
+                   lambda row=row, shard=shard: late_copy(row, shard).start())
 
             def finish(row=row):
                 @pl.loop(0, shards)
@@ -696,39 +744,45 @@
     def base(path, slot, shard, rows):
         return (side[others - 1, slot, shard, rows] if path == 0 else mine[1, slot, shard, rows]).astype(F32)
 
-    def hop(path, way, chunk, shard):
-        slot = lax.rem(chunk, depth)
-        ref = chains[path].at[way, slot, shard]
-        return remote(ref, ref, chain_send.at[path, way, slot, shard], chain_recv.at[path, way, slot, shard],
-                      above if way == 0 else below)
+    def hop(path, way, chunk, at):
+        begin, end = (at + 1, shards) if way == 0 else (0, at)
+        ref = chains[path].at[way, lax.rem(chunk, depth), begin:end]
+        return remote(ref, ref, chain_send.at[path, way, lax.rem(chunk, 3)],
+                      chain_recv.at[path, way, lax.rem(chunk, depth)], above if way == 0 else below)
+
+    def at_each(run):
+        for at in range(shards):
+            on(here == at, lambda at=at: run(at))
 
     def onward(path, way, chunk):
         slot, from_base = lax.rem(chunk, depth), lax.rem(chunk, ring)
-        arrives = here > 0 if way == 0 else here < shards - 1
-
-        @pl.loop(0, shards - 1 - here if way == 0 else here)
-        def _(index):
-            shard = shards - 1 - index if way == 0 else index
-            copy = hop(path, way, chunk, shard)
-            on(arrives, lambda: copy.wait_recv())
-            source = jnp.where(arrives, slot, depth)
-
-            def add(rows):
-                chains[path][way, slot, shard, rows] = (
-                    chains[path][way, source, shard, rows].astype(F32) + base(path, from_base, shard, rows)
-                ).astype(BF16)
-            by_rows(chain_rows[path], add)
-            copy.start()
+
+        def from_here(at):
+            first, last = (at == 0, at == shards - 1) if way == 0 else (at == shards - 1, at == 0)
+            if not first:
+                hop(path, way, chunk, at - 1 if way == 0 else at + 1).wait_recv()
+            if not last:
+                begin, count = (at + 1, shards - 1 - at) if way == 0 else (0, at)
+
+                @pl.loop(begin, begin + count)
+                def _(shard):
+                    def add(rows):
+                        value = base(path, from_base, shard, rows)
+                        if not first:
+                            value = value + chains[path][way, slot, shard, rows].astype(F32)
+                        chains[path][way, slot, shard, rows] = value.astype(BF16)
+                    by_rows(chain_rows[path], add)
+                hop(path, way, chunk, at).start()
+        at_each(from_here)
 
     def sent(path, way, chunk):
-        @pl.loop(0, shards - 1 - here if way == 0 else here)
-        def _(index):
-            hop(path, way, chunk, shards - 1 - index if way == 0 else index).wait_send()
+        def from_here(at):
+            if at != (shards - 1 if way == 0 else 0):
+                hop(path, way, chunk, at).wait_send()
+        at_each(from_here)
 
     def last_hop(path, chunk):
         from_base, slot = lax.rem(chunk, ring), lax.rem(chunk, depth)
-        on(here > 0, lambda: hop(path, 0, chunk, here).wait_recv())
-        on(here < shards - 1, lambda: hop(path, 1, chunk, here).wait_recv())
         from_below = jnp.where(here > 0, slot, depth)
         from_above = jnp.where(here < shards - 1, slot, depth)
 
@@ -802,15 +856,24 @@
     def gather(path, step, other, chunk, target):
         slot = lax.rem(chunk, slots)
         source = piece.at[path, slot] if step == 0 else target
+        if swapped[path]:
+            index = bits - 1 - step
+        else:
+            index = 0 if step == 0 else bits - step
         return remote(source, target, gather_send.at[path, step, other, slot], gather_recv.at[path, step, other, slot],
-                      across(0 if step == 0 else bits - step))
+                      across(index))
+
+    def gather_size(path, step):
+        if swapped[path]:
+            return others - step, 1
+        return others - max(step - 1, 0), 1 if step == 0 else 2
 
     def spread(path, step, chunk):
-        steps = others - max(step - 1, 0)
+        steps, copies = gather_size(path, step)
         rows = unit_rows >> steps
 
         def each(which, row, block):
-            for other in range(1 if step == 0 else 2):
+            for other in range(copies):
                 bit = half if other == 0 else 1 - half
                 target = place(which, row, block, path, bit, seat_row(steps), rows)
                 if step == 0:
@@ -819,9 +882,9 @@
         each_array(chunk, each)
 
     def gathered(path, step, chunk):
-        rows = unit_rows >> (others - max(step - 1, 0))
-        target = outs[0].at[pl.ds(0, rows), pl.ds(0, width)]
-        for other in range(1 if step == 0 else 2):
+        steps, copies = gather_size(path, step)
+        target = outs[0].at[pl.ds(0, unit_rows >> steps), pl.ds(0, width)]
+        for other in range(copies):
             copy = gather(path, step, other, chunk, target)
             copy.wait_recv()
             copy.wait_send()
@@ -995,9 +1058,6 @@
         @pl.loop(1, peers)
         def _(step):
             pl.semaphore_signal(barrier, inc=1, device_id=peer(step)[1], device_id_type=MESH)
-        pl.semaphore_wait(barrier, peers - 1)
-        for chunk in range(lag):
-            send_right(chunk)
         loads(0, lambda copy: copy.start())
         if backs:
             back_start()
@@ -1009,6 +1069,9 @@
                     def clear(rows):
                         chains[path][way, depth, shard, rows] = jnp.zeros((rows.size, width), BF16)
                     by_rows(chain_rows[path], clear)
+        pl.semaphore_wait(barrier, peers - 1)
+        for chunk in range(lag):
+            send_right(chunk)
 
         line = shards - 1
 
@@ -1055,7 +1118,7 @@
             pl.when(sec != section)(hand_over)
 
 
-def exchange(pairs, vector, shards, group, section, collective_id, unit_width, previous=None, lag=None, first_bit=0, supply=(1, 2), back=(), backs=False, parts=2, unit_rows_max=256,
+def exchange(pairs, vector, shards, group, section, collective_id, unit_width, previous=None, lag=None, first_bit=0, supply=(1, 2), back=(), backs=False, swapped=(False, False), parts=2, unit_rows_max=256,
              name="exchange"):
     bits = group.bit_length() - 1
     arrays = len(pairs)
@@ -1109,7 +1172,7 @@
         dma((others, slots)), dma((others, slots)),
         pltpu.VMEM((2, depth + 1, shards, final_rows, width), BF16),
         pltpu.VMEM((2, depth + 1, shards, unit_rows, width), BF16),
-        dma((2, 2, depth, shards)), dma((2, 2, depth, shards)),
+        dma((2, 2, 3)), dma((2, 2, depth)),
         pltpu.VMEM((others, slots, unit_rows // 2, width), BF16),
         pltpu.VMEM((others, slots, unit_rows // 2, width), BF16),
         pltpu.VMEM((others, slots, unit_rows // 2, width), F32),
@@ -1118,7 +1181,7 @@
         dma((2, slots)),
         dma((2, bits, 2, slots)), dma((2, bits, 2, slots)),
     ]
-    cfg = (shards, bits, tuple(seats), unit_rows, width, section, len(previous) > 0, late, layers, other_layers, lag, supply, order, backs)
+    cfg = (shards, bits, tuple(seats), unit_rows, width, section, len(previous) > 0, late, layers, other_layers, lag, supply, order, backs, swapped)
     operands = lefts + [r for n, r in enumerate(rights) if n not in supply] + left_others + [
         pairs[-1][3], vector] + back + [lengths] + previous
     first = len(operands) - len(previous)
@@ -1166,9 +1229,7 @@
     w_gate_up,
     w_down,
 ):
-    section = lax.axis_index("section")
     shards, group = lax.axis_size("shard"), lax.axis_size("group")
-    first, second = ((section == which).astype(jnp.int32).reshape(1) for which in range(2))
     tokens, features = ends_in.shape[1:]
     size = features // HEADS
     rows = ends_in[0]
@@ -1181,9 +1242,9 @@
     def like(array):
         return jax.ShapeDtypeStruct(array.shape, array.dtype)
 
-    def attend(active, values):
+    def attend(active, values, collective_id):
         return attention(active, lengths, values, norm_gain_a, norm_bias_a, norm_gain_f, norm_bias_f, weight_qkv,
-                         weight_out, cosine, sine)
+                         weight_out, cosine, sine, collective_id)
 
     def feed_back(active, middle, lefts, grad, sends, lands, collective_id):
         return feed_both(active, middle, lefts, grad, norm_gain_f, norm_gain_a, weight_gu, weight_down, sends, lands,
@@ -1196,38 +1257,30 @@
         return exchange(pairs, vectors, shards, group, which, which + 1, UNIT_WIDTH * features // 1024,
                         first_bit=1 - which, back=back + (cosine, sine, lengths), **more)
 
-    middle_0, lefts_0, qkv_0 = attend(first, rows)
+    middle_0, lefts_0, qkv_0, _ = attend(0, rows, None)
     passed, hidden_half_0, arrived, early_beside, rows_beside = feed(
         middle_0, lefts_0, rows, weight_gu, weight_down, unit_rows, 3)
-    middle_1, lefts_1, qkv_1 = attend(second, arrived)
-    result, hidden_1, grad_gu_1, _, vectors_1, lefts_beside, qkv_there, qkv_weight, out_weight, hidden_beside, \
+    middle_1, lefts_1, qkv_1, low_beside = attend(1, arrived, 6)
+    hidden_1, grad_gu_1, _, vectors_1, lefts_beside, qkv_there, qkv_weight, out_weight, hidden_beside, \
         grad_middle = feed_back(
             1, middle_1, lefts_1, rows,
             (lefts_1, qkv_1, weight_qkv, weight_out, lefts_0, hidden_half_0),
             (stack, stack, like(weight_qkv), like(weight_out), like(hidden_half_0), jax.ShapeDtypeStruct((tokens + 8, features), F32)), 4)
-    sums = sum_all(1, lefts_1, [(lefts_beside, at) for at in (2, 1, 0)], hidden_1, None, grad_gu_1, rows, rows_beside,
+    sums = sum_all(1, lefts_1, [(lefts_beside, 2), (lefts_beside, 1), (low_beside, None)], hidden_1, None, grad_gu_1, rows, rows_beside,
                    vectors_1, (grad_middle, passed, qkv_there, qkv_weight, out_weight), name="exchange_second")
     returned = sums[-1]
-    _, hidden_0, grad_gu_0, grad_middle, vectors_0, returned_beside = feed_back(
+    hidden_later, _ = lax.optimization_barrier((hidden_1, sums[4]))
+    result = feed_out(middle_1, hidden_later, weight_down)
+    hidden_0, grad_gu_0, grad_middle, vectors_0, returned_beside = feed_back(
         0, middle_0, lefts_0, returned, (returned,), (low,), 5)
     sums = sum_all(0, lefts_0, [(lefts_beside, 2), (early_beside, 1), (early_beside, 0)], hidden_0,
                    (hidden_beside, None), grad_gu_0, returned, returned_beside, vectors_0,
-                   (grad_middle, rows, qkv_0, weight_qkv, weight_out), backs=True, previous=[*sums[:5], result],
+                   (grad_middle, rows, qkv_0, weight_qkv, weight_out), backs=True, previous=[*sums[:5], result], swapped=(False, True),
                    name="exchange_first")
     ends_out = sums[-1][None]
     grad_gate_up, grad_out, grad_qkv, grad_down = (item.astype(F32)[None] for item in sums[:4])
-    vectors = sums[4]
-    return (
-        ends_out,
-        vectors[0:1],
-        vectors[1:2],
-        grad_qkv,
-        grad_out,
-        vectors[2:3],
-        vectors[3:4],
-        grad_gate_up,
-        grad_down,
-    )
+    gain_a, bias_a, gain_f, bias_f = (sums[4][row:row + 1] for row in range(4))
+    return (ends_out, gain_a, bias_a, grad_qkv, grad_out, gain_f, bias_f, grad_gate_up, grad_down)
 
 
 def solution(mesh):

time: 395 us -> 388 us (0.982)
  Pallas kernels: 374 us -> 367 us
    pallas_call x2 -> x1, Pallas kernels: 26.4 us -> 0.32 us  [feed_out(): pl.pallas_call(functools.partial(feed_out_kernel, parts), out_shape=jax.S...]
    pallas_call x3 -> x5, Pallas kernels: 120 us -> 140 us  [meeting_call(): pl.pallas_call(kernel, grid=(parts,), in_specs=in_specs, out_specs=out_sp...]
where the time goes in v9:
time: 388 us
  Pallas kernels  367 us (95%)
  other arithmetic  15.6 us (4%)
  local copies, waits for them, and re-layouts  4.09 us (1%)
    pallas_call x2, Pallas kernels, exchange(): pl.pallas_call(functools.partial(exchange_kernel, cfg, (x.shape[1] // HEA...  227 us
    pallas_call x5, Pallas kernels, meeting_call(): pl.pallas_call(kernel, grid=(parts,), in_specs=in_specs, out_specs=out_sp...  140 us
    broadcast_in_dim x4, other arithmetic, body(): item.astype(F32)[None]  12.7 us

profile of v9, /device:TPU:0, one launch (start us, length us, event | category | flops | bytes accessed | tf_op | source)
XLA Modules:
  0.0 387.5 jit_solution(2318272596213900617)
XLA Ops:
  0.7 1.0 fusion.7
  1.7 0.1 broadcast_bitcast_fusion.4
  1.8 0.1 broadcast_bitcast_fusion.2
  1.9 0.1 broadcast_bitcast_fusion
  2.0 1.8 multiply_sine_fusion
  3.8 19.2 %attention.2 = (f32[512,1024]{1,0:T(8,128)}, bf16[3,512,1024]{2,1,0:T(8,128)(2,1)}, bf16[3,512,1024]{2,1,0:T(8,128)(2,1)}, bf16[512,1024]{1,0:T(8,128)(2,1)}) custom-call(bf16[512,1024]{1,0:T(8,128)(2,1)} %bitcast.60, f32[1,1024]{1,0:T(1,128)} %gain_a_ref.3, f32[1,1024]{1,0:T(1,128)} %bias_ref.3, f32[1,1024]{1,0:T(1,128)} %gain_ref.7, f32[1,1024]{1,0:T(1,128)} %bias_f_ref.3, ...), custom_call_target="tpu_custom_call" | custom-call | flops 4294967296 | bytes 41943040 | tf_op jit(solution)/shard_map/attention/pallas_call | solution.py:354
  23.0 33.7 %feed.1 = (bf16[512,1024]{1,0:T(8,128)(2,1)}, bf16[512,2048]{1,0:T(8,128)(2,1)}, bf16[512,1024]{1,0:T(8,128)(2,1)}, bf16[2,512,1024]{2,1,0:T(8,128)(2,1)}, bf16[512,1024]{1,0:T(8,128)(2,1)}) custom-call(f32[512,1024]{1,0:T(8,128)} %get-tuple-element.49.mid_ref, bf16[3,512,1024]{2,1,0:T(8,128)(2,1)} %get-tuple-element.48.low_ref.lefts_ref.refs_4_.refs_0_.refs_1_.refs_2_, ...), custom_call_target="tpu_custom_call" | custom-call | flops 12884901888 | bytes 41943040 | tf_op jit(solution)/shard_map/feed/pallas_call | solution.py:354
  56.7 6.8 %attention.3 = (f32[512,1024]{1,0:T(8,128)}, bf16[3,512,1024]{2,1,0:T(8,128)(2,1)}, bf16[3,512,1024]{2,1,0:T(8,128)(2,1)}, bf16[512,1024]{1,0:T(8,128)(2,1)}) custom-call(bf16[512,1024]{1,0:T(8,128)(2,1)} %get-tuple-element.50.x_ref, f32[1,1024]{1,0:T(1,128)} %gain_a_ref.3, f32[1,1024]{1,0:T(1,128)} %bias_ref.3, f32[1,1024]{1,0:T(1,128)} %gain_ref.7, ...), custom_call_target="tpu_custom_call" | custom-call | flops 4294967296 | bytes 41943040 | tf_op jit(solution)/shard_map/attention/pallas_call | solution.py:354
  63.5 47.7 %feed_both.2 = (bf16[512,4096]{1,0:T(8,128)(2,1)}, bf16[2,512,4096]{2,1,0:T(8,128)(2,1)}, f32[520,1024]{1,0:T(8,128)}, f32[8,1024]{1,0:T(8,128)}, bf16[3,512,102...) custom-call(f32[512,1024]{1,0:T(8,128)} %get-tuple-element.52.mid_re, ...), custom_call_target="tpu_custom_call" | custom-call | flops 21474836480 | bytes 41943040 | tf_op jit(solution)/shard_map/feed_both/pallas_call | solution.py:354
  111.3 28.3 %exchange_second.1 = (bf16[256,8192]{1,0:T(8,128)(2,1)}, bf16[256,1024]{1,0:T(8,128)(2,1)}, bf16[256,3072]{1,0:T(8,128)(2,1)}, bf16[1024,1024]{1,0:T(8,128)(2,1)...) custom-call(bf16[3,512,1024]{2,1,0:T(8,128)(2,1)} %get-tuple-element, ...), custom_call_target="tpu_custom_call" | custom-call | flops 17179869184 | bytes 104857600 | tf_op jit(solution)/shard_map/exchange_second/pallas_call | solution.py:1201
  139.6 0.3 feed_out.1.refs_25_
  139.9 32.5 %feed_both.3 = (bf16[512,4096]{1,0:T(8,128)(2,1)}, bf16[2,512,4096]{2,1,0:T(8,128)(2,1)}, f32[520,1024]{1,0:T(8,128)}, f32[8,1024]{1,0:T(8,128)}, bf16[512,1024]{1,0:T(8,128)(2,1)}) custom-call(f32[512,1024]{1,0:T(8,128)} %get-tuple-element.49.mid_ref, bf16[3,512,1024]{2,1,0:T(8,128)(2,1)} %get-tuple-element.48.low_ref.lefts_ref.refs_4_.refs_0_.refs_1_.refs_2_, ...), custom_call_target="tpu_custom_call" | custom-call | flops 21474836480 | bytes 41943040 | tf_op jit(solution)/shard_map/feed_both/pallas_call | solution.py:354
  172.5 198.5 %exchange_first.1 = (bf16[256,8192]{1,0:T(8,128)(2,1)}, bf16[256,1024]{1,0:T(8,128)(2,1)}, bf16[256,3072]{1,0:T(8,128)(2,1)}, bf16[1024,1024]{1,0:T(8,128)(2,1)}...) custom-call(bf16[3,512,1024]{2,1,0:T(8,128)(2,1)} %get-tuple-element, ...), custom_call_target="tpu_custom_call", output_to_operand_aliasing={{0}: (20, {}), {1}: (21, {}), {2}: (22, {}), {3}: (23, {}),... | custom-call | flops 17179869184 | bytes 104857600 | tf_op jit(solution)/shard_map/exchange_first/pallas_call | solution.py:1201
  371.0 1.4 fusion.8
  372.4 0.0 copy-start.2
  372.4 2.3 bitcast_convert_fusion.3
  374.7 3.4 bitcast_convert_fusion.2
  378.1 0.0 copy-done.2
  378.1 0.0 copy-start.1
  378.1 2.6 bitcast_convert_fusion.1
  380.7 1.1 copy-done.1
  381.8 0.0 copy-start
  381.8 4.4 %bitcast_convert_fusion = f32[1,256,8192]{2,1,0:T(8,128)} fusion(bf16[256,8192]{1,0:T(8,128)(2,1)S(1)} %copy-done.1), kind=kLoop, calls=%fused_computation | loop fusion | flops 2097152 | bytes 12582912 | tf_op jit(solution)/shard_map/broadcast_in_dim | solution.py:1281
  386.2 0.0 copy-done
  386.2 1.3 copy.38
  (9 shorter events, 0.0 us)
Async XLA Ops:
  372.4 5.7 %copy-start.2 = (bf16[1024,1024]{1,0:T(8,128)(2,1)S(1)}, bf16[1024,1024]{1,0:T(8,128)(2,1)}, u32[]{:S(2)}) copy-start(bf16[1024,1024]{1,0:T(8,128)(2,1)} %get-tuple-element.86) | copy-start | bytes 6291460
  378.1 3.7 copy-start.1
  381.8 4.4 %copy-start = (f32[512,1024]{1,0:T(8,128)S(1)}, f32[512,1024]{1,0:T(8,128)}, u32[]{:S(2)}) copy-start(f32[512,1024]{1,0:T(8,128)} %get-tuple-element.81) | copy-start | bytes 6291460

commit v10 on v9

--- a/solution.py
+++ b/solution.py
@@ -578,7 +578,7 @@
     def on(condition, run):
         pl.when(condition)(run)
 
-    def by_rows(rows, run, tall=64):
+    def by_rows(rows, run, tall=128):
         step = min(rows, tall)
 
         @pl.loop(0, rows // step)
@@ -634,7 +634,7 @@
                     right_others[0].at[:, columns], right.at[slot, tokens:], other_sem.at[slot]))
         each_array(chunk, each)
 
-    def load_left(chunk):
+    def load_left(chunk, wanted):
         def each(which, row, block):
             rows = seats[which][3]
             kind = int(split_rows(which))
@@ -655,7 +655,7 @@
                     copy.start()
                 for copy in copies:
                     copy.wait()
-            on(block == 0, fetch)
+            on((block == 0) & wanted, fetch)
         each_array(chunk, each)
 
     def right_copy(chunk, source):
@@ -699,7 +699,7 @@
 
     def multiply(chunk):
         four, slot = lax.rem(chunk, right_slots), lax.rem(chunk, ring)
-        load_left(chunk)
+        load_left(chunk, chunk > 0)
         loads(chunk, lambda copy: copy.wait())
         last = seat_of(chunk)[0]
 
@@ -1069,6 +1069,7 @@
                     def clear(rows):
                         chains[path][way, depth, shard, rows] = jnp.zeros((rows.size, width), BF16)
                     by_rows(chain_rows[path], clear)
+        load_left(0, True)
         pl.semaphore_wait(barrier, peers - 1)
         for chunk in range(lag):
             send_right(chunk)
@@ -1275,7 +1276,7 @@
         0, middle_0, lefts_0, returned, (returned,), (low,), 5)
     sums = sum_all(0, lefts_0, [(lefts_beside, 2), (early_beside, 1), (early_beside, 0)], hidden_0,
                    (hidden_beside, None), grad_gu_0, returned, returned_beside, vectors_0,
-                   (grad_middle, rows, qkv_0, weight_qkv, weight_out), backs=True, previous=[*sums[:5], result], swapped=(False, True),
+                   (grad_middle, rows, qkv_0, weight_qkv, weight_out), backs=True, previous=[*sums[:5], result],
                    name="exchange_first")
     ends_out = sums[-1][None]
     grad_gate_up, grad_out, grad_qkv, grad_down = (item.astype(F32)[None] for item in sums[:4])

time: 388 us -> 387 us (level)
  no operation moved by 1% of the time
where the time goes in v10:
time: 387 us; the launch traced here: 386 us
  Pallas kernels  366 us (95%)
  other arithmetic  15.6 us (4%)
  local copies, waits for them, and re-layouts  4.09 us (1%)
    pallas_call x2, Pallas kernels, exchange(): pl.pallas_call(functools.partial(exchange_kernel, cfg, (x.shape[1] // HEA...  224 us
    pallas_call x5, Pallas kernels, meeting_call(): pl.pallas_call(kernel, grid=(parts,), in_specs=in_specs, out_specs=out_sp...  141 us
    broadcast_in_dim x4, other arithmetic, body(): item.astype(F32)[None]  12.7 us

profile of v10, /device:TPU:0, one launch (start us, length us, event | category | flops | bytes accessed | tf_op | source)
XLA Modules:
  0.0 386.1 jit_solution(6435885807686836721)
XLA Ops:
  0.7 1.0 fusion.7
  1.7 0.1 broadcast_bitcast_fusion.4
  1.8 0.1 broadcast_bitcast_fusion.2
  1.9 0.1 broadcast_bitcast_fusion
  2.0 1.8 multiply_sine_fusion
  3.8 19.2 %attention.2 = (f32[512,1024]{1,0:T(8,128)}, bf16[3,512,1024]{2,1,0:T(8,128)(2,1)}, bf16[3,512,1024]{2,1,0:T(8,128)(2,1)}, bf16[512,1024]{1,0:T(8,128)(2,1)}) custom-call(bf16[512,1024]{1,0:T(8,128)(2,1)} %bitcast.60, f32[1,1024]{1,0:T(1,128)} %gain_a_ref.3, f32[1,1024]{1,0:T(1,128)} %bias_ref.3, f32[1,1024]{1,0:T(1,128)} %gain_ref.7, f32[1,1024]{1,0:T(1,128)} %bias_f_ref.3, ...), custom_call_target="tpu_custom_call" | custom-call | flops 4294967296 | bytes 41943040 | tf_op jit(solution)/shard_map/attention/pallas_call | solution.py:354
  23.0 33.7 %feed.1 = (bf16[512,1024]{1,0:T(8,128)(2,1)}, bf16[512,2048]{1,0:T(8,128)(2,1)}, bf16[512,1024]{1,0:T(8,128)(2,1)}, bf16[2,512,1024]{2,1,0:T(8,128)(2,1)}, bf16[512,1024]{1,0:T(8,128)(2,1)}) custom-call(f32[512,1024]{1,0:T(8,128)} %get-tuple-element.49.mid_ref, bf16[3,512,1024]{2,1,0:T(8,128)(2,1)} %get-tuple-element.48.low_ref.lefts_ref.refs_4_.refs_0_.refs_1_.refs_2_, ...), custom_call_target="tpu_custom_call" | custom-call | flops 12884901888 | bytes 41943040 | tf_op jit(solution)/shard_map/feed/pallas_call | solution.py:354
  56.7 6.8 %attention.3 = (f32[512,1024]{1,0:T(8,128)}, bf16[3,512,1024]{2,1,0:T(8,128)(2,1)}, bf16[3,512,1024]{2,1,0:T(8,128)(2,1)}, bf16[512,1024]{1,0:T(8,128)(2,1)}) custom-call(bf16[512,1024]{1,0:T(8,128)(2,1)} %get-tuple-element.50.x_ref, f32[1,1024]{1,0:T(1,128)} %gain_a_ref.3, f32[1,1024]{1,0:T(1,128)} %bias_ref.3, f32[1,1024]{1,0:T(1,128)} %gain_ref.7, ...), custom_call_target="tpu_custom_call" | custom-call | flops 4294967296 | bytes 41943040 | tf_op jit(solution)/shard_map/attention/pallas_call | solution.py:354
  63.5 47.7 %feed_both.2 = (bf16[512,4096]{1,0:T(8,128)(2,1)}, bf16[2,512,4096]{2,1,0:T(8,128)(2,1)}, f32[520,1024]{1,0:T(8,128)}, f32[8,1024]{1,0:T(8,128)}, bf16[3,512,102...) custom-call(f32[512,1024]{1,0:T(8,128)} %get-tuple-element.52.mid_re, ...), custom_call_target="tpu_custom_call" | custom-call | flops 21474836480 | bytes 41943040 | tf_op jit(solution)/shard_map/feed_both/pallas_call | solution.py:354
  111.3 27.6 %exchange_second.1 = (bf16[256,8192]{1,0:T(8,128)(2,1)}, bf16[256,1024]{1,0:T(8,128)(2,1)}, bf16[256,3072]{1,0:T(8,128)(2,1)}, bf16[1024,1024]{1,0:T(8,128)(2,1)...) custom-call(bf16[3,512,1024]{2,1,0:T(8,128)(2,1)} %get-tuple-element, ...), custom_call_target="tpu_custom_call" | custom-call | flops 17179869184 | bytes 104857600 | tf_op jit(solution)/shard_map/exchange_second/pallas_call | solution.py:1202
  138.8 0.3 feed_out.1.refs_25_
  139.2 33.5 %feed_both.3 = (bf16[512,4096]{1,0:T(8,128)(2,1)}, bf16[2,512,4096]{2,1,0:T(8,128)(2,1)}, f32[520,1024]{1,0:T(8,128)}, f32[8,1024]{1,0:T(8,128)}, bf16[512,1024]{1,0:T(8,128)(2,1)}) custom-call(f32[512,1024]{1,0:T(8,128)} %get-tuple-element.49.mid_ref, bf16[3,512,1024]{2,1,0:T(8,128)(2,1)} %get-tuple-element.48.low_ref.lefts_ref.refs_4_.refs_0_.refs_1_.refs_2_, ...), custom_call_target="tpu_custom_call" | custom-call | flops 21474836480 | bytes 41943040 | tf_op jit(solution)/shard_map/feed_both/pallas_call | solution.py:354
  172.6 196.9 %exchange_first.1 = (bf16[256,8192]{1,0:T(8,128)(2,1)}, bf16[256,1024]{1,0:T(8,128)(2,1)}, bf16[256,3072]{1,0:T(8,128)(2,1)}, bf16[1024,1024]{1,0:T(8,128)(2,1)}...) custom-call(bf16[3,512,1024]{2,1,0:T(8,128)(2,1)} %get-tuple-element, ...), custom_call_target="tpu_custom_call", output_to_operand_aliasing={{0}: (20, {}), {1}: (21, {}), {2}: (22, {}), {3}: (23, {}),... | custom-call | flops 17179869184 | bytes 104857600 | tf_op jit(solution)/shard_map/exchange_first/pallas_call | solution.py:1202
  369.5 1.4 fusion.8
  371.0 0.0 copy-start.2
  371.0 2.3 bitcast_convert_fusion.3
  373.2 3.4 bitcast_convert_fusion.2
  376.7 0.0 copy-done.2
  376.7 0.0 copy-start.1
  376.7 2.6 bitcast_convert_fusion.1
  379.3 1.1 copy-done.1
  380.4 0.0 copy-start
  380.4 4.4 %bitcast_convert_fusion = f32[1,256,8192]{2,1,0:T(8,128)} fusion(bf16[256,8192]{1,0:T(8,128)(2,1)S(1)} %copy-done.1), kind=kLoop, calls=%fused_computation | loop fusion | flops 2097152 | bytes 12582912 | tf_op jit(solution)/shard_map/broadcast_in_dim | solution.py:1282
  384.8 0.0 copy-done
  384.8 1.3 copy.38
  (9 shorter events, 0.0 us)
Async XLA Ops:
  371.0 5.7 %copy-start.2 = (bf16[1024,1024]{1,0:T(8,128)(2,1)S(1)}, bf16[1024,1024]{1,0:T(8,128)(2,1)}, u32[]{:S(2)}) copy-start(bf16[1024,1024]{1,0:T(8,128)(2,1)} %get-tuple-element.86) | copy-start | bytes 6291460
  376.7 3.7 copy-start.1
  380.4 4.4 %copy-start = (f32[512,1024]{1,0:T(8,128)S(1)}, f32[512,1024]{1,0:T(8,128)}, u32[]{:S(2)}) copy-start(f32[512,1024]{1,0:T(8,128)} %get-tuple-element.81) | copy-start | bytes 6291460
